TPU v7x, 32 devices: a whole 2x2x4 slice. The times are simulated.
32 devices in a mesh: head: 2 (over x), blk: 16 (over z, y, core).
Axes of the slice: x: 2, y: 2, z: 4, core: 2. Of those that a mesh axis runs over, the one named last changes fastest.
Arguments:
- hidden: bfloat16 [8192, 1536], P(('head', 'blk')), may hold values from -6 to 6
- cotangent: bfloat16 [8192, 1536], P(('head', 'blk')), may hold values from -6 to 6
- block_order: int32 [1, 32], replicated, may hold values from 0 to 31, as said below
- norm1: float32 [1536], P(('head', 'blk')), may hold values from 0.1 to 1.9
- q_weight: float32 [1536, 1536], P(('head', 'blk')), may hold values from -0.15625 to 0.15625
- q_bias: float32 [1536], P(('head', 'blk')), may hold values from -3 to 3
- k_weight: float32 [1536, 256], P(('head', 'blk')), may hold values from -0.15625 to 0.15625
- k_bias: float32 [256], P(('head', 'blk')), may hold values from -3 to 3
- v_weight: float32 [1536, 256], P(('head', 'blk')), may hold values from -0.15625 to 0.15625
- v_bias: float32 [256], P(('head', 'blk')), may hold values from -3 to 3
- o_weight: float32 [1536, 1536], P(('head', 'blk')), may hold values from -6 to 6
- norm2: float32 [1536], P(('head', 'blk')), may hold values from 0.1 to 1.9
- gate_weight: float32 [1536, 8960], P('blk', 'head'), may hold values from -0.15625 to 0.15625
- up_weight: float32 [1536, 8960], P('blk', 'head'), may hold values from -0.15625 to 0.15625
- down_weight: float32 [1536, 8960], P('blk', 'head'), may hold values from -0.0625 to 0.0625
Outputs:
- output: bfloat16 [8192, 1536], P(('head', 'blk'))
- hidden_grad: bfloat16 [8192, 1536], P(('head', 'blk'))
- norm1_grad: float32 [1536], P(('head', 'blk'))
- q_weight_grad: float32 [1536, 1536], P(('head', 'blk'))
- q_bias_grad: float32 [1536], P(('head', 'blk'))
- k_weight_grad: float32 [1536, 256], P(('head', 'blk'))
- k_bias_grad: float32 [256], P(('head', 'blk'))
- v_weight_grad: float32 [1536, 256], P(('head', 'blk'))
- v_bias_grad: float32 [256], P(('head', 'blk'))
- o_weight_grad: float32 [1536, 1536], P(('head', 'blk'))
- norm2_grad: float32 [1536], P(('head', 'blk'))
- gate_weight_grad: float32 [1536, 8960], P('blk', 'head')
- up_weight_grad: float32 [1536, 8960], P('blk', 'head')
- down_weight_grad: float32 [1536, 8960], P('blk', 'head')
Inputs may be any that keep to these rules, and one draw needn't show every extreme that they name: `block_order`: each row names every block 0 to 31 once, and entries 2 k and 2 k + 1 of a row add up to 31.
All inputs are finite; a program needn't handle non-finite values.
Results may differ from a plain program's by a relative error of at most 0.03.
Values may be sent and summed in bfloat16 or wider, within the bound.
A program may use at most 704 MiB of HBM per device.

v0:
```python
import jax
import jax.numpy as jnp
from jax import lax
from jax.sharding import PartitionSpec as P

D = 1536
QHEADS = 12
KVHEADS = 2
HEAD_DIM = 128
SEQ_SPAN = 16
BLOCK = 256


EPS = 1e-06
THETA = 1000000.0
NEG = -1e30


def passed_along(block, axis, distance):
    devices = range(lax.axis_size(axis))
    route = [((i - distance) % len(devices), i) for i in devices]
    return lax.ppermute(block, axis, route)


def rms_scale(value, gain):
    return value * lax.rsqrt(jnp.mean(value * value, axis=-1, keepdims=True) + EPS) * gain


def angles_of(positions, head_size):
    frequency = THETA ** (-(jnp.arange(head_size // 2, dtype=jnp.float32) * 2.0) / head_size)
    return positions.astype(jnp.float32)[:, None] * frequency[None, :]


def rotate(value, angles, sign):
    half = value.shape[-1] // 2
    cosine = jnp.cos(angles)[:, None, :]
    sine = jnp.sin(angles)[:, None, :] * sign
    first = value[..., :half]
    second = value[..., half:]
    return jnp.concatenate(
        [first * cosine - second * sine, second * cosine + first * sine], axis=-1
    )


def over_rows(left, right):
    return lax.dot_general(
        left, right, (((0,), (0,)), ((), ())), preferred_element_type=jnp.float32
    )


def over_columns(left, right):
    return lax.dot_general(
        left, right, (((1,), (1,)), ((), ())), preferred_element_type=jnp.float32
    )


def shards(
    hidden,
    cotangent,
    block_order,
    norm1,
    q_weight,
    q_bias,
    k_weight,
    k_bias,
    v_weight,
    v_bias,
    o_weight,
    norm2,
    gate_weight,
    up_weight,
    down_weight,
):
    tok_count = hidden.shape[0]
    head_count = lax.axis_size("head")
    seq_count = lax.axis_size("blk") // SEQ_SPAN
    pair_rows = head_count * tok_count
    local_heads = QHEADS // head_count
    scale = HEAD_DIM ** (-0.5)
    blk_index = lax.axis_index("blk")
    seq_index = blk_index % seq_count
    place = blk_index // seq_count
    order_row = lax.dynamic_index_in_dim(block_order, seq_index, 0, keepdims=False)
    offsets = jnp.arange(tok_count, dtype=jnp.int32)
    own_block = lax.dynamic_index_in_dim(
        order_row, place * head_count + lax.axis_index("head"), 0, keepdims=False
    )
    own_positions = own_block * tok_count + offsets

    def pair_blocks(location):
        chosen = lax.dynamic_slice_in_dim(order_row, location * head_count, head_count)
        return ((chosen[:, None] * tok_count + offsets[None, :]) // BLOCK).reshape(pair_rows)

    def source_blocks(step_index):
        return pair_blocks((place - step_index) % SEQ_SPAN)

    query_blocks = pair_blocks(place)
    w_query, w_key, w_value, w_out, gain_one, gain_two, bias_query, bias_key, bias_value = (
        lax.all_gather(q_weight.astype(jnp.bfloat16), ("head", "blk"), axis=0, tiled=True),
        lax.all_gather(k_weight.astype(jnp.bfloat16), ("head", "blk"), axis=0, tiled=True),
        lax.all_gather(v_weight.astype(jnp.bfloat16), ("head", "blk"), axis=0, tiled=True),
        lax.all_gather(o_weight.astype(jnp.bfloat16), ("head", "blk"), axis=0, tiled=True),
        lax.all_gather(norm1.astype(jnp.bfloat16), ("head", "blk"), axis=0, tiled=True),
        lax.all_gather(norm2.astype(jnp.bfloat16), ("head", "blk"), axis=0, tiled=True),
        lax.all_gather(q_bias.astype(jnp.bfloat16), ("head", "blk"), axis=0, tiled=True),
        lax.all_gather(k_bias.astype(jnp.bfloat16), ("head", "blk"), axis=0, tiled=True),
        lax.all_gather(v_bias.astype(jnp.bfloat16), ("head", "blk"), axis=0, tiled=True),
    )
    inputs = hidden.astype(jnp.float32)
    gain_first = gain_one.astype(jnp.float32)
    gain_second = gain_two.astype(jnp.float32)
    normed = rms_scale(inputs, gain_first).astype(jnp.bfloat16)
    angles = angles_of(own_positions, HEAD_DIM)
    query_pre = jnp.dot(normed, w_query, preferred_element_type=jnp.float32) + bias_query.astype(
        jnp.float32
    )
    key_pre = jnp.dot(normed, w_key, preferred_element_type=jnp.float32) + bias_key.astype(
        jnp.float32
    )
    value_rows = (
        jnp.dot(normed, w_value, preferred_element_type=jnp.float32)
        + bias_value.astype(jnp.float32)
    ).astype(jnp.bfloat16)
    query_turned = (
        rotate(query_pre.reshape(tok_count, QHEADS, HEAD_DIM), angles, 1.0)
        .reshape(tok_count, QHEADS * HEAD_DIM)
        .astype(jnp.bfloat16)
    )
    key_turned = (
        rotate(key_pre.reshape(tok_count, KVHEADS, HEAD_DIM), angles, 1.0)
        .reshape(tok_count, KVHEADS * HEAD_DIM)
        .astype(jnp.bfloat16)
    )
    queries, key_local, value_local = (
        lax.all_to_all(query_turned, "head", split_axis=1, concat_axis=0, tiled=True),
        lax.all_to_all(key_turned, "head", split_axis=1, concat_axis=0, tiled=True),
        lax.all_to_all(value_rows, "head", split_axis=1, concat_axis=0, tiled=True),
    )
    query_heads = queries.reshape(pair_rows, local_heads, HEAD_DIM)

    def score_block(key_block, key_blocks):
        raw = (
            jnp.einsum("qgd,cd->gqc", query_heads, key_block, preferred_element_type=jnp.float32)
            * scale
        )
        allowed = key_blocks[None, :] <= query_blocks[:, None]
        return jnp.where(allowed[None], raw, NEG)

    def update_stats(top, total, key_block, step_index):
        scores = score_block(key_block, source_blocks(step_index))
        new_top = jnp.maximum(top, jnp.max(scores, axis=-1))
        total = total * jnp.exp(top - new_top) + jnp.sum(
            jnp.exp(scores - new_top[..., None]), axis=-1
        )
        return (new_top, total)

    def visit_turn(carry, step_index):
        key_block, value_block, top, total = carry
        top, total = update_stats(top, total, key_block, step_index)
        key_next, value_next = passed_along((key_block, value_block), "blk", seq_count)
        return ((key_next, value_next, top, total), (key_block, value_block))

    start_stats = (
        key_local,
        value_local,
        jnp.full((local_heads, pair_rows), NEG, jnp.float32),
        jnp.zeros((local_heads, pair_rows), jnp.float32),
    )
    carry, stored = lax.scan(visit_turn, start_stats, jnp.arange(SEQ_SPAN - 1, dtype=jnp.int32))
    last_key, last_value, top, total = carry
    top, total = update_stats(top, total, last_key, SEQ_SPAN - 1)
    log_total = top + jnp.log(total)
    key_store = jnp.concatenate([stored[0], last_key[None]], axis=0)
    value_store = jnp.concatenate([stored[1], last_value[None]], axis=0)
    all_steps = jnp.arange(SEQ_SPAN, dtype=jnp.int32)

    def add_output(running, items):
        key_block, value_block, step_index = items
        shares_low = jnp.exp(
            score_block(key_block, source_blocks(step_index)) - log_total[..., None]
        ).astype(jnp.bfloat16)
        return (
            running
            + jnp.einsum(
                "gqc,cd->gqd", shares_low, value_block, preferred_element_type=jnp.float32
            ),
            None,
        )

    attended, _ = lax.scan(
        add_output,
        jnp.zeros((local_heads, pair_rows, HEAD_DIM), jnp.float32),
        (key_store, value_store, all_steps),
    )
    attn_local = (
        attended.transpose(1, 0, 2).reshape(pair_rows, local_heads * HEAD_DIM).astype(jnp.bfloat16)
    )
    attn_rows = lax.all_to_all(attn_local, "head", split_axis=0, concat_axis=1, tiled=True)
    mixed = inputs + jnp.dot(attn_rows, w_out, preferred_element_type=jnp.float32)
    normed_two = rms_scale(mixed, gain_second).astype(jnp.bfloat16)
    gate_rows, up_rows, down_rows = (
        lax.all_gather(gate_weight.astype(jnp.bfloat16), "blk", axis=0, tiled=True),
        lax.all_gather(up_weight.astype(jnp.bfloat16), "blk", axis=0, tiled=True),
        lax.all_gather(down_weight.astype(jnp.bfloat16), "blk", axis=0, tiled=True),
    )
    w_gate, w_up, w_down = (
        lax.all_gather(gate_rows, "head", axis=1, tiled=True),
        lax.all_gather(up_rows, "head", axis=1, tiled=True),
        lax.all_gather(down_rows, "head", axis=1, tiled=True),
    )
    width = w_gate.shape[1]
    gate_act = jnp.dot(normed_two, w_gate, preferred_element_type=jnp.float32)
    up_act = jnp.dot(normed_two, w_up, preferred_element_type=jnp.float32)
    hidden_act = (jax.nn.silu(gate_act) * up_act).astype(jnp.bfloat16)
    branch_part = over_columns(hidden_act, w_down)
    hidden_grad_act = jnp.dot(cotangent, w_down, preferred_element_type=jnp.float32)
    sigmoid_gate = jax.nn.sigmoid(gate_act)
    gate_grad = (
        hidden_grad_act * up_act * sigmoid_gate * (1.0 + gate_act * (1.0 - sigmoid_gate))
    ).astype(jnp.bfloat16)
    up_grad = (hidden_grad_act * gate_act * sigmoid_gate).astype(jnp.bfloat16)
    normed_part = over_columns(gate_grad, w_gate) + over_columns(up_grad, w_up)
    output = (mixed + branch_part).astype(jnp.bfloat16)
    out_grad = cotangent.astype(jnp.float32)
    row_share = D // lax.axis_size("blk")
    mlp_sums = lax.psum_scatter(
        jnp.concatenate(
            [
                over_rows(normed_two, gate_grad),
                over_rows(normed_two, up_grad),
                over_rows(cotangent, hidden_act),
            ],
            axis=1,
        ),
        "blk",
        scatter_dimension=0,
        tiled=True,
    )
    split_sums = mlp_sums.reshape(row_share, 3, head_count, width // head_count)
    mlp_parts = (
        lax.psum_scatter(split_sums.astype(jnp.bfloat16), "head", scatter_dimension=2, tiled=True)
        .astype(jnp.float32)
        .reshape(row_share, 3, width // head_count)
    )
    _, second_pull = jax.vjp(rms_scale, mixed, gain_second)
    mixed_norm_grad, gain_two_grad = second_pull(normed_part)
    mixed_grad = out_grad + mixed_norm_grad
    proj_grad = mixed_grad.astype(jnp.bfloat16)
    w_out_grad = over_rows(attn_rows, proj_grad)
    attn_grad = over_columns(proj_grad, w_out).astype(jnp.bfloat16)
    out_heads = lax.all_to_all(attn_grad, "head", split_axis=1, concat_axis=0, tiled=True).reshape(
        pair_rows, local_heads, HEAD_DIM
    )
    delta = jnp.einsum("qgd,gqd->gq", out_heads.astype(jnp.float32), attended)

    def block_grads(query_sum, step_index):
        key_block = lax.dynamic_index_in_dim(key_store, step_index, 0, keepdims=False)
        value_block = lax.dynamic_index_in_dim(value_store, step_index, 0, keepdims=False)
        shares = jnp.exp(score_block(key_block, source_blocks(step_index)) - log_total[..., None])
        value_part = jnp.einsum(
            "gqc,qgd->cd",
            shares.astype(jnp.bfloat16),
            out_heads,
            preferred_element_type=jnp.float32,
        )
        share_grad = jnp.einsum(
            "qgd,cd->gqc", out_heads, value_block, preferred_element_type=jnp.float32
        )
        score_grad = (shares * (share_grad - delta[..., None])).astype(jnp.bfloat16)
        query_sum = (
            query_sum
            + jnp.einsum("gqc,cd->qgd", score_grad, key_block, preferred_element_type=jnp.float32)
            * scale
        )
        key_part = (
            jnp.einsum("gqc,qgd->cd", score_grad, query_heads, preferred_element_type=jnp.float32)
            * scale
        )
        return (query_sum, key_part, value_part)

    first_sums = block_grads(
        jnp.zeros((pair_rows, local_heads, HEAD_DIM), jnp.float32), 1 % SEQ_SPAN
    )

    def return_turn(carry, step_index):
        query_sum, key_sum, value_sum = carry
        key_sum, value_sum = (
            passed_along(key_sum.astype(jnp.bfloat16), "blk", seq_count).astype(key_sum.dtype),
            passed_along(value_sum.astype(jnp.bfloat16), "blk", seq_count).astype(value_sum.dtype),
        )
        query_sum, key_part, value_part = block_grads(query_sum, (step_index + 1) % SEQ_SPAN)
        return ((query_sum, key_sum + key_part, value_sum + value_part), None)

    (query_sum, key_sum, value_sum), _ = lax.scan(
        return_turn, first_sums, jnp.arange(1, SEQ_SPAN, dtype=jnp.int32)
    )
    query_back = query_sum.reshape(pair_rows, local_heads * HEAD_DIM).astype(jnp.bfloat16)
    query_grad, key_grad, value_grad = (
        lax.all_to_all(query_back, "head", split_axis=0, concat_axis=1, tiled=True),
        lax.all_to_all(
            key_sum.astype(jnp.bfloat16), "head", split_axis=0, concat_axis=1, tiled=True
        ),
        lax.all_to_all(
            value_sum.astype(jnp.bfloat16), "head", split_axis=0, concat_axis=1, tiled=True
        ),
    )
    query_pre_grad = (
        rotate(query_grad.astype(jnp.float32).reshape(tok_count, QHEADS, HEAD_DIM), angles, -1.0)
        .reshape(tok_count, QHEADS * HEAD_DIM)
        .astype(jnp.bfloat16)
    )
    key_pre_grad = (
        rotate(key_grad.astype(jnp.float32).reshape(tok_count, KVHEADS, HEAD_DIM), angles, -1.0)
        .reshape(tok_count, KVHEADS * HEAD_DIM)
        .astype(jnp.bfloat16)
    )
    w_query_grad = over_rows(normed, query_pre_grad)
    w_key_grad = over_rows(normed, key_pre_grad)
    w_value_grad = over_rows(normed, value_grad)
    bias_query_grad = jnp.sum(query_pre_grad.astype(jnp.float32), axis=0)
    bias_key_grad = jnp.sum(key_pre_grad.astype(jnp.float32), axis=0)
    bias_value_grad = jnp.sum(value_grad.astype(jnp.float32), axis=0)
    normed_grad = (
        over_columns(query_pre_grad, w_query)
        + over_columns(key_pre_grad, w_key)
        + over_columns(value_grad, w_value)
    )
    _, first_pull = jax.vjp(rms_scale, inputs, gain_first)
    input_norm_grad, gain_one_grad = first_pull(normed_grad)
    input_grad = (mixed_grad + input_norm_grad).astype(jnp.bfloat16)
    sums = (
        lax.psum_scatter(w_query_grad, ("head", "blk"), scatter_dimension=0, tiled=True),
        lax.psum_scatter(w_key_grad, ("head", "blk"), scatter_dimension=0, tiled=True),
        lax.psum_scatter(w_value_grad, ("head", "blk"), scatter_dimension=0, tiled=True),
        lax.psum_scatter(w_out_grad, ("head", "blk"), scatter_dimension=0, tiled=True),
        lax.psum_scatter(gain_one_grad, ("head", "blk"), scatter_dimension=0, tiled=True),
        lax.psum_scatter(gain_two_grad, ("head", "blk"), scatter_dimension=0, tiled=True),
        lax.psum_scatter(bias_query_grad, ("head", "blk"), scatter_dimension=0, tiled=True),
        lax.psum_scatter(bias_key_grad, ("head", "blk"), scatter_dimension=0, tiled=True),
        lax.psum_scatter(bias_value_grad, ("head", "blk"), scatter_dimension=0, tiled=True),
    )
    return (
        output,
        input_grad,
        sums[4],
        sums[0],
        sums[6],
        sums[1],
        sums[7],
        sums[2],
        sums[8],
        sums[3],
        sums[5],
        mlp_parts[:, 0],
        mlp_parts[:, 1],
        mlp_parts[:, 2],
    )


def solution(mesh):
    return jax.shard_map(
        shards,
        mesh=mesh,
        in_specs=(
            P(("head", "blk"), None),
            P(("head", "blk"), None),
            P(),
            P(("head", "blk")),
            P(("head", "blk"), None),
            P(("head", "blk")),
            P(("head", "blk"), None),
            P(("head", "blk")),
            P(("head", "blk"), None),
            P(("head", "blk")),
            P(("head", "blk"), None),
            P(("head", "blk")),
            P("blk", "head"),
            P("blk", "head"),
            P("blk", "head"),
        ),
        out_specs=(
            P(("head", "blk"), None),
            P(("head", "blk"), None),
            P(("head", "blk")),
            P(("head", "blk"), None),
            P(("head", "blk")),
            P(("head", "blk"), None),
            P(("head", "blk")),
            P(("head", "blk"), None),
            P(("head", "blk")),
            P(("head", "blk"), None),
            P(("head", "blk")),
            P("blk", "head"),
            P("blk", "head"),
            P("blk", "head"),
        ),
        check_vma=False,
    )
```

profile of v0, /device:TPU:0, one launch (start us, length us, event | category | flops | bytes accessed | tf_op | source)
XLA Modules:
  0.0 3975.1 jit_solution(11569386613981516607)
XLA Ops:
  14.7 107.1 %all-gather.17.cloned.1.call-done = bf16[1536,4480]{1,0:T(8,128)(2,1)} async-done(((bf16[96,4480]{1,0:T(8,128)(2,1)}), bf16[1536,4480]{1,0:T(8,128)(2,1)}) %all-gather.17.cloned.1.call-update) | async-done | bytes 13762576 | tf_op jit(solution)/shard_map/all_gather | solution.py:203
  123.7 39.4 all-reduce.11
  163.4 45.1 %all_gather.48 = bf16[1536,256]{1,0:T(8,128)(2,1)S(1)} all-gather(bf16[48,256]{1,0:T(8,128)(2,1)S(1)} %convert_element_type.231), channel_id=1, replica_groups=mesh['head'=2,'blk'=16] {'head','blk'}, dimensions={0}, use_global_device_ids=true | all-gather | bytes 811008 | tf_op jit(solution)/shard_map/all_gather | solution.py:101
  217.2 42.5 %all_gather.46 = bf16[1536,256]{1,0:T(8,128)(2,1)S(1)} all-gather(bf16[48,256]{1,0:T(8,128)(2,1)S(1)} %convert_element_type.227), channel_id=1, replica_groups=mesh['head'=2,'blk'=16] {'head','blk'}, dimensions={0}, use_global_device_ids=true | all-gather | bytes 811008 | tf_op jit(solution)/shard_map/all_gather | solution.py:100
  305.2 176.6 %while.54 = (s32[]{:T(128)}, bf16[512,128]{1,0:T(8,128)(2,1)S(1)}, bf16[512,128]{1,0:T(8,128)(2,1)S(1)}, f32[6,512]{1,0:T(8,128)S(1)}, f32[6,512]{1,0:T(8,128)S(...) while((s32[]{:T(128)}, bf16[512,128]{1,0:T(8,128)(2,1)S(1)}, ...), condition=%wide.region_4.5_spmd.clone, body=%wide.region_1.4_spmd.clone.sunk | while | flops 413957152 | bytes 16564707 | solution.py:169
  489.2 91.8 %while.55 = (s32[]{:T(128)}, f32[6,512,128]{2,1,0:T(8,128)S(1)}, s32[16]{0:T(128)S(1)}, s32[]{:T(128)}, s32[32]{0:T(128)S(1)}, /*index=5*/bf16[16,512,128]{2,1,0...) while((s32[]{:T(128)}, f32[6,512,128]{2,1,0:T(8,128)S(1)}, ...), condition=%wide.region_8.9_spmd.clone, body=%wide.region_7.8_spmd.clone.sunk | while | flops 812662784 | bytes 4753277 | solution.py:190
  593.6 17.2 all-to-all-done.3
  616.2 218.3 %all-gather.19.cloned.1.call-done = bf16[1536,8960]{1,0:T(8,128)(2,1)} async-done(((bf16[1536,4480]{1,0:T(8,128)(2,1)}), bf16[1536,8960]{1,0:T(8,128)(2,1)}) %all-gather.19.cloned.1.call-update) | async-done | bytes 27525136 | tf_op jit(solution)/shard_map/all_gather | solution.py:208
  834.5 17.5 fusion.137
  851.9 306.1 %all-gather.15.cloned.1.call-done = bf16[1536,8960]{1,0:T(8,128)(2,1)} async-done(((bf16[1536,4480]{1,0:T(8,128)(2,1)}), bf16[1536,8960]{1,0:T(8,128)(2,1)}) %all-gather.15.cloned.1.call-update) | async-done | bytes 27525136 | tf_op jit(solution)/shard_map/all_gather | solution.py:207
  1158.1 17.4 fusion.136
  1175.4 306.2 %all-gather.23.cloned.1.call-done = bf16[1536,8960]{1,0:T(8,128)(2,1)} async-done(((bf16[1536,4480]{1,0:T(8,128)(2,1)}), bf16[1536,8960]{1,0:T(8,128)(2,1)}) %all-gather.23.cloned.1.call-update) | async-done | bytes 27525136 | tf_op jit(solution)/shard_map/all_gather | solution.py:209
  1481.6 25.1 multiply_convert_fusion
  1506.8 23.4 convolution_bitcast_fusion.1
  1530.2 23.6 fusion.141
  1553.8 23.5 fusion.140
  1577.3 105.9 %pad_maximum_fusion = f32[1536,26880]{1,0:T(8,128)} fusion(f32[1536,8960]{1,0:T(8,128)} %convolution_bitcast_fusion.1, f32[1536,8960]{1,0:T(8,128)} %fusion.141, f32[1536,8960]{1,0:T(8,128)} %fusion.140), kind=kLoop, calls=%fused_computation.106 | loop fusion | flops 82575360 | bytes 330301440 | tf_op jit(solution)/shard_map/concatenate | solution.py:227
  1700.3 20.8 multiply_reduce_fusion.1
  1763.3 1395.9 %reduce-scatter.15.cloned.1.call-done = f32[96,26880]{1,0:T(8,128)} async-done(((f32[1536,26880]{1,0:T(8,128)}), f32[96,26880]{1,0:T(8,128)}) %reduce-scatter.15.cloned.1.call-update) | async-done | bytes 10321936 | tf_op jit(solution)/shard_map/reduce_scatter | solution.py:226
  3179.1 297.6 %while.53 = (s32[]{:T(128)}, f32[512,6,128]{0,2,1:T(8,128)S(1)}, bf16[512,128]{1,0:T(8,128)(2,1)}, bf16[512,128]{1,0:T(8,128)(2,1)}, s32[15]{0:T(128)S(1)}, /*in...) while((s32[]{:T(128)}, f32[512,6,128]{0,2,1:T(8,128)S(1)}, ...), condition=%wide.region_12.13_spmd.clone, body=%wide.region_11.12_spmd.clone.sunk | while | flops 2030518272 | bytes 90891000 | solution.py:294
  3546.8 41.1 %all-reduce.10 = (f32[1536]{0:T(1024)S(1)}, f32[1536]{0:T(1024)S(1)}, f32[256]{0:T(256)S(1)}, f32[256]{0:T(256)S(1)}, f32[1536]{0:T(1024)S(1)}) all-reduce(f32[1536]{0:T(1024)S(1)} %get-tuple-element.757, f32[1536]{0:T(1024)S(1)} %bitcast.377, f32[256]{0:T(256)S(1)} %bitcast.382, ...), channel_id=2, replica_groups=mesh['head'=2,'blk'=16] {'head','blk'}, use_global_device_ids=true, to_apply=%region_15.16.clone | all-reduce | flops 5120 | bytes 40960
  3598.1 87.1 %reduce-scatter.9.cloned.1.call-done = f32[48,256]{1,0:T(8,128)} async-done(((f32[1536,256]{1,0:T(8,128)}), f32[48,256]{1,0:T(8,128)}) %reduce-scatter.9.cloned.1.call-update) | async-done | bytes 49168 | tf_op jit(solution)/shard_map/reduce_scatter | solution.py:333
  3685.2 141.0 %reduce-scatter.13.cloned.1.call-done = f32[48,1536]{1,0:T(8,128)} async-done(((f32[1536,1536]{1,0:T(8,128)}), f32[48,1536]{1,0:T(8,128)}) %reduce-scatter.13.cloned.1.call-update) | async-done | bytes 294928 | tf_op jit(solution)/shard_map/reduce_scatter | solution.py:335
  3826.2 142.2 %reduce-scatter.7.cloned.1.call-done = f32[48,1536]{1,0:T(8,128)} async-done(((f32[1536,1536]{1,0:T(8,128)}), f32[48,1536]{1,0:T(8,128)}) %reduce-scatter.7.cloned.1.call-update) | async-done | bytes 294928 | tf_op jit(solution)/shard_map/reduce_scatter | solution.py:332
  (1134 shorter events, 779.1 us)
Async XLA Ops:
  7.2 114.6 %all-gather.17.cloned.1.call-start = ((), (), s32[]{:S(2)}) async-start(), calls=%async_computation.18 | async-start | bytes 14622720 | tf_op jit(solution)/shard_map/all_gather | solution.py:203
  9.8 253.2 %all-gather.9.cloned.1.call-start = ((), (), s32[]{:S(2)}) async-start(), calls=%async_computation.14 | async-start | bytes 4866048 | tf_op jit(solution)/shard_map/all_gather | solution.py:99
  11.7 292.8 %all-gather.13.cloned.1.call-start = ((), (), s32[]{:S(2)}) async-start(), calls=%async_computation.16 | async-start | bytes 14622720 | tf_op jit(solution)/shard_map/all_gather | solution.py:202
  12.7 475.0 %all-gather.21.cloned.1.call-start = ((), (), s32[]{:S(2)}) async-start(), calls=%async_computation.20 | async-start | bytes 14622720 | tf_op jit(solution)/shard_map/all_gather | solution.py:204
  13.8 579.7 %all-gather.11.cloned.1.call-start = ((), (), s32[]{:S(2)}) async-start(), calls=%async_computation.15 | async-start | bytes 4866048 | tf_op jit(solution)/shard_map/all_gather | solution.py:102
  14.6 819.9 %all-gather.19.cloned.1.call-start = ((), (), s32[]{:S(2)}) async-start(), calls=%async_computation.19 | async-start | bytes 41287680 | tf_op jit(solution)/shard_map/all_gather | solution.py:208
  210.6 59.7 %all-to-all-start.1 = ((bf16[256,2,128]{0,2,1:T(8,128)(2,1)}), bf16[256,2,128]{0,2,1:T(8,128)(2,1)S(1)}, u32[]{:S(2)}, u32[]{:S(2)}) async-start(bf16[256,2,128]{0,2,1:T(8,128)(2,1)} %bitcast.6), calls=%async_computation.1 | async-start | bytes 262144 | tf_op jit(solution)/shard_map/all_to_all | solution.py:137
  281.8 876.3 %all-gather.15.cloned.1.call-start = ((), (), s32[]{:S(2)}) async-start(), calls=%async_computation.17 | async-start | bytes 41287680 | tf_op jit(solution)/shard_map/all_gather | solution.py:207
  304.5 1177.1 %all-gather.23.cloned.1.call-start = ((), (), s32[]{:S(2)}) async-start(), calls=%async_computation.21 | async-start | bytes 41287680 | tf_op jit(solution)/shard_map/all_gather | solution.py:209
  589.5 21.2 all-to-all-start.3
  593.1 2566.1 %reduce-scatter.15.cloned.1.call-start = ((), (), s32[]{:S(2)}) async-start(), calls=%async_computation.26 | async-start | bytes 175472640 | tf_op jit(solution)/shard_map/reduce_scatter | solution.py:226
  1731.0 1862.6 %reduce-scatter.17.cloned.1.call-start = ((), (), s32[]{:S(2)}) async-start(), calls=%async_computation.27 | async-start | bytes 7741440 | tf_op jit(solution)/shard_map/reduce_scatter | solution.py:241
  3178.0 420.1 %reduce-scatter.11.cloned.1.call-start = ((), (), s32[]{:S(2)}) async-start(), calls=%async_computation.24 | async-start | bytes 1622016 | tf_op jit(solution)/shard_map/reduce_scatter | solution.py:334
  3179.2 17.8 collective-permute-start
  3237.7 18.4 collective-permute-start
  3258.7 17.4 collective-permute-start
  3297.3 17.3 collective-permute-start
  3317.3 18.9 collective-permute-start
  3338.8 17.7 collective-permute-start
  3397.2 18.4 collective-permute-start
  3418.2 17.4 collective-permute-start
  3486.4 198.8 %reduce-scatter.9.cloned.1.call-start = ((), (), s32[]{:S(2)}) async-start(), calls=%async_computation.23 | async-start | bytes 1622016 | tf_op jit(solution)/shard_map/reduce_scatter | solution.py:333
  3496.3 329.9 %reduce-scatter.13.cloned.1.call-start = ((), (), s32[]{:S(2)}) async-start(), calls=%async_computation.25 | async-start | bytes 9732096 | tf_op jit(solution)/shard_map/reduce_scatter | solution.py:335
  3502.8 465.7 %reduce-scatter.7.cloned.1.call-start = ((), (), s32[]{:S(2)}) async-start(), calls=%async_computation.22 | async-start | bytes 9732096 | tf_op jit(solution)/shard_map/reduce_scatter | solution.py:332
  (187 other events, 3853.5 us)
Sparse Core Ops, SparseCore 0:
  10.9 110.8 all-gather.16
  125.3 64.4 all-gather.8
  192.6 111.8 all-gather.12
  306.7 122.8 all-gather.20
  432.9 70.9 all-gather.10
  505.2 329.1 all-gather.18
  836.0 321.9 all-gather.14
  1159.6 321.9 all-gather.22
  1683.3 1475.8 reduce-scatter.14
  3178.1 63.9 reduce-scatter.16
  3486.5 96.8 reduce-scatter.10
  3589.1 96.1 reduce-scatter.8
  3691.7 134.4 reduce-scatter.12
  3833.5 134.8 reduce-scatter.6
where the time goes:
time: 3990 us; the launch traced here: 3980 us
  waiting for transfers between devices  2840 us (71%)
  matrix products  542 us (14%)
  blocking collectives  194 us (5%)
  other arithmetic  183 us (5%)
  local copies, waits for them, and re-layouts  121 us (3%)
  starting transfers between devices  42.2 us (1%)
    reduce_scatter x1, waiting for transfers between devices, shards(): lax.psum_scatter(jnp.concatenate([over_rows(normed_two, gate_grad), over_...  1400 us
    all_gather x1, waiting for transfers between devices, shards(): lax.all_gather(down_rows, 'head', axis=1, tiled=True)  306 us
    all_gather x1, waiting for transfers between devices, shards(): lax.all_gather(gate_rows, 'head', axis=1, tiled=True)  306 us
    all_gather x1, waiting for transfers between devices, shards(): lax.all_gather(up_rows, 'head', axis=1, tiled=True)  218 us
    reduce_scatter x1, waiting for transfers between devices, shards(): lax.psum_scatter(w_query_grad, ('head', 'blk'), scatter_dimension=0, tile...  142 us
    reduce_scatter x1, waiting for transfers between devices, shards(): lax.psum_scatter(w_out_grad, ('head', 'blk'), scatter_dimension=0, tiled=...  141 us
    all_gather x1, waiting for transfers between devices, shards(): lax.all_gather(up_weight.astype(jnp.bfloat16), 'blk', axis=0, tiled=True)  107 us
    concatenate x1, other arithmetic, shards(): jnp.concatenate([over_rows(normed_two, gate_grad), over_rows(normed_two,...  106 us
  transfers between devices with their start and end apart: 79, of which 43 were waited for; matrix products, arithmetic and copies ran while one was open for 15% of the time, Pallas kernels for 0%

commit v1 on v0

v1 whole, which is shorter than its diff:
```python
import functools

import jax
import jax.numpy as jnp
import numpy as np
from jax import lax
from jax.experimental import pallas as pl
from jax.experimental.pallas import tpu as pltpu
from jax.sharding import PartitionSpec as P

D = 1536
QHEADS = 12
KVHEADS = 2
HEAD_DIM = 128
SEQ_SPAN = 16
BLOCK = 256

EPS = 1e-06
THETA = 1000000.0
SCALE = HEAD_DIM**-0.5
LOG2E = 1.4426950408889634
SCALE2 = SCALE * LOG2E
BF = jnp.bfloat16
F32 = jnp.float32
MESH = pl.DeviceIdType.MESH
VMEM_LIMIT = 56 * 2**20
AXES = ("head", "g", "z", "y", "c")
BLK = ("g", "z", "y", "c")
LANES = 128


def dot_nn(a, b):
    return lax.dot_general(a, b, (((1,), (0,)), ((), ())), preferred_element_type=F32)


def dot_nt(a, b):
    return lax.dot_general(a, b, (((1,), (1,)), ((), ())), preferred_element_type=F32)


def dot_tn(a, b):
    return lax.dot_general(a, b, (((0,), (0,)), ((), ())), preferred_element_type=F32)


def live(axes, sizes):
    return tuple(a for a in axes if sizes[a] > 1)


def greet(axes, sizes):
    barrier = pltpu.get_barrier_semaphore()
    count = 0
    for a in axes:
        me = lax.axis_index(a)
        for d in range(1, sizes[a]):
            pl.semaphore_signal(
                barrier,
                inc=1,
                device_id={a: lax.rem(me + d, sizes[a])},
                device_id_type=MESH,
            )
            count += 1
    pl.semaphore_wait(barrier, count)


def place_of(offsets, axes, sizes):
    value = 0
    for a in axes:
        me = lax.axis_index(a)
        off = offsets.get(a, 0)
        value = value * sizes[a] + (lax.rem(me + off, sizes[a]) if off else me)
    return value


def remote(src, dst, send, recv, axis, distance, sizes):
    to = lax.rem(lax.axis_index(axis) + distance, sizes[axis])
    return pltpu.make_async_remote_copy(
        src_ref=src,
        dst_ref=dst,
        send_sem=send,
        recv_sem=recv,
        device_id={axis: to},
        device_id_type=MESH,
    )


def gather_kernel(plans, sizes, *refs):
    count = len(plans)
    xs, outs = refs[:count], refs[count : 2 * count]
    send_sems, recv_sems, local_sems = refs[2 * count :]
    greet(live(AXES, {a: (sizes[a] if any(a in p[0] for p in plans) else 1) for a in AXES}), sizes)
    sends, locals_, queue = [], [], []
    sem = 0
    for i, (axes, split) in enumerate(plans):
        mine = xs[i].at[lax.axis_index(axes[0])] if split else xs[i]
        copy = pltpu.make_async_copy(mine, outs[i].at[place_of({}, axes, sizes)], local_sems.at[i])
        copy.start()
        locals_.append(copy)
        queue.append((i, {}, -1, None))
    at = 0
    while at < len(queue):
        i, offsets, phase, arrived = queue[at]
        at += 1
        axes, split = plans[i]
        slot = outs[i].at[place_of(offsets, axes, sizes)]
        if arrived is None:
            src = xs[i].at[lax.axis_index(axes[0])] if split else xs[i]
        else:
            src = slot
            remote(
                slot, slot, send_sems.at[arrived], recv_sems.at[arrived], axes[0], 0, sizes
            ).wait_recv()
        for p in range(phase + 1, len(axes)):
            a = axes[p]
            for d in range(1, sizes[a]):
                piece = src
                if split and p == 0:
                    piece = xs[i].at[lax.rem(lax.axis_index(a) + d, sizes[a])]
                copy = remote(piece, slot, send_sems.at[sem], recv_sems.at[sem], a, d, sizes)
                copy.start()
                sends.append(copy)
                later = dict(offsets)
                later[a] = sizes[a] - d
                queue.append((i, later, p, sem))
                sem += 1
    for copy in locals_:
        copy.wait()
    for copy in sends:
        copy.wait_send()


def gather(arrays, plans, sizes, collective_id):
    plans = [(live(axes, sizes), split) for axes, split in plans]
    counts = [int(np.prod([sizes[a] for a in axes])) for axes, _ in plans]
    total = sum(counts) - len(counts)
    shapes = [
        jax.ShapeDtypeStruct((n,) + (x.shape[1:] if split else x.shape), x.dtype)
        for n, x, (_, split) in zip(counts, arrays, plans)
    ]
    spec = pl.BlockSpec(memory_space=pltpu.VMEM)
    return pl.pallas_call(
        functools.partial(gather_kernel, plans, sizes),
        out_shape=shapes,
        in_specs=[spec] * len(arrays),
        out_specs=[spec] * len(arrays),
        scratch_shapes=[
            pltpu.SemaphoreType.DMA((total,)),
            pltpu.SemaphoreType.DMA((total,)),
            pltpu.SemaphoreType.DMA((len(arrays),)),
        ],
        compiler_params=pltpu.CompilerParams(
            collective_id=collective_id, has_side_effects=True, vmem_limit_bytes=VMEM_LIMIT
        ),
        cost_estimate=pl.CostEstimate(flops=0, bytes_accessed=60 * 2**20, transcendentals=0),
    )(*arrays)


def offset_keys(axes, sizes):
    keys = [{}]
    for a in axes:
        keys = [dict(k, **{a: d}) for k in keys for d in list(range(1, sizes[a])) + [0]]
    return keys


def scatter_kernel(plans, sizes, *refs):
    count = len(plans)
    xs, outs = refs[:count], refs[count : 2 * count]
    at = 2 * count
    bufs = []
    for axes, swap in plans:
        phases = len(axes)
        bufs.append((refs[at : at + phases], refs[at + phases : at + 2 * phases]))
        at += 2 * phases
    send_sems, recv_sems, local_sems = refs[at:]
    used = {
        a: (
            sizes[a]
            if any(a in axes or (swap and a == "head") for axes, swap in plans)
            else 1
        )
        for a in AXES
    }
    greet(live(AXES, used), sizes)
    sem = 0
    sends = []
    arrivals = [dict() for _ in plans]

    def number(offsets, axes):
        value = 0
        for a in axes:
            value = value * sizes[a] + offsets.get(a, 0)
        return value

    def total_of(i, offsets, phase):
        axes = plans[i][0]
        order = axes[::-1]
        total = xs[i][place_of(offsets, axes, sizes)].astype(F32)
        for q in range(phase):
            rest = axes[: len(axes) - 1 - q]
            for d in range(1, sizes[order[q]]):
                key = (q, d, number(offsets, rest))
                s = arrivals[i].pop(key)
                buf = bufs[i][1][q].at[d - 1, number(offsets, rest)]
                remote(buf, buf, send_sems.at[s], recv_sems.at[s], order[q], 0, sizes).wait_recv()
                total = total + buf[...].astype(F32)
        return total

    depth = max(len(axes) for axes, _ in plans)
    for phase in range(depth):
        for i, (axes, swap) in enumerate(plans):
            if phase >= len(axes):
                continue
            order = axes[::-1]
            a = order[phase]
            rest = axes[: len(axes) - 1 - phase]
            for d in range(1, sizes[a]):
                for key in offset_keys(rest, sizes):
                    offsets = dict(key)
                    offsets[a] = d
                    where = number(key, rest)
                    if phase == 0:
                        src = xs[i].at[place_of(offsets, axes, sizes)]
                    else:
                        src = bufs[i][0][phase].at[d - 1, where]
                        src[...] = total_of(i, offsets, phase).astype(src.dtype)
                    dst = bufs[i][1][phase].at[d - 1, where]
                    copy = remote(src, dst, send_sems.at[sem], recv_sems.at[sem], a, d, sizes)
                    copy.start()
                    sends.append(copy)
                    arrivals[i][(phase, d, where)] = sem
                    sem += 1
    swaps = []
    for i, (axes, swap) in enumerate(plans):
        total = total_of(i, {}, len(axes))
        if swap:
            hold, out = bufs[i][0][0], outs[i]
            hold[...] = total.astype(hold.dtype)
            me = lax.axis_index("head")
            copy = pltpu.make_async_copy(hold.at[me], out.at[me], local_sems.at[i])
            copy.start()
            for d in range(1, sizes["head"]):
                to = lax.rem(me + d, sizes["head"])
                copy2 = remote(
                    hold.at[to], out.at[me], send_sems.at[sem], recv_sems.at[sem], "head", d, sizes
                )
                copy2.start()
                sends.append(copy2)
                source = out.at[lax.rem(me + sizes["head"] - d, sizes["head"])]
                swaps.append((source, sem))
                sem += 1
            swaps.append((copy, None))
        else:
            outs[i][...] = total.astype(outs[i].dtype)
    for item, s in swaps:
        if s is None:
            item.wait()
        else:
            remote(item, item, send_sems.at[s], recv_sems.at[s], "head", 0, sizes).wait_recv()
    for copy in sends:
        copy.wait_send()


def scatter(arrays, plans, out_types, sizes, collective_id):
    plans = [(live(axes, sizes), swap) for axes, swap in plans]
    scratch, total = [], 0
    for x, (axes, swap), kind in zip(arrays, plans, out_types):
        block = x.shape[1:]
        order = axes[::-1]
        send_bufs, recv_bufs = [], []
        for p, a in enumerate(order):
            rest = int(np.prod([sizes[b] for b in axes[: len(axes) - 1 - p]], dtype=int))
            shape = (sizes[a] - 1, rest) + block
            recv_bufs.append(pltpu.VMEM(shape, x.dtype))
            if p == 0:
                send_bufs.append(pltpu.VMEM(block if swap else (8, LANES), kind if swap else F32))
            else:
                send_bufs.append(pltpu.VMEM(shape, x.dtype))
            total += (sizes[a] - 1) * rest
        scratch += send_bufs + recv_bufs
        if swap:
            total += sizes["head"] - 1
    shapes = [jax.ShapeDtypeStruct(x.shape[1:], kind) for x, kind in zip(arrays, out_types)]
    spec = pl.BlockSpec(memory_space=pltpu.VMEM)
    return pl.pallas_call(
        functools.partial(scatter_kernel, plans, sizes),
        out_shape=shapes,
        in_specs=[spec] * len(arrays),
        out_specs=[spec] * len(arrays),
        scratch_shapes=scratch
        + [
            pltpu.SemaphoreType.DMA((total,)),
            pltpu.SemaphoreType.DMA((total,)),
            pltpu.SemaphoreType.DMA((len(arrays),)),
        ],
        compiler_params=pltpu.CompilerParams(
            collective_id=collective_id, has_side_effects=True, vmem_limit_bytes=VMEM_LIMIT
        ),
        cost_estimate=pl.CostEstimate(flops=0, bytes_accessed=60 * 2**20, transcendentals=0),
    )(*arrays)


def forward_kernel(heads, slots, tops, q_ref, kv_ref, o_ref, lse_ref, top_s, sum_s, acc_s):
    def score(keys, a, h):
        return dot_nt(keys, q_ref[a * BLOCK : (a + 1) * BLOCK, h * HEAD_DIM : (h + 1) * HEAD_DIM])

    for a in range(2):
        top_s[...] = jnp.full(top_s.shape, -1e30, F32)
        sum_s[...] = jnp.zeros(sum_s.shape, F32)
        acc_s[...] = jnp.zeros(acc_s.shape, F32)
        count = tops[a] + 1

        def step(keys, values_t):
            ahead = min(3, heads)
            ready = [score(keys, a, h) for h in range(ahead)]
            for h in range(heads):
                s = ready[h]
                if h + ahead < heads:
                    ready.append(score(keys, a, h + ahead))
                old = top_s[h : h + 1, :]
                new = jnp.maximum(old, jnp.max(s, axis=0, keepdims=True))
                p = jnp.exp2((s - new) * SCALE2)
                fade = jnp.exp2((old - new) * SCALE2)
                sum_s[h : h + 1, :] = sum_s[h : h + 1, :] * fade + jnp.sum(p, axis=0, keepdims=True)
                top_s[h : h + 1, :] = new
                acc_s[h] = acc_s[h] * fade + dot_nn(values_t, p.astype(BF))

        def two(i, carry):
            first, second = slots[2 * i], slots[2 * i + 1]
            both = jnp.concatenate([kv_ref[first], kv_ref[second]], axis=0)
            step(both[:, :HEAD_DIM], both[:, HEAD_DIM:].T)
            return carry

        lax.fori_loop(0, count // 2, two, 0)

        @pl.when(count % 2 == 1)
        def _():
            last = kv_ref[slots[count - 1]]
            step(last[:, :HEAD_DIM], last[:, HEAD_DIM:].T)

        for h in range(heads):
            total = sum_s[h : h + 1, :]
            o_ref[a * BLOCK : (a + 1) * BLOCK, h * HEAD_DIM : (h + 1) * HEAD_DIM] = (
                acc_s[h] / total
            ).T
            lse_ref[a, h : h + 1, :] = top_s[h : h + 1, :] * SCALE2 + jnp.log2(total)


def attend(slots, tops, q, kv):
    heads = q.shape[1] // HEAD_DIM
    spec = pl.BlockSpec(memory_space=pltpu.VMEM)
    pairs = 33 * BLOCK * BLOCK * heads
    return pl.pallas_call(
        functools.partial(forward_kernel, heads),
        grid_spec=pltpu.PrefetchScalarGridSpec(
            num_scalar_prefetch=2,
            grid=(1,),
            in_specs=[spec] * 2,
            out_specs=[spec] * 2,
            scratch_shapes=[
                pltpu.VMEM((8, BLOCK), F32),
                pltpu.VMEM((8, BLOCK), F32),
                pltpu.VMEM((heads, HEAD_DIM, BLOCK), F32),
            ],
        ),
        out_shape=(
            jax.ShapeDtypeStruct(q.shape, F32),
            jax.ShapeDtypeStruct((2, 8, BLOCK), F32),
        ),
        compiler_params=pltpu.CompilerParams(vmem_limit_bytes=VMEM_LIMIT),
        cost_estimate=pl.CostEstimate(
            flops=pairs * 4 * HEAD_DIM, bytes_accessed=80 * 2**20, transcendentals=pairs
        ),
    )(slots, tops, q, kv)


def backward_kernel(
    heads, slots, tops, q_ref, kv_ref, do_ref, lse_ref, delta_ref, dq_ref, dkv_ref, dq_s, dkv_s
):
    dkv_s[...] = jnp.zeros(dkv_s.shape, F32)
    for a in range(2):
        dq_s[...] = jnp.zeros(dq_s.shape, F32)

        def part(ref, h):
            return ref[a * BLOCK : (a + 1) * BLOCK, h * HEAD_DIM : (h + 1) * HEAD_DIM]

        def one(n, carry):
            slot = slots[n]
            keys, values = kv_ref[slot, :, :HEAD_DIM], kv_ref[slot, :, HEAD_DIM:]
            keys_t = keys.T

            def products(h):
                return dot_nt(keys, part(q_ref, h)), dot_nt(values, part(do_ref, h))

            dk = jnp.zeros((BLOCK, HEAD_DIM), F32)
            dv = jnp.zeros((BLOCK, HEAD_DIM), F32)
            ahead = min(2, heads)
            ready = [products(h) for h in range(ahead)]
            for h in range(heads):
                s, dp = ready[h]
                if h + ahead < heads:
                    ready.append(products(h + ahead))
                p = jnp.exp2(s * SCALE2 - lse_ref[a, h : h + 1, :])
                dv = dv + dot_nn(p.astype(BF), part(do_ref, h))
                ds = (p * (dp - delta_ref[a, h : h + 1, :])).astype(BF)
                dk = dk + dot_nn(ds, part(q_ref, h))
                dq_s[h] = dq_s[h] + dot_nn(keys_t, ds)
            dkv_s[slot, :, :HEAD_DIM] = dkv_s[slot, :, :HEAD_DIM] + dk
            dkv_s[slot, :, HEAD_DIM:] = dkv_s[slot, :, HEAD_DIM:] + dv
            return carry

        lax.fori_loop(0, tops[a] + 1, one, 0)
        for h in range(heads):
            dq_ref[a * BLOCK : (a + 1) * BLOCK, h * HEAD_DIM : (h + 1) * HEAD_DIM] = (
                (dq_s[h] * SCALE).T
            ).astype(BF)
    dkv_ref[:, :, :HEAD_DIM] = (dkv_s[:, :, :HEAD_DIM] * SCALE).astype(BF)
    dkv_ref[:, :, HEAD_DIM:] = dkv_s[:, :, HEAD_DIM:].astype(BF)


def attend_back(slots, tops, q, kv, do, lse, delta):
    heads = q.shape[1] // HEAD_DIM
    spec = pl.BlockSpec(memory_space=pltpu.VMEM)
    pairs = 33 * BLOCK * BLOCK * heads
    return pl.pallas_call(
        functools.partial(backward_kernel, heads),
        grid_spec=pltpu.PrefetchScalarGridSpec(
            num_scalar_prefetch=2,
            grid=(1,),
            in_specs=[spec] * 5,
            out_specs=[spec] * 2,
            scratch_shapes=[
                pltpu.VMEM((heads, HEAD_DIM, BLOCK), F32),
                pltpu.VMEM(kv.shape, F32),
            ],
        ),
        out_shape=(
            jax.ShapeDtypeStruct(q.shape, BF),
            jax.ShapeDtypeStruct(kv.shape, BF),
        ),
        compiler_params=pltpu.CompilerParams(vmem_limit_bytes=VMEM_LIMIT),
        cost_estimate=pl.CostEstimate(
            flops=pairs * 10 * HEAD_DIM, bytes_accessed=120 * 2**20, transcendentals=pairs
        ),
    )(slots, tops, q, kv, do, lse, delta)


def inverse_rms(value):
    return lax.rsqrt(jnp.mean(value * value, axis=-1, keepdims=True) + EPS)


def rotate(value, cosine, sine):
    rows, width = value.shape
    half = HEAD_DIM // 2
    parts = value.reshape(rows, width // HEAD_DIM, HEAD_DIM)
    first, second = parts[..., :half], parts[..., half:]
    cosine, sine = cosine[:, None, :], sine[:, None, :]
    return jnp.concatenate(
        [first * cosine - second * sine, second * cosine + first * sine], axis=-1
    ).reshape(rows, width)


def shift(value, axis, distance, sizes):
    n = sizes[axis]
    return lax.ppermute(value, axis, [(i, (i + distance) % n) for i in range(n)])


def small_rows(*rows):
    return jnp.stack(
        [jnp.pad(r.astype(F32), ((0, LANES - r.shape[0]),)) for r in rows]
        + [jnp.zeros((LANES,), F32)] * (8 - len(rows))
    )


def shards(
    sizes,
    hidden,
    cotangent,
    block_order,
    norm1,
    q_weight,
    q_bias,
    k_weight,
    k_bias,
    v_weight,
    v_bias,
    o_weight,
    norm2,
    gate_weight,
    up_weight,
    down_weight,
):
    tok = hidden.shape[0]
    pair = sizes["head"] * tok
    blk = int(np.prod([sizes[a] for a in BLK]))
    seqs = blk // SEQ_SPAN
    place_axes = {1: BLK, 2: BLK[:3], 4: BLK[:2]}[seqs]
    seq_axes = BLK[len(place_axes) :]
    head = lax.axis_index("head")
    place = place_of({}, place_axes, sizes)
    seq = place_of({}, seq_axes, sizes) if seq_axes else 0
    order = lax.dynamic_index_in_dim(block_order, seq, 0, keepdims=False)
    tops = lax.dynamic_slice_in_dim(order, place * 2, 2)
    slots = jnp.argsort(order).astype(jnp.int32)
    positions = (tops[:, None] * tok + jnp.arange(tok, dtype=jnp.int32)[None, :]).reshape(pair)
    frequency = THETA ** (-(jnp.arange(HEAD_DIM // 2, dtype=F32) * 2.0) / HEAD_DIM)
    angles = positions.astype(F32)[:, None] * frequency[None, :]
    cosine, sine = jnp.cos(angles), jnp.sin(angles)

    q_cols = D // 2
    kv_cols = HEAD_DIM
    rows = q_weight.shape[0]
    halves = [
        jnp.concatenate(
            [
                q_weight[:, i * q_cols : (i + 1) * q_cols],
                k_weight[:, i * kv_cols : (i + 1) * kv_cols],
                v_weight[:, i * kv_cols : (i + 1) * kv_cols],
            ],
            axis=1,
        ).astype(BF)
        for i in range(2)
    ]
    small = small_rows(
        *[v.astype(BF) for v in (norm1, norm2, q_bias, k_bias, v_bias)]
    )
    w_qkv, x_pair, small_all = gather(
        [jnp.stack(halves), hidden, small],
        [(AXES, True), (("head",), False), (AXES, False)],
        sizes,
        1,
    )
    w_qkv = w_qkv.reshape(D, q_cols + 2 * kv_cols)
    x_pair = x_pair.reshape(pair, D).astype(F32)
    gain_one = small_all[:, 0, :rows].reshape(D)
    gain_two = small_all[:, 1, :rows].reshape(D)
    bias_q = lax.dynamic_slice_in_dim(small_all[:, 2, :rows].reshape(D), head * q_cols, q_cols)
    bias_k, bias_v = (
        lax.dynamic_slice_in_dim(
            small_all[:, i, : k_bias.shape[0]].reshape(2 * kv_cols), head * kv_cols, kv_cols
        )
        for i in (3, 4)
    )

    nz = sizes["z"]
    width = gate_weight.shape[1]
    lanes = -(-width // (LANES * nz)) * LANES
    wide = lanes * nz
    z = lax.axis_index("z")
    core = lax.axis_index("c")
    ff_rows = gate_weight.shape[0]

    def quarters(weight):
        padded = jnp.pad(weight.astype(BF), ((0, 0), (0, wide - width)))
        return padded.reshape(ff_rows, nz, lanes).transpose(1, 0, 2)

    def spread(packed):
        got = [lax.dynamic_index_in_dim(packed, z, 0, keepdims=False)]
        for d in range(1, nz):
            piece = lax.dynamic_index_in_dim(packed, (z + d) % nz, 0, keepdims=False)
            got.append(shift(piece, "z", d, sizes))
        mine = jnp.stack(got)
        over = ("head", "g", "y")
        everything = lax.all_gather(mine, live(over, sizes), axis=0, tiled=False)
        everything = everything.reshape((2, sizes["g"], sizes["y"]) + mine.shape)
        other = lax.dynamic_index_in_dim(everything, 1 - core, 0, keepdims=False)
        keep = lax.dynamic_index_in_dim(everything, core, 0, keepdims=False)
        swapped = shift(other, "c", 1, sizes)
        both = jnp.where(core == 0, jnp.stack([keep, swapped]), jnp.stack([swapped, keep]))
        by_z = jnp.stack(
            [lax.dynamic_index_in_dim(both, (z - i) % nz, 3, keepdims=False) for i in range(nz)]
        )
        full = by_z.transpose(4, 2, 0, 3, 1, 5, 6)
        return full.reshape(full.shape[0], D, lanes)

    tied = lax.optimization_barrier((gate_weight, up_weight, down_weight, w_qkv))
    w_gate, w_up = spread(jnp.stack([quarters(tied[0]), quarters(tied[1])], axis=1))
    (w_down,) = spread(quarters(tied[2])[:, None])

    w_out = lax.all_gather(o_weight.astype(BF), live(AXES, sizes), axis=0, tiled=True)
    cot_all = lax.all_gather(cotangent, ("z", "c"), axis=0, tiled=True)

    scale_one = inverse_rms(x_pair)
    normed = (x_pair * scale_one * gain_one).astype(BF)
    qkv = dot_nn(normed, w_qkv)
    queries = rotate(qkv[:, :q_cols] + bias_q, cosine, sine).astype(BF)
    keys = rotate(qkv[:, q_cols : q_cols + kv_cols] + bias_k, cosine, sine).astype(BF)
    values = (qkv[:, q_cols + kv_cols :] + bias_v).astype(BF)
    (kv,) = gather(
        [jnp.concatenate([keys, values], axis=1)], [(place_axes, False)], sizes, 2
    )
    kv = kv.reshape(2 * SEQ_SPAN, tok, 2 * HEAD_DIM)
    attended, lse = attend(slots, tops, queries, kv)
    attn_local = attended.astype(BF)
    (attn_halves,) = gather([attn_local.reshape(2, tok, q_cols)], [(("head",), True)], sizes, 3)
    inputs = lax.dynamic_slice_in_dim(x_pair, head * tok, tok)
    mixed = inputs + (
        dot_nn(attn_halves[0], w_out[:q_cols]) + dot_nn(attn_halves[1], w_out[q_cols:])
    )
    scale_two = inverse_rms(mixed)
    normed_two = (mixed * scale_two * gain_two).astype(BF)
    (tokens,) = gather([normed_two], [(("z", "c"), False)], sizes, 4)
    tokens = tokens.reshape(-1, D)

    gate = dot_nn(tokens, w_gate)
    up = dot_nn(tokens, w_up)
    sig = jax.nn.sigmoid(gate)
    act = (gate * sig * up).astype(BF)
    dact = dot_nn(cot_all, w_down)
    dgate = (dact * up * sig * (1.0 + gate * (1.0 - sig))).astype(BF)
    dup = (dact * gate * sig).astype(BF)
    dtokens = (dot_nt(dgate, w_gate) + dot_nt(dup, w_up)).astype(BF)
    (dnormed_two,) = scatter(
        [dtokens.reshape(-1, tok, D)], [(("z", "c"), False)], [F32], sizes, 5
    )
    branch = dot_nt(act, w_down).astype(BF)
    branch_sum = lax.psum_scatter(branch, ("z", "c"), scatter_dimension=0, tiled=True)
    output = (mixed + branch_sum.astype(F32)).astype(BF)

    def collect(grad):
        mats = grad.shape[0]
        parts = grad.reshape(
            (mats, sizes["g"], nz, sizes["y"], sizes["c"], ff_rows, lanes)
        ).transpose(4, 1, 3, 2, 0, 5, 6)
        other = lax.dynamic_index_in_dim(parts, 1 - core, 0, keepdims=False)
        keep = lax.dynamic_index_in_dim(parts, core, 0, keepdims=False)
        swapped = shift(other, "c", 1, sizes)
        both = jnp.where(core == 0, jnp.stack([keep, swapped]), jnp.stack([swapped, keep]))
        both = both.reshape((-1,) + both.shape[3:])
        mine = lax.psum_scatter(
            both, live(("head", "g", "y"), sizes), scatter_dimension=0, tiled=True
        )[0]
        got = [lax.dynamic_index_in_dim(mine, z, 0, keepdims=False)]
        for d in range(1, nz):
            piece = lax.dynamic_index_in_dim(mine, (z + d) % nz, 0, keepdims=False)
            got.append(shift(piece, "z", d, sizes))
        held = jnp.stack(got)
        by_z = jnp.stack(
            [lax.dynamic_index_in_dim(held, (z - i) % nz, 0, keepdims=False) for i in range(nz)]
        )
        return by_z.transpose(1, 2, 0, 3).reshape(mats, ff_rows, wide)[:, :, :width].astype(F32)

    d_gate_up = collect(
        jnp.stack([dot_tn(tokens, dgate).astype(BF), dot_tn(tokens, dup).astype(BF)])
    )
    d_down = collect(dot_tn(cot_all, act).astype(BF)[None])

    z_two = mixed * scale_two
    u_two = gain_two * dnormed_two
    norm2_part = jnp.sum(dnormed_two * z_two, axis=0)
    dmixed = cotangent.astype(F32) + scale_two * (
        u_two - z_two * jnp.mean(z_two * u_two, axis=-1, keepdims=True)
    )
    dproj = dmixed.astype(BF)
    dattn = dot_nt(dproj, w_out).astype(BF)
    (dout,) = gather(
        [dattn.reshape(tok, 2, q_cols).transpose(1, 0, 2)], [(("head",), True)], sizes, 6
    )
    dout = dout.reshape(pair, q_cols)
    delta = jnp.sum(
        (dout.astype(F32) * attended).reshape(2, tok, q_cols // HEAD_DIM, HEAD_DIM), axis=-1
    ).transpose(0, 2, 1)
    delta = jnp.pad(delta, ((0, 0), (0, 8 - delta.shape[1]), (0, 0)))

    dproj_other = shift(dproj, "head", 1, sizes)
    own_attn = lax.dynamic_slice_in_dim(attn_local, head * tok, tok)
    other_attn = lax.dynamic_slice_in_dim(attn_local, (1 - head) * tok, tok)
    o_part = (dot_tn(own_attn, dproj) + dot_tn(other_attn, dproj_other)).astype(BF)
    d_out_weight = lax.psum_scatter(
        o_part, live(BLK, sizes), scatter_dimension=0, tiled=True
    ).astype(F32)

    dq, dkv_parts = attend_back(slots, tops, queries, kv, dout, lse, delta)
    (dkv,) = scatter(
        [dkv_parts.reshape(SEQ_SPAN, pair, 2 * HEAD_DIM)],
        [(place_axes, False)],
        [BF],
        sizes,
        7,
    )
    dq_pre = rotate(dq.astype(F32), cosine, -sine).astype(BF)
    dk_pre = rotate(dkv[:, :HEAD_DIM].astype(F32), cosine, -sine).astype(BF)
    dv = dkv[:, HEAD_DIM:]
    dpre = jnp.concatenate([dq_pre, dk_pre, dv], axis=1)
    w_part = dot_tn(normed, dpre).astype(BF)
    bias_part = jnp.sum(dpre.astype(F32), axis=0)
    dnormed = dot_nt(dpre, w_qkv)
    norm1_part = jnp.sum(dnormed * (x_pair * scale_one), axis=0)
    own = (jnp.arange(2) == head).astype(F32)[:, None]

    def owners(vector):
        return vector.reshape(2, blk, -1).transpose(1, 0, 2)

    def owned(vector):
        return owners((own * vector[None, :]).reshape(-1))

    small_grads = jnp.stack(
        [
            jnp.pad(part, ((0, 0), (0, 0), (0, LANES - part.shape[2])))
            for part in (
                owners(norm1_part),
                owners(norm2_part),
                owned(bias_part[:q_cols]),
                owned(bias_part[q_cols : q_cols + kv_cols]),
                owned(bias_part[q_cols + kv_cols :]),
            )
        ]
        + [jnp.zeros((blk, 2, LANES), F32)] * 3,
        axis=2,
    )
    small_grads = small_grads.transpose(1, 0, 2, 3).reshape(2 * blk, 8, LANES)
    w_grads, small_sum, dnormed_sum = scatter(
        [
            w_part.reshape(2, blk, rows, -1).transpose(1, 0, 2, 3),
            small_grads,
            dnormed.astype(BF).reshape(2, tok, D),
        ],
        [(BLK, True), (AXES, False), (("head",), False)],
        [F32, F32, F32],
        sizes,
        8,
    )
    own_scale = lax.dynamic_slice_in_dim(scale_one, head * tok, tok)
    z_one = inputs * own_scale
    u_one = gain_one * dnormed_sum
    hidden_grad = (
        dmixed + own_scale * (u_one - z_one * jnp.mean(z_one * u_one, axis=-1, keepdims=True))
    ).astype(BF)
    kn = k_bias.shape[0]
    return (
        output,
        hidden_grad,
        small_sum[0, :rows],
        jnp.concatenate([w_grads[0, :, :q_cols], w_grads[1, :, :q_cols]], axis=1),
        small_sum[2, :rows],
        jnp.concatenate([w_grads[i, :, q_cols : q_cols + kv_cols] for i in range(2)], axis=1),
        small_sum[3, :kn],
        jnp.concatenate([w_grads[i, :, q_cols + kv_cols :] for i in range(2)], axis=1),
        small_sum[4, :kn],
        d_out_weight,
        small_sum[1, :rows],
        d_gate_up[0],
        d_gate_up[1],
        d_down[0],
    )


def solution(mesh):
    heads, blk = mesh.devices.shape
    split = jax.sharding.Mesh(mesh.devices.reshape(heads, blk // 16, 4, 2, 2), AXES)
    sizes = dict(split.shape)
    rows = P(AXES, None)
    vector = P(AXES)
    feed = P(BLK, "head")
    return jax.shard_map(
        functools.partial(shards, sizes),
        mesh=split,
        in_specs=(
            rows,
            rows,
            P(),
            vector,
            rows,
            vector,
            rows,
            vector,
            rows,
            vector,
            rows,
            vector,
            feed,
            feed,
            feed,
        ),
        out_specs=(
            rows,
            rows,
            vector,
            rows,
            vector,
            rows,
            vector,
            rows,
            vector,
            rows,
            vector,
            feed,
            feed,
            feed,
        ),
        check_vma=False,
    )
```

time: 3990 us -> 1090 us (0.27)
  waiting for transfers between devices: 2840 us -> 224 us
  Pallas kernels: 0 us -> 492 us
  matrix products: 542 us -> 149 us
  blocking collectives: 194 us -> 0 us
  other arithmetic: 183 us -> 86.9 us
  local copies, waits for them, and re-layouts: 121 us -> 80.3 us
    reduce_scatter x6 -> x2, waiting for transfers between devices: 1770 us -> 0.01 us  [the longest x1 0.01 us: shards(): lax.psum_scatter(o_part, live(BLK, sizes), scatter_dimension=0, tiled=True)]
    all_gather x8 -> x4, waiting for transfers between devices: 945 us -> 41.8 us  [the longest x1 27.4 us: shards(): lax.all_gather(o_weight.astype(BF), live(AXES, sizes), axis=0, tiled=True)]
    pallas_call x0 -> x10, Pallas kernels: none -> 492 us  [the longest x5 224 us: gather(): pl.pallas_call(functools.partial(gather_kernel, plans, sizes), out_shape=...]
    dot_general x133 -> x17, matrix products: 542 us -> 149 us  [the longest x6 53.3 us: dot_nn(): lax.dot_general(a, b, (((1,), (0,)), ((), ())), preferred_element_type=F32)]
    concatenate x2 -> x4, other arithmetic: 108 us -> 2.71 us  [the longest x1 0.73 us: shards(): jnp.concatenate([w_grads[0, :, :q_cols], w_grads[1, :, :q_cols]], axis=1)]
    all_gather x2 -> x0, blocking collectives: 87.7 us -> none  [the longest x1 45.1 us: shards(): lax.all_gather(v_weight.astype(jnp.bfloat16), ('head', 'blk'), axis=0, ti...]
    unnamed x14 -> x8, waiting for transfers between devices: 0.23 us -> 83.9 us
    unnamed x2 -> x0, blocking collectives: 80.5 us -> none
  transfers between devices with their start and end apart: 79 -> 24, of which waited for: 43 -> 13; matrix products, arithmetic and copies ran while one was open for 15% -> 20% of each run, Pallas kernels for 0% -> 35%
where the time goes in v1:
time: 1090 us; the launch traced here: 1070 us
  Pallas kernels  492 us (45%)
  waiting for transfers between devices  224 us (21%)
  matrix products  149 us (14%)
  other arithmetic  86.9 us (8%)
  local copies, waits for them, and re-layouts  80.3 us (7%)
  starting transfers between devices  22.3 us (2%)
  between operations  16.4 us (2%)
    pallas_call x5, Pallas kernels, gather(): pl.pallas_call(functools.partial(gather_kernel, plans, sizes), out_shape=...  224 us
    pallas_call x3, Pallas kernels, scatter(): pl.pallas_call(functools.partial(scatter_kernel, plans, sizes), out_shape...  197 us
    ppermute x17, waiting for transfers between devices, shift(): lax.ppermute(value, axis, [(i, (i + distance) % n) for i in range(n)])  98.4 us
    unnamed x8, waiting for transfers between devices  83.9 us
    dot_general x6, matrix products, dot_nn(): lax.dot_general(a, b, (((1,), (0,)), ((), ())), preferred_element_type=F32)  53.3 us
    dot_general x5, matrix products, dot_nt(): lax.dot_general(a, b, (((1,), (1,)), ((), ())), preferred_element_type=F32)  51.5 us
    dot_general x6, matrix products, dot_tn(): lax.dot_general(a, b, (((0,), (0,)), ((), ())), preferred_element_type=F32)  43.8 us
    pallas_call x1, Pallas kernels, attend_back(): pl.pallas_call(functools.partial(backward_kernel, heads), grid_spec=pltpu...  43.2 us
  transfers between devices with their start and end apart: 24, of which 13 were waited for; matrix products, arithmetic and copies ran while one was open for 20% of the time, Pallas kernels for 35%

profile of v1, /device:TPU:0, one launch (start us, length us, event | category | flops | bytes accessed | tf_op | source)
XLA Modules:
  0.0 1071.0 jit_solution(2526043368559458235)
XLA Ops:
  14.6 39.8 %shard_map.254 = (bf16[32,48,1024]{2,1,0:T(8,128)(2,1)}, bf16[2,256,1536]{2,1,0:T(8,128)(2,1)}, f32[32,8,128]{2,1,0:T(8,128)}) custom-call(bf16[2,48,1024]{2,1,0:T(8,128)(2,1)} %maximum_maximum_fusion.refs_0_, bf16[256,1536]{1,0:T(8,128)(2,1)} %refs_1_.1, f32[8,128]{1,0:T(8,128)} %stack.236.refs_2_), custom_call_target="tpu_custom_call" | custom-call | bytes 62914560 | tf_op jit(solution)/shard_map/pallas_call | solution.py:139
  100.3 17.3 %collective-permute-done.1 = bf16[2,96,1152]{2,1,0:T(8,128)(2,1)S(1)} collective-permute-done((bf16[2,96,1152]{2,1,0:T(8,128)(2,1)S(1)}, bf16[2,96,1152]{2,1,0:T(8,128)(2,1)S(1)}, u32[]{:S(2)}, u32[]{:S(2)}) %collective-permute-start.1) | collective-permute-done | bytes 442400 | tf_op jit(solution)/shard_map/ppermute | solution.py:462
  139.7 53.1 %shard_map.255 = bf16[16,512,256]{2,1,0:T(8,128)(2,1)} custom-call(bf16[512,256]{1,0:T(8,128)(2,1)} %pad_maximum_fusion.8.refs_0_), custom_call_target="tpu_custom_call" | custom-call | bytes 62914560 | tf_op jit(solution)/shard_map/pallas_call | solution.py:139
  206.3 28.0 %shard_map.256 = (f32[512,768]{1,0:T(8,128)}, f32[2,8,256]{2,1,0:T(8,128)}) custom-call(s32[32]{0:T(128)} %get-tuple-element.29.slots, s32[2]{0:T(128)} %get-tuple-element.52.tops, bf16[512,768]{1,0:T(8,128)(2,1)} %copy.109.q_ref, bf16[32,256,256]{2,1,0:T(8,128)(2,1)} %bitcast.322), custom_call_target="tpu_custom_call" | custom-call | flops 6643777536 | bytes 83886080 | tf_op jit(solution)/shard_map/pallas_call | solution.py:350
  236.8 14.8 %shard_map.257 = bf16[2,256,768]{2,1,0:T(8,128)(2,1)} custom-call(bf16[2,256,768]{2,1,0:T(8,128)(2,1)} %bitcast.309), custom_call_target="tpu_custom_call" | custom-call | bytes 62914560 | tf_op jit(solution)/shard_map/pallas_call | solution.py:139
  266.4 27.4 %all-gather.7.cloned.1.call-done = bf16[1536,1536]{1,0:T(8,128)(2,1)} async-done(((bf16[48,1536]{1,0:T(8,128)(2,1)}), bf16[1536,1536]{1,0:T(8,128)(2,1)}) %all-gather.7.cloned.1.call-update) | async-done | bytes 4718608 | tf_op jit(solution)/shard_map/all_gather | solution.py:577
  300.4 102.5 %shard_map.258 = bf16[8,256,1536]{2,1,0:T(8,128)(2,1)} custom-call(bf16[256,1536]{1,0:T(8,128)(2,1)} %multiply_convert_fusion.4.refs_0_), custom_call_target="tpu_custom_call" | custom-call | bytes 62914560 | tf_op jit(solution)/shard_map/pallas_call | solution.py:139
  402.9 14.4 %all-gather.9.cloned.1.call-done = bf16[2048,1536]{1,0:T(8,128)(2,1)} async-done(((bf16[256,1536]{1,0:T(8,128)(2,1)}), bf16[2048,1536]{1,0:T(8,128)(2,1)}) %all-gather.9.cloned.1.call-update) | async-done | bytes 6291472 | tf_op jit(solution)/shard_map/all_gather | solution.py:578
  417.3 13.8 %fusion.61 = f32[1152,2048]{0,1:T(8,128)} fusion(bf16[2048,1536]{1,0:T(8,128)(2,1)} %all-gather.9.cloned.1.call-done, bf16[1536,1152]{1,0:T(8,128)(2,1)} %bitcast.327), kind=kOutput, calls=%fused_computation.225 | convolution fusion | flops 7247757312 | bytes 19267584 | tf_op jit(solution)/shard_map/dot_general | solution.py:33
  445.9 10.6 fusion.59
  456.5 21.6 %fusion.4 = (bf16[2048,1152]{1,0:T(8,128)(2,1)}, bf16[2048,1152]{1,0:T(8,128)(2,1)}, bf16[2048,1152]{1,0:T(8,128)(2,1)}) fusion(f32[1152,2048]{0,1:T(8,128)} %fusion.61, f32[2048,1152]{1,0:T(8,128)} %fusion.59, bf16[2048,1536]{1,0:T(8,128)(2,1)} %bitcast.313, bf16[1536,1152]{1,0:T(8,128)(2,1)} %bitcast.331), kind=kOutput, calls=%fused_computation.7 | convolution fusion | flops 7285506048 | bytes 42860544 | tf_op jit(solution)/shard_map/dot_general | solution.py:33
  478.1 14.4 %fusion.60 = f32[2048,1536]{1,0:T(8,128)} fusion(bf16[2048,1152]{1,0:T(8,128)(2,1)} %get-tuple-element.54, bf16[1536,1152]{1,0:T(8,128)(2,1)} %bitcast.332), kind=kOutput, calls=%fused_computation.224 | convolution fusion | flops 7247757312 | bytes 20840448 | tf_op jit(solution)/shard_map/dot_general | solution.py:37
  492.5 12.7 %add_convert_fusion = bf16[2048,1536]{1,0:T(8,128)(2,1)} fusion(f32[2048,1536]{1,0:T(8,128)} %fusion.60, bf16[2048,1152]{1,0:T(8,128)(2,1)S(1)} %copy-done.44, bf16[1536,1152]{1,0:T(8,128)(2,1)S(1)} %bitcast.330), kind=kOutput, calls=%fused_computation | convolution fusion | flops 7254048768 | bytes 27131904 | tf_op jit(solution)/shard_map/dot_general | solution.py:37
  505.3 72.7 %shard_map.259 = f32[256,1536]{1,0:T(8,128)} custom-call(bf16[8,256,1536]{2,1,0:T(8,128)(2,1)} %bitcast.321), custom_call_target="tpu_custom_call" | custom-call | bytes 62914560 | tf_op jit(solution)/shard_map/pallas_call | solution.py:282
  585.0 16.3 %collective-permute-done.8 = bf16[256,1536]{1,0:T(8,128)(2,1)} collective-permute-done((bf16[256,1536]{1,0:T(8,128)(2,1)}, bf16[256,1536]{1,0:T(8,128)(2,1)}, u32[]{:S(2)}, u32[]{:S(2)}) %collective-permute-start.8) | collective-permute-done | bytes 786464 | tf_op jit(solution)/shard_map/ppermute | solution.py:462
  604.7 13.4 %convolution_convert_fusion.3 = bf16[2048,1536]{1,0:T(8,128)(2,1)} fusion(bf16[2048,1152]{1,0:T(8,128)(2,1)} %get-tuple-element.55, bf16[1536,1152]{1,0:T(8,128)(2,1)} %bitcast.328), kind=kOutput, calls=%fused_computation.17 | convolution fusion | flops 7250903040 | bytes 14548992 | tf_op jit(solution)/shard_map/dot_general | solution.py:37
  618.1 12.5 %convolution_convert_fusion.1 = bf16[1536,1152]{1,0:T(8,128)(2,1)S(1)} fusion(bf16[2048,1536]{1,0:T(8,128)(2,1)} %bitcast.314, bf16[2048,1152]{1,0:T(8,128)(2,1)} %get-tuple-element.53), kind=kOutput, calls=%fused_computation.15 | convolution fusion | flops 7249526784 | bytes 14548992 | tf_op jit(solution)/shard_map/dot_general | solution.py:41
  630.7 12.3 %convolution_convert_fusion.2 = bf16[1536,1152]{1,0:T(8,128)(2,1)S(1)} fusion(bf16[2048,1536]{1,0:T(8,128)(2,1)} %bitcast.315, bf16[2048,1152]{1,0:T(8,128)(2,1)} %get-tuple-element.54), kind=kOutput, calls=%fused_computation.16 | convolution fusion | flops 7249526784 | bytes 14548992 | tf_op jit(solution)/shard_map/dot_general | solution.py:41
  691.3 13.6 %shard_map.260 = bf16[2,256,768]{2,1,0:T(8,128)(2,1)} custom-call(bf16[2,256,768]{2,1,0:T(8,128)(2,1)} %bitcast.343), custom_call_target="tpu_custom_call" | custom-call | bytes 62914560 | tf_op jit(solution)/shard_map/pallas_call | solution.py:139
  716.4 43.2 %shard_map.261 = (bf16[512,768]{1,0:T(8,128)(2,1)}, bf16[32,256,256]{2,1,0:T(8,128)(2,1)}) custom-call(s32[32]{0:T(128)} %get-tuple-element.29.slots, s32[2]{0:T(128)} %get-tuple-element.52.tops, bf16[512,768]{1,0:T(8,128)(2,1)} %copy.109.q_ref, bf16[32,256,256]{2,1,0:T(8,128)(2,1)} %bitcast.323, bf16[512,768]{1,0:T(8,128)(2,1)} %bitcast.344, ...), custom_call_target="tpu_custom_call" | custom-call | flops 16609443840 | bytes 125829120 | tf_op jit(solution)/shard_map/pallas_call | solution.py:422
  762.2 71.5 %shard_map.262 = bf16[512,256]{1,0:T(8,128)(2,1)} custom-call(bf16[16,512,256]{2,1,0:T(8,128)(2,1)} %bitcast.324), custom_call_target="tpu_custom_call" | custom-call | bytes 62914560 | tf_op jit(solution)/shard_map/pallas_call | solution.py:282
  857.3 53.2 %shard_map.263 = (f32[2,48,1024]{2,1,0:T(8,128)}, f32[8,128]{1,0:T(8,128)}, f32[256,1536]{1,0:T(8,128)}) custom-call(bf16[16,2,48,1024]{3,2,1,0:T(8,128)(2,1)} %bitcast.308, f32[32,8,128]{2,1,0:T(8,128)} %bitcast.350, bf16[2,256,1536]{2,1,0:T(8,128)(2,1)} %bitcast.347), custom_call_target="tpu_custom_call" | custom-call | bytes 62914560 | tf_op jit(solution)/shard_map/pallas_call | solution.py:282
  922.5 83.3 %all-reduce.19.cloned.1.call-done = (bf16[4,4,2,96,1152]{4,3,2,1,0:T(8,128)(2,1)}, bf16[4,4,1,96,1152]{4,3,1,0,2:T(8,128)(2,1)}) async-done(((bf16[4,4,2,96,1152]{4,3,2,1,0:T(8,128)(2,1)}, bf16[4,4,1,96,1152]{4,3,1,0,2:T(8,128)(2,1)}), (bf16[4,4,2,96,1152]{4,3,2,1,0:T(8,128)(2,1)}, bf16[4,4,1,96,1152]{4,3,1,0,2:T(8,128)(2,1)})) %all-reduce.19.cloned.1.call-update) | async-done | bytes 10616848
  1038.1 22.5 %collective-permute-done.11 = bf16[2,96,1152]{2,1,0:T(8,128)(2,1)S(1)} collective-permute-done((bf16[2,96,1152]{2,1,0:T(8,128)(2,1)S(1)}, bf16[2,96,1152]{2,1,0:T(8,128)(2,1)S(1)}, u32[]{:S(2)}, u32[]{:S(2)}) %collective-permute-start.11) | collective-permute-done | bytes 442400 | tf_op jit(solution)/shard_map/ppermute | solution.py:462
  (327 shorter events, 269.7 us)
Async XLA Ops:
  7.2 128.0 %all-gather.13.cloned.1.call-start = ((), (), s32[]{:S(2)}) async-start(), calls=%async_computation.7 | async-start | bytes 4423680 | tf_op jit(solution)/shard_map/all_gather | solution.py:561
  56.8 10.2 collective-permute-start.4
  57.4 18.6 %collective-permute-start.5 = (bf16[1,96,1152]{2,1,0:T(8,128)(2,1)S(1)}, bf16[1,96,1152]{2,1,0:T(8,128)(2,1)S(1)}, u32[]{:S(2)}, u32[]{:S(2)}) collective-permute-start(bf16[1,96,1152]{2,1,0:T(8,128)(2,1)S(1)} %bitcast.367), channel_id=1, source_target_pairs={{0,8},{4,12},{8,0},{12,4},{1,9},{5,13},{9,1},{13,5},{2,10},{6,14},... | collective-permute-start | bytes 663560 | tf_op jit(solution)/shard_map/ppermute | solution.py:462
  58.9 17.1 %collective-permute-start.6 = (bf16[1,96,1152]{2,1,0:T(8,128)(2,1)S(1)}, bf16[1,96,1152]{2,1,0:T(8,128)(2,1)S(1)}, u32[]{:S(2)}, u32[]{:S(2)}) collective-permute-start(bf16[1,96,1152]{2,1,0:T(8,128)(2,1)S(1)} %bitcast.368), channel_id=1, source_target_pairs={{0,12},{4,0},{8,4},{12,8},{1,13},{5,1},{9,5},{13,9},{2,14},{6,2},{... | collective-permute-start | bytes 663560 | tf_op jit(solution)/shard_map/ppermute | solution.py:462
  77.1 182.3 %all-gather.11.cloned.1.call-start = ((), (), s32[]{:S(2)}) async-start(), calls=%async_computation.6 | async-start | bytes 8847360 | tf_op jit(solution)/shard_map/all_gather | solution.py:561
  84.1 15.5 %collective-permute-start = (bf16[2,96,1152]{2,1,0:T(8,128)(2,1)S(1)}, bf16[2,96,1152]{2,1,0:T(8,128)(2,1)S(1)}, u32[]{:S(2)}, u32[]{:S(2)}) collective-permute-start(bf16[2,96,1152]{2,1,0:T(8,128)(2,1)S(1)} %bitcast.354), channel_id=1, source_target_pairs={{0,4},{4,8},{8,12},{12,0},{1,5},{5,9},{9,13},{13,1},{2,6},{6,10},{... | collective-permute-start | bytes 1327112 | tf_op jit(solution)/shard_map/ppermute | solution.py:462
  88.9 28.6 %collective-permute-start.1 = (bf16[2,96,1152]{2,1,0:T(8,128)(2,1)S(1)}, bf16[2,96,1152]{2,1,0:T(8,128)(2,1)S(1)}, u32[]{:S(2)}, u32[]{:S(2)}) collective-permute-start(bf16[2,96,1152]{2,1,0:T(8,128)(2,1)S(1)} %bitcast.356), channel_id=1, source_target_pairs={{0,8},{4,12},{8,0},{12,4},{1,9},{5,13},{9,1},{13,5},{2,10},{6,14},... | collective-permute-start | bytes 1327112 | tf_op jit(solution)/shard_map/ppermute | solution.py:462
  89.2 29.1 %collective-permute-start.2 = (bf16[2,96,1152]{2,1,0:T(8,128)(2,1)S(1)}, bf16[2,96,1152]{2,1,0:T(8,128)(2,1)S(1)}, u32[]{:S(2)}, u32[]{:S(2)}) collective-permute-start(bf16[2,96,1152]{2,1,0:T(8,128)(2,1)S(1)} %bitcast.358), channel_id=1, source_target_pairs={{0,12},{4,0},{8,4},{12,8},{1,13},{5,1},{9,5},{13,9},{2,14},{6,2},{... | collective-permute-start | bytes 1327112 | tf_op jit(solution)/shard_map/ppermute | solution.py:462
  124.6 169.2 %all-gather.7.cloned.1.call-start = ((), (), s32[]{:S(2)}) async-start(), calls=%async_computation.2 | async-start | bytes 4866048 | tf_op jit(solution)/shard_map/all_gather | solution.py:577
  125.3 291.9 %all-gather.9.cloned.1.call-start = ((), (), s32[]{:S(2)}) async-start(), calls=%async_computation.4 | async-start | bytes 7077888 | tf_op jit(solution)/shard_map/all_gather | solution.py:578
  125.9 790.3 %reduce-scatter.8.cloned.1.call-start = ((), (), s32[]{:S(2)}) async-start(), calls=%async_computation.5 | async-start | bytes 2506752 | tf_op jit(solution)/shard_map/reduce_scatter | solution.py:666
  138.8 114.8 %collective-permute-start.7 = (bf16[1,2,4,1,96,1152]{5,4,2,1,3,0:T(8,128)(2,1)}, bf16[1,2,4,1,96,1152]{5,4,2,1,3,0:T(8,128)(2,1)}, u32[]{:S(2)}, u32[]{:S(2)}) collective-permute-start(bf16[1,2,4,1,96,1152]{5,4,2,1,3,0:T(8,128)(2,1)} %get-tuple-element.80), channel_id=1, source_target_pairs={{0,1},{1,0},{2,3},{3,2},{4,5},{5,4},{6,7},{7,6},{8,9},{9,8},{10,11... | collective-permute-start | bytes 5308424 | tf_op jit(solution)/shard_map/ppermute | solution.py:462
  266.4 164.7 %collective-permute-start.3 = (bf16[1,2,4,2,96,1152]{5,4,3,2,1,0:T(8,128)(2,1)}, bf16[1,2,4,2,96,1152]{5,4,3,2,1,0:T(8,128)(2,1)}, u32[]{:S(2)}, u32[]{:S(2)}) collective-permute-start(bf16[1,2,4,2,96,1152]{5,4,3,2,1,0:T(8,128)(2,1)} %get-tuple-element.69), channel_id=1, source_target_pairs={{0,1},{1,0},{2,3},{3,2},{4,5},{5,4},{6,7},{7,6},{8,9},{9,8},{10,11... | collective-permute-start | bytes 10616840 | tf_op jit(solution)/shard_map/ppermute | solution.py:462
  581.4 19.8 %collective-permute-start.8 = (bf16[256,1536]{1,0:T(8,128)(2,1)}, bf16[256,1536]{1,0:T(8,128)(2,1)}, u32[]{:S(2)}, u32[]{:S(2)}) collective-permute-start(bf16[256,1536]{1,0:T(8,128)(2,1)} %fusion.52), channel_id=1, source_target_pairs={{0,16},{16,0},{1,17},{17,1},{2,18},{18,2},{3,19},{19,3},{4,20},{20... | collective-permute-start | bytes 2359304 | tf_op jit(solution)/shard_map/ppermute | solution.py:462
  604.6 313.3 %reduce-scatter.6.cloned.1.call-start = ((), (), s32[]{:S(2)}) async-start(), calls=%async_computation.3 | async-start | bytes 7077888 | tf_op jit(solution)/shard_map/reduce_scatter | solution.py:614
  618.1 387.7 %all-reduce.19.cloned.1.call-start = ((), (), s32[]{:S(2)}) async-start(), calls=%async_computation.8 | async-start | bytes 21233664
  647.3 23.8 %collective-permute-start.9 = (bf16[1,2,4,2,96,1152]{5,4,3,2,1,0:T(8,128)(2,1)}, bf16[1,2,4,2,96,1152]{5,4,3,2,1,0:T(8,128)(2,1)}, u32[]{:S(2)}, u32[]{:S(2)}) collective-permute-start(bf16[1,2,4,2,96,1152]{5,4,3,2,1,0:T(8,128)(2,1)} %bitcast.288), channel_id=1, source_target_pairs={{0,1},{1,0},{2,3},{3,2},{4,5},{5,4},{6,7},{7,6},{8,9},{9,8},{10,11... | collective-permute-start | bytes 10616840 | tf_op jit(solution)/shard_map/ppermute | solution.py:462
  665.2 3.9 collective-permute-start.13
  1008.8 10.3 collective-permute-start.14
  1010.4 18.3 %collective-permute-start.15 = (bf16[1,96,1152]{2,1,0:T(8,128)(2,1)S(1)}, bf16[1,96,1152]{2,1,0:T(8,128)(2,1)S(1)}, u32[]{:S(2)}, u32[]{:S(2)}) collective-permute-start(bf16[1,96,1152]{2,1,0:T(8,128)(2,1)S(1)} %get-tuple-element.72), channel_id=1, source_target_pairs={{0,8},{4,12},{8,0},{12,4},{1,9},{5,13},{9,1},{13,5},{2,10},{6,14},... | collective-permute-start | bytes 663560 | tf_op jit(solution)/shard_map/ppermute | solution.py:462
  1012.8 15.9 %collective-permute-start.16 = (bf16[1,96,1152]{2,1,0:T(8,128)(2,1)S(1)}, bf16[1,96,1152]{2,1,0:T(8,128)(2,1)S(1)}, u32[]{:S(2)}, u32[]{:S(2)}) collective-permute-start(bf16[1,96,1152]{2,1,0:T(8,128)(2,1)S(1)} %get-tuple-element.71), channel_id=1, source_target_pairs={{0,12},{4,0},{8,4},{12,8},{1,13},{5,1},{9,5},{13,9},{2,14},{6,2},{... | collective-permute-start | bytes 663560 | tf_op jit(solution)/shard_map/ppermute | solution.py:462
  1015.8 22.4 %collective-permute-start.10 = (bf16[2,96,1152]{2,1,0:T(8,128)(2,1)S(1)}, bf16[2,96,1152]{2,1,0:T(8,128)(2,1)S(1)}, u32[]{:S(2)}, u32[]{:S(2)}) collective-permute-start(bf16[2,96,1152]{2,1,0:T(8,128)(2,1)S(1)} %get-tuple-element.58), channel_id=1, source_target_pairs={{0,4},{4,8},{8,12},{12,0},{1,5},{5,9},{9,13},{13,1},{2,6},{6,10},{... | collective-permute-start | bytes 1327112 | tf_op jit(solution)/shard_map/ppermute | solution.py:462
  1016.4 44.3 %collective-permute-start.11 = (bf16[2,96,1152]{2,1,0:T(8,128)(2,1)S(1)}, bf16[2,96,1152]{2,1,0:T(8,128)(2,1)S(1)}, u32[]{:S(2)}, u32[]{:S(2)}) collective-permute-start(bf16[2,96,1152]{2,1,0:T(8,128)(2,1)S(1)} %get-tuple-element.57), channel_id=1, source_target_pairs={{0,8},{4,12},{8,0},{12,4},{1,9},{5,13},{9,1},{13,5},{2,10},{6,14},... | collective-permute-start | bytes 1327112 | tf_op jit(solution)/shard_map/ppermute | solution.py:462
  1019.1 41.6 %collective-permute-start.12 = (bf16[2,96,1152]{2,1,0:T(8,128)(2,1)S(1)}, bf16[2,96,1152]{2,1,0:T(8,128)(2,1)S(1)}, u32[]{:S(2)}, u32[]{:S(2)}) collective-permute-start(bf16[2,96,1152]{2,1,0:T(8,128)(2,1)S(1)} %get-tuple-element.59), channel_id=1, source_target_pairs={{0,12},{4,0},{8,4},{12,8},{1,13},{5,1},{9,5},{13,9},{2,14},{6,2},{... | collective-permute-start | bytes 1327112 | tf_op jit(solution)/shard_map/ppermute | solution.py:462
  (51 other events, 1198.4 us)
Sparse Core Ops, SparseCore 0:
  77.2 47.7 all-gather.12
  126.8 97.1 all-gather.10
  227.5 66.2 all-gather.6
  295.3 121.9 all-gather.8
  604.8 78.9 reduce-scatter.7
  686.0 68.8 reduce-scatter.5
  759.2 246.5 all-reduce.18

commit v2 on v1

--- a/solution.py
+++ b/solution.py
@@ -83,59 +83,76 @@
 
 
 def gather_kernel(plans, sizes, *refs):
-    count = len(plans)
+    count = max(p[0] for p in plans) + 1
     xs, outs = refs[:count], refs[count : 2 * count]
     send_sems, recv_sems, local_sems = refs[2 * count :]
-    greet(live(AXES, {a: (sizes[a] if any(a in p[0] for p in plans) else 1) for a in AXES}), sizes)
-    sends, locals_, queue = [], [], []
+    used = {a: (sizes[a] if any(a in p[3] for p in plans) else 1) for a in AXES}
+    greet(live(AXES, used), sizes)
+
+    def cut(ref, rows):
+        return ref if rows is None else ref.at[pl.ds(*rows)]
+
+    def source(plan, place):
+        i, rows, layout, phases, split = plan
+        return cut(xs[i].at[place] if split else xs[i], rows)
+
+    sends, kept, queue = [], [], []
     sem = 0
-    for i, (axes, split) in enumerate(plans):
-        mine = xs[i].at[lax.axis_index(axes[0])] if split else xs[i]
-        copy = pltpu.make_async_copy(mine, outs[i].at[place_of({}, axes, sizes)], local_sems.at[i])
-        copy.start()
-        locals_.append(copy)
-        queue.append((i, {}, -1, None))
+    for j, plan in enumerate(plans):
+        i, rows, layout, phases, split = plan
+        mine = source(plan, lax.axis_index(phases[0]))
+        slot = cut(outs[i].at[place_of({}, layout, sizes)], rows)
+        copy = pltpu.make_async_copy(mine, slot, local_sems.at[j])
+        queue.append((plan, {}, -1, None))
+        kept.append(copy)
     at = 0
     while at < len(queue):
-        i, offsets, phase, arrived = queue[at]
+        plan, offsets, phase, arrived = queue[at]
         at += 1
-        axes, split = plans[i]
-        slot = outs[i].at[place_of(offsets, axes, sizes)]
+        i, rows, layout, phases, split = plan
+        slot = cut(outs[i].at[place_of(offsets, layout, sizes)], rows)
         if arrived is None:
-            src = xs[i].at[lax.axis_index(axes[0])] if split else xs[i]
+            src = source(plan, lax.axis_index(phases[0]))
         else:
             src = slot
             remote(
-                slot, slot, send_sems.at[arrived], recv_sems.at[arrived], axes[0], 0, sizes
+                slot, slot, send_sems.at[arrived], recv_sems.at[arrived], phases[0], 0, sizes
             ).wait_recv()
-        for p in range(phase + 1, len(axes)):
-            a = axes[p]
+        for p in range(phase + 1, len(phases)):
+            a = phases[p]
             for d in range(1, sizes[a]):
                 piece = src
                 if split and p == 0:
-                    piece = xs[i].at[lax.rem(lax.axis_index(a) + d, sizes[a])]
+                    piece = source(plan, lax.rem(lax.axis_index(a) + d, sizes[a]))
                 copy = remote(piece, slot, send_sems.at[sem], recv_sems.at[sem], a, d, sizes)
                 copy.start()
                 sends.append(copy)
                 later = dict(offsets)
                 later[a] = sizes[a] - d
-                queue.append((i, later, p, sem))
+                queue.append((plan, later, p, sem))
                 sem += 1
-    for copy in locals_:
+        if at == len(plans):
+            for copy in kept:
+                copy.start()
+    for copy in kept:
         copy.wait()
     for copy in sends:
         copy.wait_send()
 
 
 def gather(arrays, plans, sizes, collective_id):
-    plans = [(live(axes, sizes), split) for axes, split in plans]
-    counts = [int(np.prod([sizes[a] for a in axes])) for axes, _ in plans]
+    plans = [
+        (i, rows, live(layout, sizes), live(phases, sizes), split)
+        for i, rows, layout, phases, split in plans
+    ]
+    counts = [int(np.prod([sizes[a] for a in p[2]])) for p in plans]
     total = sum(counts) - len(counts)
-    shapes = [
-        jax.ShapeDtypeStruct((n,) + (x.shape[1:] if split else x.shape), x.dtype)
-        for n, x, (_, split) in zip(counts, arrays, plans)
-    ]
+    shapes = []
+    for i, x in enumerate(arrays):
+        n, split = next((c, p[4]) for c, p in zip(counts, plans) if p[0] == i)
+        shapes.append(jax.ShapeDtypeStruct((n,) + (x.shape[1:] if split else x.shape), x.dtype))
     spec = pl.BlockSpec(memory_space=pltpu.VMEM)
+    moved = sum(int(np.prod(s.shape)) * s.dtype.itemsize for s in shapes)
     return pl.pallas_call(
         functools.partial(gather_kernel, plans, sizes),
         out_shape=shapes,
@@ -144,12 +161,12 @@
         scratch_shapes=[
             pltpu.SemaphoreType.DMA((total,)),
             pltpu.SemaphoreType.DMA((total,)),
-            pltpu.SemaphoreType.DMA((len(arrays),)),
+            pltpu.SemaphoreType.DMA((len(plans),)),
         ],
         compiler_params=pltpu.CompilerParams(
             collective_id=collective_id, has_side_effects=True, vmem_limit_bytes=VMEM_LIMIT
         ),
-        cost_estimate=pl.CostEstimate(flops=0, bytes_accessed=60 * 2**20, transcendentals=0),
+        cost_estimate=pl.CostEstimate(flops=0, bytes_accessed=20 * moved, transcendentals=0),
     )(*arrays)
 
 
@@ -160,22 +177,18 @@
     return keys
 
 
-def scatter_kernel(plans, sizes, *refs):
-    count = len(plans)
+def scatter_kernel(plans, sizes, *refs, between=None):
+    count = max(p[0] for p in plans) + 1
     xs, outs = refs[:count], refs[count : 2 * count]
     at = 2 * count
     bufs = []
-    for axes, swap in plans:
-        phases = len(axes)
-        bufs.append((refs[at : at + phases], refs[at + phases : at + 2 * phases]))
-        at += 2 * phases
+    for _, _, _, phases, swap in plans:
+        n = len(phases)
+        bufs.append((refs[at : at + n], refs[at + n : at + 2 * n]))
+        at += 2 * n
     send_sems, recv_sems, local_sems = refs[at:]
     used = {
-        a: (
-            sizes[a]
-            if any(a in axes or (swap and a == "head") for axes, swap in plans)
-            else 1
-        )
+        a: (sizes[a] if any(a in p[3] or (p[4] and a == "head") for p in plans) else 1)
         for a in AXES
     }
     greet(live(AXES, used), sizes)
@@ -189,66 +202,70 @@
             value = value * sizes[a] + offsets.get(a, 0)
         return value
 
-    def total_of(i, offsets, phase):
-        axes = plans[i][0]
-        order = axes[::-1]
-        total = xs[i][place_of(offsets, axes, sizes)].astype(F32)
+    def block_of(j, offsets):
+        i, rows, layout, phases, swap = plans[j]
+        block = xs[i].at[place_of(offsets, layout, sizes)]
+        return block if rows is None else block.at[pl.ds(*rows)]
+
+    def total_of(j, offsets, phase):
+        phases = plans[j][3]
+        total = block_of(j, offsets)[...].astype(F32)
         for q in range(phase):
-            rest = axes[: len(axes) - 1 - q]
-            for d in range(1, sizes[order[q]]):
-                key = (q, d, number(offsets, rest))
-                s = arrivals[i].pop(key)
-                buf = bufs[i][1][q].at[d - 1, number(offsets, rest)]
-                remote(buf, buf, send_sems.at[s], recv_sems.at[s], order[q], 0, sizes).wait_recv()
+            rest = phases[q + 1 :]
+            for d in range(1, sizes[phases[q]]):
+                s = arrivals[j].pop((q, d, number(offsets, rest)))
+                buf = bufs[j][1][q].at[d - 1, number(offsets, rest)]
+                remote(buf, buf, send_sems.at[s], recv_sems.at[s], phases[q], 0, sizes).wait_recv()
                 total = total + buf[...].astype(F32)
         return total
 
-    depth = max(len(axes) for axes, _ in plans)
+    depth = max(len(p[3]) for p in plans)
     for phase in range(depth):
-        for i, (axes, swap) in enumerate(plans):
-            if phase >= len(axes):
+        for j, (i, rows, layout, phases, swap) in enumerate(plans):
+            if phase >= len(phases):
                 continue
-            order = axes[::-1]
-            a = order[phase]
-            rest = axes[: len(axes) - 1 - phase]
+            a, rest = phases[phase], phases[phase + 1 :]
             for d in range(1, sizes[a]):
                 for key in offset_keys(rest, sizes):
                     offsets = dict(key)
                     offsets[a] = d
                     where = number(key, rest)
                     if phase == 0:
-                        src = xs[i].at[place_of(offsets, axes, sizes)]
+                        src = block_of(j, offsets)
                     else:
-                        src = bufs[i][0][phase].at[d - 1, where]
-                        src[...] = total_of(i, offsets, phase).astype(src.dtype)
-                    dst = bufs[i][1][phase].at[d - 1, where]
+                        src = bufs[j][0][phase].at[d - 1, where]
+                        src[...] = total_of(j, offsets, phase).astype(src.dtype)
+                    dst = bufs[j][1][phase].at[d - 1, where]
                     copy = remote(src, dst, send_sems.at[sem], recv_sems.at[sem], a, d, sizes)
                     copy.start()
                     sends.append(copy)
-                    arrivals[i][(phase, d, where)] = sem
+                    arrivals[j][(phase, d, where)] = sem
                     sem += 1
+        if between is not None:
+            between(phase)
     swaps = []
-    for i, (axes, swap) in enumerate(plans):
-        total = total_of(i, {}, len(axes))
+    for j, (i, rows, layout, phases, swap) in enumerate(plans):
+        total = total_of(j, {}, len(phases))
         if swap:
-            hold, out = bufs[i][0][0], outs[i]
+            hold, out = bufs[j][0][0], outs[i]
             hold[...] = total.astype(hold.dtype)
             me = lax.axis_index("head")
-            copy = pltpu.make_async_copy(hold.at[me], out.at[me], local_sems.at[i])
+            copy = pltpu.make_async_copy(hold.at[me], out.at[me], local_sems.at[j])
             copy.start()
+            swaps.append((copy, None))
             for d in range(1, sizes["head"]):
                 to = lax.rem(me + d, sizes["head"])
-                copy2 = remote(
+                copy = remote(
                     hold.at[to], out.at[me], send_sems.at[sem], recv_sems.at[sem], "head", d, sizes
                 )
-                copy2.start()
-                sends.append(copy2)
-                source = out.at[lax.rem(me + sizes["head"] - d, sizes["head"])]
-                swaps.append((source, sem))
+                copy.start()
+                sends.append(copy)
+                swaps.append((out.at[lax.rem(me + sizes["head"] - d, sizes["head"])], sem))
                 sem += 1
-            swaps.append((copy, None))
+        elif rows is None:
+            outs[i][...] = total.astype(outs[i].dtype)
         else:
-            outs[i][...] = total.astype(outs[i].dtype)
+            outs[i][pl.ds(*rows)] = total.astype(outs[i].dtype)
     for item, s in swaps:
         if s is None:
             item.wait()
@@ -258,15 +275,14 @@
         copy.wait_send()
 
 
-def scatter(arrays, plans, out_types, sizes, collective_id):
-    plans = [(live(axes, sizes), swap) for axes, swap in plans]
+def scatter_scratch(arrays, plans, out_types, sizes):
     scratch, total = [], 0
-    for x, (axes, swap), kind in zip(arrays, plans, out_types):
-        block = x.shape[1:]
-        order = axes[::-1]
+    for i, rows, layout, phases, swap in plans:
+        x, kind = arrays[i], out_types[i]
+        block = x.shape[1:] if rows is None else (rows[1],) + x.shape[2:]
         send_bufs, recv_bufs = [], []
-        for p, a in enumerate(order):
-            rest = int(np.prod([sizes[b] for b in axes[: len(axes) - 1 - p]], dtype=int))
+        for p, a in enumerate(phases):
+            rest = int(np.prod([sizes[b] for b in phases[p + 1 :]], dtype=int))
             shape = (sizes[a] - 1, rest) + block
             recv_bufs.append(pltpu.VMEM(shape, x.dtype))
             if p == 0:
@@ -277,24 +293,207 @@
         scratch += send_bufs + recv_bufs
         if swap:
             total += sizes["head"] - 1
+    return scratch + [
+        pltpu.SemaphoreType.DMA((total,)),
+        pltpu.SemaphoreType.DMA((total,)),
+        pltpu.SemaphoreType.DMA((len(plans),)),
+    ]
+
+
+def alive(plans, sizes):
+    return [
+        (i, rows, live(layout, sizes), live(phases, sizes), flag)
+        for i, rows, layout, phases, flag in plans
+    ]
+
+
+def scatter(arrays, plans, out_types, sizes, collective_id):
+    plans = alive(plans, sizes)
     shapes = [jax.ShapeDtypeStruct(x.shape[1:], kind) for x, kind in zip(arrays, out_types)]
     spec = pl.BlockSpec(memory_space=pltpu.VMEM)
+    moved = sum(int(np.prod(x.shape)) * x.dtype.itemsize for x in arrays)
     return pl.pallas_call(
         functools.partial(scatter_kernel, plans, sizes),
         out_shape=shapes,
         in_specs=[spec] * len(arrays),
         out_specs=[spec] * len(arrays),
-        scratch_shapes=scratch
-        + [
-            pltpu.SemaphoreType.DMA((total,)),
-            pltpu.SemaphoreType.DMA((total,)),
-            pltpu.SemaphoreType.DMA((len(arrays),)),
-        ],
+        scratch_shapes=scatter_scratch(arrays, plans, out_types, sizes),
         compiler_params=pltpu.CompilerParams(
             collective_id=collective_id, has_side_effects=True, vmem_limit_bytes=VMEM_LIMIT
         ),
-        cost_estimate=pl.CostEstimate(flops=0, bytes_accessed=60 * 2**20, transcendentals=0),
+        cost_estimate=pl.CostEstimate(flops=0, bytes_accessed=20 * moved, transcendentals=0),
     )(*arrays)
+
+
+def feed_kernel(chunks, t_ref, c_ref, w_ref, *refs):
+    act_ref, dgate_ref, dup_ref, branch_ref, dtok_ref = refs[-5:]
+    before = refs[:-5]
+    tokens, cot = t_ref[...], c_ref[...]
+    places, _, rows, width = w_ref.shape
+    per = max(1, LANES * 3 // rows)
+
+    def products(j):
+        low, n = chunks[j]
+
+        def weight(m):
+            return w_ref[:, m, :, low : low + n].reshape(D, n)
+
+        return dot_nn(tokens, weight(1)), dot_nn(tokens, weight(2)), dot_nn(cot, weight(0))
+
+    ready = [products(0)]
+    for j, (low, n) in enumerate(chunks):
+        gate, up, dact = ready[j]
+        if j + 1 < len(chunks):
+            ready.append(products(j + 1))
+        sig = 1.0 / (1.0 + jnp.exp(-gate))
+        silu = gate * sig
+        act_ref[:, low : low + n] = (silu * up).astype(BF)
+        dgate_ref[:, low : low + n] = (dact * up * (sig + silu * (1.0 - sig))).astype(BF)
+        dup_ref[:, low : low + n] = (dact * silu).astype(BF)
+    for z in range(0, places, per):
+        cols = slice(z * rows, (z + per) * rows)
+
+        def weight(m):
+            return w_ref[z : z + per, m].reshape(per * rows, width)
+
+        dtok = dot_nt(dgate_ref[...], weight(1)) + dot_nt(dup_ref[...], weight(2))
+        branch = dot_nt(act_ref[...], weight(0))
+        if before:
+            branch = branch + before[0][:, cols].astype(F32)
+            dtok = dtok + before[1][:, cols].astype(F32)
+        dtok_ref[:, cols] = dtok.astype(BF)
+        branch_ref[:, cols] = branch.astype(BF)
+
+
+def feed(tokens, cot, weights, *before):
+    n, width, tile = tokens.shape[0], weights.shape[-1], 256
+    chunks = [(i, min(256, width - i)) for i in range(0, width, 256)]
+    wide = pl.BlockSpec((tile, D), lambda i: (i, 0))
+    inner = pl.BlockSpec((tile, width), lambda i: (i, 0))
+    return pl.pallas_call(
+        functools.partial(feed_kernel, chunks),
+        grid=(n // tile,),
+        in_specs=[wide, wide, pl.BlockSpec(memory_space=pltpu.VMEM)] + [wide] * len(before),
+        out_specs=[inner, inner, inner, wide, wide],
+        out_shape=[jax.ShapeDtypeStruct((n, k), BF) for k in (width, width, width, D, D)],
+        compiler_params=pltpu.CompilerParams(vmem_limit_bytes=VMEM_LIMIT),
+        cost_estimate=pl.CostEstimate(
+            flops=12 * n * D * width, bytes_accessed=40 * 2**20, transcendentals=n * width
+        ),
+    )(tokens, cot, weights, *before)
+
+
+def plain_grads_kernel(t_ref, c_ref, act_ref, dgate_ref, dup_ref, grad_ref):
+    per, _, rows, width = grad_ref.shape
+    for m, (left, right) in enumerate(((c_ref, act_ref), (t_ref, dgate_ref), (t_ref, dup_ref))):
+        made = dot_tn(left[...], right[...]).astype(BF)
+        grad_ref[:, m] = made.reshape(per, rows, width)
+
+
+def plain_grads(tokens, cot, act, dgate, dup, places):
+    n, width = act.shape
+    rows = D // places
+    per = max(1, LANES * 3 // rows)
+    left = pl.BlockSpec((n, per * rows), lambda k: (0, k))
+    right = pl.BlockSpec(memory_space=pltpu.VMEM)
+    return pl.pallas_call(
+        plain_grads_kernel,
+        grid=(places // per,),
+        in_specs=[left, left, right, right, right],
+        out_specs=pl.BlockSpec((per, 3, rows, width), lambda k: (k, 0, 0, 0)),
+        out_shape=jax.ShapeDtypeStruct((places, 3, rows, width), BF),
+        compiler_params=pltpu.CompilerParams(vmem_limit_bytes=VMEM_LIMIT),
+        cost_estimate=pl.CostEstimate(
+            flops=6 * n * D * width, bytes_accessed=40 * 2**20, transcendentals=0
+        ),
+    )(tokens, cot, act, dgate, dup)
+
+
+def grads_kernel(plans, sizes, dtok_ref, t_hbm, c_hbm, act_hbm, dgate_hbm, dup_hbm, *refs):
+    sum_ref, grad_hbm, left_s, right_s, made_s, load_sems, made_sems = refs[:7]
+    per, rows = made_s.shape[1:3]
+    cols = per * rows
+    loads = [
+        pltpu.make_async_copy(c_hbm, left_s.at[0], load_sems.at[0]),
+        pltpu.make_async_copy(act_hbm, right_s.at[0], load_sems.at[1]),
+        pltpu.make_async_copy(t_hbm, left_s.at[1], load_sems.at[2]),
+        pltpu.make_async_copy(dgate_hbm, right_s.at[1], load_sems.at[3]),
+        pltpu.make_async_copy(dup_hbm, right_s.at[0], load_sems.at[4]),
+    ]
+    for copy in loads[:4]:
+        copy.start()
+
+    def stored(m, k, slot):
+        return pltpu.make_async_copy(
+            made_s.at[slot], grad_hbm.at[pl.ds(k * per, per), m], made_sems.at[slot]
+        )
+
+    def some(m, low, high, left, right, fresh):
+        def one(k, carry):
+            slot = lax.rem(k, 2)
+            if fresh:
+                pl.when(k >= 2)(lambda: stored(m, k, slot).wait())
+            else:
+                stored(m, k, slot).wait()
+            part = left_s[left, :, pl.ds(pl.multiple_of(k * cols, LANES), cols)]
+            made_s[slot] = dot_tn(part, right_s[right]).astype(BF).reshape(made_s.shape[1:])
+            stored(m, k, slot).start()
+            return carry
+
+        lax.fori_loop(low, high, one, 0)
+
+    chunks = D // cols
+
+    def between(phase):
+        if phase == 0:
+            loads[0].wait()
+            loads[1].wait()
+            some(0, 0, chunks // 2, 0, 0, True)
+        elif phase == 1:
+            some(0, chunks // 2, chunks, 0, 0, False)
+            loads[4].start()
+            loads[2].wait()
+            loads[3].wait()
+            some(1, 0, chunks, 1, 1, False)
+        else:
+            loads[4].wait()
+            some(2, 0, chunks, 1, 0, False)
+
+    scatter_kernel(plans, sizes, dtok_ref, sum_ref, *refs[7:], between=between)
+    for slot in range(2):
+        stored(2, slot, slot).wait()
+
+
+def feed_grads(dtok, tokens, cot, act, dgate, dup, places, plans, sizes, collective_id):
+    plans = alive(plans, sizes)
+    n, width = act.shape
+    rows = D // places
+    per = max(1, LANES * 3 // rows)
+    spec = pl.BlockSpec(memory_space=pltpu.VMEM)
+    far = pl.BlockSpec(memory_space=pl.ANY)
+    return pl.pallas_call(
+        functools.partial(grads_kernel, plans, sizes),
+        out_shape=[
+            jax.ShapeDtypeStruct(dtok.shape[1:], F32),
+            jax.ShapeDtypeStruct((places, 3, rows, width), BF),
+        ],
+        in_specs=[spec] + [far] * 5,
+        out_specs=[spec, far],
+        scratch_shapes=[
+            pltpu.VMEM((2, n, D), BF),
+            pltpu.VMEM((2, n, width), BF),
+            pltpu.VMEM((2, per, rows, width), BF),
+            pltpu.SemaphoreType.DMA((5,)),
+            pltpu.SemaphoreType.DMA((2,)),
+        ]
+        + scatter_scratch([dtok], plans, [F32], sizes),
+        compiler_params=pltpu.CompilerParams(
+            collective_id=collective_id, has_side_effects=True, vmem_limit_bytes=VMEM_LIMIT
+        ),
+        cost_estimate=pl.CostEstimate(
+            flops=6 * n * D * width, bytes_accessed=100 * 2**20, transcendentals=0
+        ),
+    )(dtok, tokens, cot, act, dgate, dup)
 
 
 def forward_kernel(heads, slots, tops, q_ref, kv_ref, o_ref, lse_ref, top_s, sum_s, acc_s):
@@ -341,6 +540,7 @@
                 acc_s[h] / total
             ).T
             lse_ref[a, h : h + 1, :] = top_s[h : h + 1, :] * SCALE2 + jnp.log2(total)
+        lse_ref[a, heads:8, :] = jnp.zeros((8 - heads, BLOCK), F32)
 
 
 def attend(slots, tops, q, kv):
@@ -521,12 +721,18 @@
     small = small_rows(
         *[v.astype(BF) for v in (norm1, norm2, q_bias, k_bias, v_bias)]
     )
-    w_qkv, x_pair, small_all = gather(
-        [jnp.stack(halves), hidden, small],
-        [(AXES, True), (("head",), False), (AXES, False)],
+    w_qkv, x_pair, small_all, w_out = gather(
+        [jnp.stack(halves), hidden, small, o_weight.astype(BF)],
+        [
+            (0, None, AXES, AXES, True),
+            (1, None, ("head",), ("head",), False),
+            (2, None, AXES, AXES, False),
+            (3, None, BLK, BLK, False),
+        ],
         sizes,
         1,
     )
+    w_out = w_out.reshape(q_cols, D)
     w_qkv = w_qkv.reshape(D, q_cols + 2 * kv_cols)
     x_pair = x_pair.reshape(pair, D).astype(F32)
     gain_one = small_all[:, 0, :rows].reshape(D)
@@ -539,43 +745,51 @@
         for i in (3, 4)
     )
 
-    nz = sizes["z"]
+    near = ("y", "c")
+    parts = sizes["y"] * sizes["c"]
     width = gate_weight.shape[1]
-    lanes = -(-width // (LANES * nz)) * LANES
-    wide = lanes * nz
-    z = lax.axis_index("z")
-    core = lax.axis_index("c")
+    lanes = -(-width // (LANES * parts)) * LANES
+    wide = lanes * parts
+    corner = place_of({}, near, sizes)
     ff_rows = gate_weight.shape[0]
+
+    def corner_send(blocks):
+        got = [lax.dynamic_index_in_dim(blocks, corner, 0, keepdims=False)]
+        for d in range(1, parts):
+            piece = lax.dynamic_index_in_dim(blocks, corner ^ d, 0, keepdims=False)
+            got.append(lax.ppermute(piece, near, [(i, i ^ d) for i in range(parts)]))
+        return got
+
+    def corner_sort(got):
+        held = jnp.stack(got)
+        return [lax.dynamic_index_in_dim(held, corner ^ i, 0, keepdims=False) for i in range(parts)]
 
     def quarters(weight):
         padded = jnp.pad(weight.astype(BF), ((0, 0), (0, wide - width)))
-        return padded.reshape(ff_rows, nz, lanes).transpose(1, 0, 2)
-
-    def spread(packed):
-        got = [lax.dynamic_index_in_dim(packed, z, 0, keepdims=False)]
-        for d in range(1, nz):
-            piece = lax.dynamic_index_in_dim(packed, (z + d) % nz, 0, keepdims=False)
-            got.append(shift(piece, "z", d, sizes))
-        mine = jnp.stack(got)
-        over = ("head", "g", "y")
-        everything = lax.all_gather(mine, live(over, sizes), axis=0, tiled=False)
-        everything = everything.reshape((2, sizes["g"], sizes["y"]) + mine.shape)
-        other = lax.dynamic_index_in_dim(everything, 1 - core, 0, keepdims=False)
-        keep = lax.dynamic_index_in_dim(everything, core, 0, keepdims=False)
-        swapped = shift(other, "c", 1, sizes)
-        both = jnp.where(core == 0, jnp.stack([keep, swapped]), jnp.stack([swapped, keep]))
-        by_z = jnp.stack(
-            [lax.dynamic_index_in_dim(both, (z - i) % nz, 3, keepdims=False) for i in range(nz)]
-        )
-        full = by_z.transpose(4, 2, 0, 3, 1, 5, 6)
-        return full.reshape(full.shape[0], D, lanes)
-
-    tied = lax.optimization_barrier((gate_weight, up_weight, down_weight, w_qkv))
-    w_gate, w_up = spread(jnp.stack([quarters(tied[0]), quarters(tied[1])], axis=1))
-    (w_down,) = spread(quarters(tied[2])[:, None])
-
-    w_out = lax.all_gather(o_weight.astype(BF), live(AXES, sizes), axis=0, tiled=True)
-    cot_all = lax.all_gather(cotangent, ("z", "c"), axis=0, tiled=True)
+        return padded.reshape(ff_rows, parts, lanes).transpose(1, 0, 2)
+
+    packed = jnp.stack([quarters(w) for w in (down_weight, gate_weight, up_weight)], axis=1)
+    mine = jnp.stack(corner_sort(corner_send(packed)), axis=1)
+    mine = mine.reshape(1, 3, parts * ff_rows, lanes)
+    first = lanes * 4 // 9 // LANES * LANES
+
+    def along_z(part, zero):
+        part = (part.astype(F32) + zero).astype(BF)
+        return lax.all_gather(part, live(("g", "z"), sizes), axis=0, tiled=True)
+
+    w_feed_one = along_z(mine[..., :first], small_all[0, 7, 0])
+
+    def halved(value, axis, dim, kind=BF):
+        me = lax.axis_index(axis)
+        away = lax.dynamic_index_in_dim(value, 1 - me, dim, keepdims=False)
+        keep = lax.dynamic_index_in_dim(value, me, dim, keepdims=False)
+        return (keep.astype(F32) + shift(away, axis, 1, sizes).astype(F32)).astype(kind)
+
+    def group_sum(value, kind):
+        near_sum = halved(value.reshape(2, 2, 2, tok, D), "c", 2)
+        one = halved(near_sum[:, :, :half], "head", 0)
+        two = halved(near_sum[:, :, half:], "y", 1)
+        return jnp.concatenate([halved(one, "y", 0, kind), halved(two, "head", 0, kind)])
 
     scale_one = inverse_rms(x_pair)
     normed = (x_pair * scale_one * gain_one).astype(BF)
@@ -583,64 +797,71 @@
     queries = rotate(qkv[:, :q_cols] + bias_q, cosine, sine).astype(BF)
     keys = rotate(qkv[:, q_cols : q_cols + kv_cols] + bias_k, cosine, sine).astype(BF)
     values = (qkv[:, q_cols + kv_cols :] + bias_v).astype(BF)
-    (kv,) = gather(
-        [jnp.concatenate([keys, values], axis=1)], [(place_axes, False)], sizes, 2
-    )
+    group = ("head", "y", "c")
+    half = tok // 2
+    crossed = [
+        ((0, half), group, ("head", "y", "c"), False),
+        ((half, half), group, ("y", "head", "c"), False),
+    ]
+    kv, cot_all = gather(
+        [jnp.concatenate([keys, values], axis=1), cotangent],
+        [
+            (0, None, place_axes, place_axes, False),
+            (1, None, group, ("y", "head", "c"), False),
+        ],
+        sizes,
+        2,
+    )
+    cot_all = cot_all.reshape(-1, D)
     kv = kv.reshape(2 * SEQ_SPAN, tok, 2 * HEAD_DIM)
     attended, lse = attend(slots, tops, queries, kv)
+    w_feed_two = along_z(mine[..., first:], lse[0, 7, 0])
     attn_local = attended.astype(BF)
-    (attn_halves,) = gather([attn_local.reshape(2, tok, q_cols)], [(("head",), True)], sizes, 3)
     inputs = lax.dynamic_slice_in_dim(x_pair, head * tok, tok)
-    mixed = inputs + (
-        dot_nn(attn_halves[0], w_out[:q_cols]) + dot_nn(attn_halves[1], w_out[q_cols:])
-    )
+    mixed_part = dot_nn(attn_local, w_out).astype(BF).reshape(2, tok, D)
+    (mixed_sum,) = scatter(
+        [mixed_part], [(0, None, ("head",), ("head",), False)], [F32], sizes, 3
+    )
+    mixed = inputs + mixed_sum
     scale_two = inverse_rms(mixed)
     normed_two = (mixed * scale_two * gain_two).astype(BF)
-    (tokens,) = gather([normed_two], [(("z", "c"), False)], sizes, 4)
+    (tokens,) = gather([normed_two], [(0,) + c for c in crossed], sizes, 4)
     tokens = tokens.reshape(-1, D)
 
-    gate = dot_nn(tokens, w_gate)
-    up = dot_nn(tokens, w_up)
-    sig = jax.nn.sigmoid(gate)
-    act = (gate * sig * up).astype(BF)
-    dact = dot_nn(cot_all, w_down)
-    dgate = (dact * up * sig * (1.0 + gate * (1.0 - sig))).astype(BF)
-    dup = (dact * gate * sig).astype(BF)
-    dtokens = (dot_nt(dgate, w_gate) + dot_nt(dup, w_up)).astype(BF)
-    (dnormed_two,) = scatter(
-        [dtokens.reshape(-1, tok, D)], [(("z", "c"), False)], [F32], sizes, 5
-    )
-    branch = dot_nt(act, w_down).astype(BF)
-    branch_sum = lax.psum_scatter(branch, ("z", "c"), scatter_dimension=0, tiled=True)
-    output = (mixed + branch_sum.astype(F32)).astype(BF)
+    places = w_feed_one.shape[0]
+    act, dgate, dup, branch, dtokens = feed(tokens, cot_all, w_feed_one)
+    parts_one = plain_grads(tokens, cot_all, act, dgate, dup, places)
+    act, dgate, dup, branch, dtokens = feed(tokens, cot_all, w_feed_two, branch, dtokens)
+    dnormed_two, parts_two = feed_grads(
+        dtokens.reshape(-1, tok, D),
+        tokens,
+        cot_all,
+        act,
+        dgate,
+        dup,
+        places,
+        [
+            (0, (0, half), group, ("c", "head", "y"), False),
+            (0, (half, half), group, ("c", "y", "head"), False),
+        ],
+        sizes,
+        5,
+    )
+    branch_sum = group_sum(branch, F32)
+    output = (mixed + branch_sum).astype(BF)
 
     def collect(grad):
-        mats = grad.shape[0]
-        parts = grad.reshape(
-            (mats, sizes["g"], nz, sizes["y"], sizes["c"], ff_rows, lanes)
-        ).transpose(4, 1, 3, 2, 0, 5, 6)
-        other = lax.dynamic_index_in_dim(parts, 1 - core, 0, keepdims=False)
-        keep = lax.dynamic_index_in_dim(parts, core, 0, keepdims=False)
-        swapped = shift(other, "c", 1, sizes)
-        both = jnp.where(core == 0, jnp.stack([keep, swapped]), jnp.stack([swapped, keep]))
-        both = both.reshape((-1,) + both.shape[3:])
-        mine = lax.psum_scatter(
-            both, live(("head", "g", "y"), sizes), scatter_dimension=0, tiled=True
-        )[0]
-        got = [lax.dynamic_index_in_dim(mine, z, 0, keepdims=False)]
-        for d in range(1, nz):
-            piece = lax.dynamic_index_in_dim(mine, (z + d) % nz, 0, keepdims=False)
-            got.append(shift(piece, "z", d, sizes))
-        held = jnp.stack(got)
-        by_z = jnp.stack(
-            [lax.dynamic_index_in_dim(held, (z - i) % nz, 0, keepdims=False) for i in range(nz)]
+        total = lax.psum_scatter(grad, live(("g", "z"), sizes), scatter_dimension=0, tiled=True)
+        total = total.reshape(3, parts, ff_rows, grad.shape[-1])
+        return corner_sort(corner_send(total.transpose(1, 0, 2, 3)))
+
+    back = list(zip(collect(parts_one), collect(parts_two)))
+    d_down, d_gate, d_up = (
+        jnp.concatenate([half[m] for pair_ in back for half in pair_], axis=1)[:, :width].astype(
+            F32
         )
-        return by_z.transpose(1, 2, 0, 3).reshape(mats, ff_rows, wide)[:, :, :width].astype(F32)
-
-    d_gate_up = collect(
-        jnp.stack([dot_tn(tokens, dgate).astype(BF), dot_tn(tokens, dup).astype(BF)])
-    )
-    d_down = collect(dot_tn(cot_all, act).astype(BF)[None])
+        for m in range(3)
+    )
 
     z_two = mixed * scale_two
     u_two = gain_two * dnormed_two
@@ -649,28 +870,20 @@
         u_two - z_two * jnp.mean(z_two * u_two, axis=-1, keepdims=True)
     )
     dproj = dmixed.astype(BF)
-    dattn = dot_nt(dproj, w_out).astype(BF)
-    (dout,) = gather(
-        [dattn.reshape(tok, 2, q_cols).transpose(1, 0, 2)], [(("head",), True)], sizes, 6
-    )
-    dout = dout.reshape(pair, q_cols)
+    (dproj_pair,) = gather([dproj], [(0, None, ("head",), ("head",), False)], sizes, 6)
+    dproj_pair = dproj_pair.reshape(pair, D)
+    dout = dot_nt(dproj_pair, w_out).astype(BF)
     delta = jnp.sum(
         (dout.astype(F32) * attended).reshape(2, tok, q_cols // HEAD_DIM, HEAD_DIM), axis=-1
     ).transpose(0, 2, 1)
     delta = jnp.pad(delta, ((0, 0), (0, 8 - delta.shape[1]), (0, 0)))
 
-    dproj_other = shift(dproj, "head", 1, sizes)
-    own_attn = lax.dynamic_slice_in_dim(attn_local, head * tok, tok)
-    other_attn = lax.dynamic_slice_in_dim(attn_local, (1 - head) * tok, tok)
-    o_part = (dot_tn(own_attn, dproj) + dot_tn(other_attn, dproj_other)).astype(BF)
-    d_out_weight = lax.psum_scatter(
-        o_part, live(BLK, sizes), scatter_dimension=0, tiled=True
-    ).astype(F32)
+    o_part = dot_tn(attn_local, dproj_pair).astype(BF)
 
     dq, dkv_parts = attend_back(slots, tops, queries, kv, dout, lse, delta)
     (dkv,) = scatter(
         [dkv_parts.reshape(SEQ_SPAN, pair, 2 * HEAD_DIM)],
-        [(place_axes, False)],
+        [(0, None, place_axes, place_axes[::-1], False)],
         [BF],
         sizes,
         7,
@@ -706,14 +919,20 @@
         axis=2,
     )
     small_grads = small_grads.transpose(1, 0, 2, 3).reshape(2 * blk, 8, LANES)
-    w_grads, small_sum, dnormed_sum = scatter(
+    w_grads, small_sum, dnormed_sum, d_out_weight = scatter(
         [
             w_part.reshape(2, blk, rows, -1).transpose(1, 0, 2, 3),
             small_grads,
             dnormed.astype(BF).reshape(2, tok, D),
+            o_part.reshape(blk, -1, D),
         ],
-        [(BLK, True), (AXES, False), (("head",), False)],
-        [F32, F32, F32],
+        [
+            (0, None, BLK, BLK[::-1], True),
+            (1, None, AXES, AXES[::-1], False),
+            (2, None, ("head",), ("head",), False),
+            (3, None, BLK, BLK[::-1], False),
+        ],
+        [F32, F32, F32, F32],
         sizes,
         8,
     )
@@ -736,9 +955,9 @@
         small_sum[4, :kn],
         d_out_weight,
         small_sum[1, :rows],
-        d_gate_up[0],
-        d_gate_up[1],
-        d_down[0],
+        d_gate,
+        d_up,
+        d_down,
     )
 
 

time: 1090 us -> 747 us (0.69)
  waiting for transfers between devices: 224 us -> 55.6 us
  matrix products: 149 us -> 24.4 us
  other arithmetic: 86.9 us -> 64.2 us
  local copies, waits for them, and re-layouts: 80.3 us -> 68.6 us
    pallas_call x0 -> x4, Pallas kernels: none -> 123 us  [the longest x2 68.9 us: feed(): pl.pallas_call(functools.partial(feed_kernel, chunks), grid=(n // tile,),...]
    unnamed x8 -> x4, waiting for transfers between devices: 83.9 us -> 0.07 us
    ppermute x17 -> x5, waiting for transfers between devices: 98.4 us -> 20.3 us  [shift(): lax.ppermute(value, axis, [(i, (i + distance) % n) for i in range(n)])]
    pallas_call x3, Pallas kernels: 197 us -> 121 us  [scatter(): pl.pallas_call(functools.partial(scatter_kernel, plans, sizes), out_shape...]
    dot_general x6 -> x2, matrix products: 53.3 us -> 5.98 us  [dot_nn(): lax.dot_general(a, b, (((1,), (0,)), ((), ())), preferred_element_type=F32)]
    pallas_call x5 -> x4, Pallas kernels: 224 us -> 182 us  [gather(): pl.pallas_call(functools.partial(gather_kernel, plans, sizes), out_shape=...]
    dot_general x5 -> x2, matrix products: 51.5 us -> 10.1 us  [dot_nt(): lax.dot_general(a, b, (((1,), (1,)), ((), ())), preferred_element_type=F32)]
    dot_general x6 -> x2, matrix products: 43.8 us -> 8.34 us  [dot_tn(): lax.dot_general(a, b, (((0,), (0,)), ((), ())), preferred_element_type=F32)]
  transfers between devices with their start and end apart: 24 -> 18, of which waited for: 13 -> 8; matrix products, arithmetic and copies ran while one was open for 20% -> 15% of each run, Pallas kernels for 35% -> 68%
where the time goes in v2:
time: 747 us; the launch traced here: 738 us
  Pallas kernels  498 us (67%)
  local copies, waits for them, and re-layouts  68.6 us (9%)
  other arithmetic  64.2 us (9%)
  waiting for transfers between devices  55.6 us (7%)
  matrix products  24.4 us (3%)
  between operations  14.9 us (2%)
  starting transfers between devices  11.7 us (2%)
    pallas_call x4, Pallas kernels, gather(): pl.pallas_call(functools.partial(gather_kernel, plans, sizes), out_shape=...  182 us
    pallas_call x3, Pallas kernels, scatter(): pl.pallas_call(functools.partial(scatter_kernel, plans, sizes), out_shape...  121 us
    pallas_call x2, Pallas kernels, feed(): pl.pallas_call(functools.partial(feed_kernel, chunks), grid=(n // tile,),...  68.9 us
    pallas_call x1, Pallas kernels, attend_back(): pl.pallas_call(functools.partial(backward_kernel, heads), grid_spec=pltpu...  43.3 us
    pallas_call x1, Pallas kernels, feed_grads(): pl.pallas_call(functools.partial(grads_kernel, plans, sizes), out_shape=[...  39.1 us
    pallas_call x1, Pallas kernels, attend(): pl.pallas_call(functools.partial(forward_kernel, heads), grid_spec=pltpu....  28.3 us
    ppermute x9, waiting for transfers between devices, corner_send(): got.append(lax.ppermute(piece, near, [(i, i ^ d) for i in range(parts)]))  20.8 us
    ppermute x5, waiting for transfers between devices, shift(): lax.ppermute(value, axis, [(i, (i + distance) % n) for i in range(n)])  20.3 us
  transfers between devices with their start and end apart: 18, of which 8 were waited for; matrix products, arithmetic and copies ran while one was open for 15% of the time, Pallas kernels for 68%

profile of v2, /device:TPU:0, one launch (start us, length us, event | category | flops | bytes accessed | tf_op | source)
XLA Modules:
  0.0 737.6 jit_solution(2652267577476033765)
XLA Ops:
  17.1 5.5 constant_dynamic-slice_fusion.10
  30.9 62.1 %shard_map.254 = (bf16[32,48,1024]{2,1,0:T(8,128)(2,1)}, bf16[2,256,1536]{2,1,0:T(8,128)(2,1)}, f32[32,8,128]{2,1,0:T(8,128)}, bf16[16,48,1536]{2,1,0:T(8,128)(2,1)}) custom-call(bf16[2,48,1024]{2,1,0:T(8,128)(2,1)} %maximum_maximum_fusion.refs_0_, bf16[256,1536]{1,0:T(8,128)(2,1)} %refs_1_.2, f32[8,128]{1,0:T(8,128)} %stack.140.refs_2_, ...), custom_call_target="tpu_custom_call" | custom-call | bytes 144179200 | tf_op jit(solution)/shard_map/pallas_call | solution.py:156
  100.6 6.2 pad_maximum_fusion.1
  106.8 5.8 constant_dynamic-slice_fusion.6
  132.7 63.4 %shard_map.255 = (bf16[16,512,256]{2,1,0:T(8,128)(2,1)}, bf16[8,256,1536]{2,1,0:T(8,128)(2,1)}) custom-call(bf16[512,256]{1,0:T(8,128)(2,1)} %pad_maximum_fusion.9.refs_0_, bf16[256,1536]{1,0:T(8,128)(2,1)} %refs_1_.3), custom_call_target="tpu_custom_call" | custom-call | bytes 209715200 | tf_op jit(solution)/shard_map/pallas_call | solution.py:156
  197.7 28.3 %shard_map.256 = (f32[512,768]{1,0:T(8,128)}, f32[2,8,256]{2,1,0:T(8,128)}) custom-call(s32[32]{0:T(128)} %get-tuple-element.42.slots, s32[2]{0:T(128)} %get-tuple-element.78.tops, bf16[512,768]{1,0:T(8,128)(2,1)} %copy.90.q_ref, bf16[32,256,256]{2,1,0:T(8,128)(2,1)} %bitcast.358), custom_call_target="tpu_custom_call" | custom-call | flops 6643777536 | bytes 83886080 | tf_op jit(solution)/shard_map/pallas_call | solution.py:550
  233.7 22.5 %shard_map.257 = f32[256,1536]{1,0:T(8,128)} custom-call(bf16[2,256,1536]{2,1,0:T(8,128)(2,1)} %bitcast.328), custom_call_target="tpu_custom_call" | custom-call | bytes 31457280 | tf_op jit(solution)/shard_map/pallas_call | solution.py:315
  261.2 34.7 %shard_map.258 = bf16[8,256,1536]{2,1,0:T(8,128)(2,1)} custom-call(bf16[256,1536]{1,0:T(8,128)(2,1)} %multiply_convert_fusion.3.refs_0_), custom_call_target="tpu_custom_call" | custom-call | bytes 125829120 | tf_op jit(solution)/shard_map/pallas_call | solution.py:156
  295.9 28.5 %shard_map.259 = (bf16[2048,512]{1,0:T(8,128)(2,1)}, bf16[2048,512]{1,0:T(8,128)(2,1)}, bf16[2048,512]{1,0:T(8,128)(2,1)}, bf16[2048,1536]{1,0:T(8,128)(2,1)}, bf16[2048,1536]{1,0:T(8,128)(2,1)}) custom-call(bf16[2048,1536]{1,0:T(8,128)(2,1)} %bitcast.308, bf16[2048,1536]{1,0:T(8,128)(2,1)} %bitcast.354, ...), custom_call_target="tpu_custom_call" | custom-call | flops 19327352832 | bytes 41943040 | tf_op jit(solution)/shard_map/pallas_call | solution.py:373
  324.4 15.5 %shard_map.266 = bf16[4,3,384,512]{3,2,1,0:T(8,128)(2,1)} custom-call(bf16[2048,1536]{1,0:T(8,128)(2,1)} %bitcast.309, bf16[2048,1536]{1,0:T(8,128)(2,1)} %bitcast.355, bf16[2048,512]{1,0:T(8,128)(2,1)} %get-tuple-element.64.act_ref, bf16[2048,512]{1,0:T(8,128)(2,1)} %get-tuple-element.65.dgate_ref, bf16[2048,512]{1,0:T(8,128)(2,1)} %get-tuple-element.66.dup_ref), custom_call_target="tpu_custom_call" | custom-call | flops 9663676416 | bytes 41943040 | tf_op jit(solution)/shard_map/pallas_call | solution.py:399
  341.8 14.4 %all-gather.3.cloned.1.call-done.w_ref = bf16[4,3,384,640]{3,2,1,0:T(8,128)(2,1)} async-done(((bf16[1,3,384,640]{3,2,1,0:T(8,128)(2,1)}), bf16[4,3,384,640]{3,2,1,0:T(8,128)(2,1)}) %all-gather.3.cloned.1.call-update) | async-done | bytes 5898256 | tf_op jit(solution)/shard_map/all_gather | solution.py:778
  356.3 40.4 %shard_map.260 = (bf16[2048,640]{1,0:T(8,128)(2,1)}, bf16[2048,640]{1,0:T(8,128)(2,1)}, bf16[2048,640]{1,0:T(8,128)(2,1)}, bf16[2048,1536]{1,0:T(8,128)(2,1)}, bf16[2048,1536]{1,0:T(8,128)(2,1)}) custom-call(bf16[2048,1536]{1,0:T(8,128)(2,1)} %bitcast.310, bf16[2048,1536]{1,0:T(8,128)(2,1)} %bitcast.356, ...), custom_call_target="tpu_custom_call" | custom-call | flops 24159191040 | bytes 41943040 | tf_op jit(solution)/shard_map/pallas_call | solution.py:373
  396.7 39.1 %shard_map.261 = (f32[256,1536]{1,0:T(8,128)}, bf16[4,3,384,640]{3,2,1,0:T(8,128)(2,1)}) custom-call(bf16[8,256,1536]{2,1,0:T(8,128)(2,1)} %bitcast.364, bf16[2048,1536]{1,0:T(8,128)(2,1)} %bitcast.311, bf16[2048,1536]{1,0:T(8,128)(2,1)} %bitcast.357, bf16[2048,640]{1,0:T(8,128)(2,1)} %get-tuple-element.54.act_hbm, ...), custom_call_target="tpu_custom_call" | custom-call | flops 12079595520 | bytes 104857600 | tf_op jit(solution)/shard_map/pallas_call | solution.py:474
  442.3 21.7 %shard_map.262 = bf16[2,256,1536]{2,1,0:T(8,128)(2,1)} custom-call(bf16[256,1536]{1,0:T(8,128)(2,1)} %fusion.56.refs_0_), custom_call_target="tpu_custom_call" | custom-call | bytes 31457280 | tf_op jit(solution)/shard_map/pallas_call | solution.py:156
  476.7 43.3 %shard_map.263 = (bf16[512,768]{1,0:T(8,128)(2,1)}, bf16[32,256,256]{2,1,0:T(8,128)(2,1)}) custom-call(s32[32]{0:T(128)} %get-tuple-element.42.slots, s32[2]{0:T(128)} %get-tuple-element.78.tops, bf16[512,768]{1,0:T(8,128)(2,1)} %copy.90.q_ref, bf16[32,256,256]{2,1,0:T(8,128)(2,1)} %bitcast.359, bf16[512,768]{1,0:T(8,128)(2,1)} %get-tuple-element.167.do_ref, ...), custom_call_target="tpu_custom_call" | custom-call | flops 16609443840 | bytes 125829120 | tf_op jit(solution)/shard_map/pallas_call | solution.py:622
  522.5 44.7 %shard_map.264 = bf16[512,256]{1,0:T(8,128)(2,1)} custom-call(bf16[16,512,256]{2,1,0:T(8,128)(2,1)} %bitcast.315), custom_call_target="tpu_custom_call" | custom-call | bytes 83886080 | tf_op jit(solution)/shard_map/pallas_call | solution.py:315
  572.9 5.1 constant_dynamic-slice_fusion.2
  581.9 5.9 fusion.58
  594.7 4.7 convolution_convert_fusion.1
  599.4 54.1 %shard_map.265 = (f32[2,48,1024]{2,1,0:T(8,128)}, f32[8,128]{1,0:T(8,128)}, f32[256,1536]{1,0:T(8,128)}, f32[48,1536]{1,0:T(8,128)}) custom-call(bf16[16,2,48,1024]{3,2,1,0:T(8,128)(2,1)} %bitcast.305, f32[32,8,128]{2,1,0:T(8,128)} %bitcast.332, bf16[2,256,1536]{2,1,0:T(8,128)(2,1)} %bitcast.325, bf16[16,48,1536]{2,1,0:T(8,128)(2,1)} %bitcast.324), custom_call_target="tpu_custom_call" | custom-call | bytes 144179200 | tf_op jit(solution)/shard_map/pallas_call | solution.py:315
  663.7 15.9 %collective-permute-done.4 = bf16[2,128,1536]{2,1,0:T(8,128)(2,1)S(1)} collective-permute-done((bf16[2,128,1536]{2,1,0:T(8,128)(2,1)S(1)}, bf16[2,128,1536]{2,1,0:T(8,128)(2,1)S(1)}, u32[]{:S(2)}, u32[]{:S(2)}) %collective-permute-start.4) | collective-permute-done | bytes 786464 | tf_op jit(solution)/shard_map/ppermute | solution.py:662
  704.5 5.5 collective-permute-done.10
  711.3 7.3 collective-permute-done.12
  718.6 7.1 collective-permute-done.13
  (283 shorter events, 141.2 us)
Async XLA Ops:
  7.2 288.7 %all-gather.5.cloned.1.call-start = ((), (), s32[]{:S(2)}) async-start(), calls=%async_computation.3 | async-start | bytes 5898240 | tf_op jit(solution)/shard_map/all_gather | solution.py:778
  23.6 70.6 %collective-permute-start = (bf16[3,96,1152]{2,1,0:T(8,128)(2,1)}, bf16[3,96,1152]{2,1,0:T(8,128)(2,1)}, u32[]{:S(2)}, u32[]{:S(2)}) collective-permute-start(bf16[3,96,1152]{2,1,0:T(8,128)(2,1)} %bitcast.300), channel_id=1, source_target_pairs={{0,1},{1,0},{2,3},{3,2},{4,5},{5,4},{6,7},{7,6},{8,9},{9,8},{10,11... | collective-permute-start | bytes 1990664 | tf_op jit(solution)/shard_map/ppermute | solution.py:760
  25.0 71.3 %collective-permute-start.1 = (bf16[3,96,1152]{2,1,0:T(8,128)(2,1)}, bf16[3,96,1152]{2,1,0:T(8,128)(2,1)}, u32[]{:S(2)}, u32[]{:S(2)}) collective-permute-start(bf16[3,96,1152]{2,1,0:T(8,128)(2,1)} %bitcast.299), channel_id=1, source_target_pairs={{0,2},{1,3},{2,0},{3,1},{4,6},{5,7},{6,4},{7,5},{8,10},{9,11},{10,... | collective-permute-start | bytes 1990664 | tf_op jit(solution)/shard_map/ppermute | solution.py:760
  28.5 69.9 %collective-permute-start.2 = (bf16[3,96,1152]{2,1,0:T(8,128)(2,1)}, bf16[3,96,1152]{2,1,0:T(8,128)(2,1)}, u32[]{:S(2)}, u32[]{:S(2)}) collective-permute-start(bf16[3,96,1152]{2,1,0:T(8,128)(2,1)} %bitcast.298), channel_id=1, source_target_pairs={{0,3},{1,2},{2,1},{3,0},{4,7},{5,6},{6,5},{7,4},{8,11},{9,10},{10,... | collective-permute-start | bytes 1990664 | tf_op jit(solution)/shard_map/ppermute | solution.py:760
  117.2 239.1 %all-gather.3.cloned.1.call-start = ((), (), s32[]{:S(2)}) async-start(), calls=%async_computation.2 | async-start | bytes 7372800 | tf_op jit(solution)/shard_map/all_gather | solution.py:778
  197.7 29.5 %copy-start.5 = (bf16[3,4,96,1152]{3,2,1,0:T(8,128)(2,1)S(1)}, bf16[3,4,96,1152]{3,2,1,0:T(8,128)(2,1)}, u32[]{:S(2)}) copy-start(bf16[3,4,96,1152]{3,2,1,0:T(8,128)(2,1)} %copy-done.4) | copy-start | bytes 7962628
  229.4 460.7 %reduce-scatter.3.cloned.1.call-start = ((), (), s32[]{:S(2)}) async-start(), calls=%async_computation.4 | async-start | bytes 5898240 | tf_op jit(solution)/shard_map/reduce_scatter | solution.py:854
  260.1 178.2 %copy-start.27 = (f32[256]{0:T(256)}, f32[256]{0:T(256)S(1)}, u32[]{:S(2)}) copy-start(f32[256]{0:T(256)S(1)} %add_rsqrt_fusion.1) | copy-start | bytes 3076
  339.9 356.3 %reduce-scatter.5.cloned.1.call-start = ((), (), s32[]{:S(2)}) async-start(), calls=%async_computation.5 | async-start | bytes 7372800 | tf_op jit(solution)/shard_map/reduce_scatter | solution.py:854
  522.5 45.7 %copy-start.25 = (f32[1,2,2,128]{3,1,2,0:T(2,128)S(1)}, f32[1,2,2,128]{3,1,2,0:T(2,128)}, u32[]{:S(2)}) copy-start(f32[1,2,2,128]{3,1,2,0:T(2,128)} %copy-done.24) | copy-start | bytes 6148
  522.5 45.7 %copy-start.33 = (f32[64]{0:T(128)S(1)}, f32[64]{0:T(128)}, u32[]{:S(2)}) copy-start(f32[64]{0:T(128)} %copy-done.32) | copy-start | bytes 772
  579.9 78.1 %collective-permute-start.3 = (bf16[2,2,256,1536]{3,2,0,1:T(8,128)(2,1)}, bf16[2,2,256,1536]{3,2,0,1:T(8,128)(2,1)}, u32[]{:S(2)}, u32[]{:S(2)}) collective-permute-start(bf16[2,2,256,1536]{3,2,0,1:T(8,128)(2,1)} %bitcast.297), channel_id=1, source_target_pairs={{0,1},{1,0},{2,3},{3,2},{4,5},{5,4},{6,7},{7,6},{8,9},{9,8},{10,11... | collective-permute-start | bytes 9437192 | tf_op jit(solution)/shard_map/ppermute | solution.py:662
  599.4 55.6 %copy-start = (f32[512,1536]{1,0:T(8,128)S(1)}, f32[512,1536]{1,0:T(8,128)}, u32[]{:S(2)}) copy-start(f32[512,1536]{1,0:T(8,128)} %convert.118) | copy-start | bytes 9437188
  599.4 55.6 %copy-start.29 = (f32[256,1]{0,1:T(1,128)S(1)}, f32[256,1]{0,1:T(1,128)}, u32[]{:S(2)}) copy-start(f32[256,1]{0,1:T(1,128)} %constant_dynamic-slice_fusion) | copy-start | bytes 3076
  661.0 18.6 %collective-permute-start.4 = (bf16[2,128,1536]{2,1,0:T(8,128)(2,1)S(1)}, bf16[2,128,1536]{2,1,0:T(8,128)(2,1)S(1)}, u32[]{:S(2)}, u32[]{:S(2)}) collective-permute-start(bf16[2,128,1536]{2,1,0:T(8,128)(2,1)S(1)} %dynamic-slice_bitcast_fusion.1), channel_id=1, source_target_pairs={{0,16},{16,0},{1,17},{17,1},{2,18},{18,2},{3,19},{19,3},{4,20},{20... | collective-permute-start | bytes 2359304 | tf_op jit(solution)/shard_map/ppermute | solution.py:662
  662.4 18.3 %collective-permute-start.6 = (bf16[2,128,1536]{2,1,0:T(8,128)(2,1)S(1)}, bf16[2,128,1536]{2,1,0:T(8,128)(2,1)S(1)}, u32[]{:S(2)}, u32[]{:S(2)}) collective-permute-start(bf16[2,128,1536]{2,1,0:T(8,128)(2,1)S(1)} %dynamic-slice_bitcast_fusion), channel_id=1, source_target_pairs={{0,2},{2,0},{1,3},{3,1},{4,6},{6,4},{5,7},{7,5},{8,10},{10,8},{9,1... | collective-permute-start | bytes 2359304 | tf_op jit(solution)/shard_map/ppermute | solution.py:662
  679.8 9.3 %collective-permute-start.5 = (bf16[128,1536]{1,0:T(8,128)(2,1)S(1)}, bf16[128,1536]{1,0:T(8,128)(2,1)S(1)}, u32[]{:S(2)}, u32[]{:S(2)}) collective-permute-start(bf16[128,1536]{1,0:T(8,128)(2,1)S(1)} %dynamic-slice_bitcast_fusion.3), channel_id=1, source_target_pairs={{0,2},{2,0},{1,3},{3,1},{4,6},{6,4},{5,7},{7,5},{8,10},{10,8},{9,1... | collective-permute-start | bytes 1179656 | tf_op jit(solution)/shard_map/ppermute | solution.py:662
  682.6 9.8 %collective-permute-start.7 = (bf16[128,1536]{1,0:T(8,128)(2,1)}, bf16[128,1536]{1,0:T(8,128)(2,1)}, u32[]{:S(2)}, u32[]{:S(2)}) collective-permute-start(bf16[128,1536]{1,0:T(8,128)(2,1)} %dynamic-slice_bitcast_fusion.2), channel_id=1, source_target_pairs={{0,16},{16,0},{1,17},{17,1},{2,18},{18,2},{3,19},{19,3},{4,20},{20... | collective-permute-start | bytes 1179656 | tf_op jit(solution)/shard_map/ppermute | solution.py:662
  692.4 6.5 collective-permute-start.8
  694.4 10.1 %collective-permute-start.9 = (bf16[3,96,512]{2,1,0:T(8,128)(2,1)}, bf16[3,96,512]{2,1,0:T(8,128)(2,1)}, u32[]{:S(2)}, u32[]{:S(2)}) collective-permute-start(bf16[3,96,512]{2,1,0:T(8,128)(2,1)} %get-tuple-element.131), channel_id=1, source_target_pairs={{0,2},{1,3},{2,0},{3,1},{4,6},{5,7},{6,4},{7,5},{8,10},{9,11},{10,... | collective-permute-start | bytes 884744 | tf_op jit(solution)/shard_map/ppermute | solution.py:760
  695.0 15.0 %collective-permute-start.10 = (bf16[3,96,512]{2,1,0:T(8,128)(2,1)}, bf16[3,96,512]{2,1,0:T(8,128)(2,1)}, u32[]{:S(2)}, u32[]{:S(2)}) collective-permute-start(bf16[3,96,512]{2,1,0:T(8,128)(2,1)} %get-tuple-element.130), channel_id=1, source_target_pairs={{0,3},{1,2},{2,1},{3,0},{4,7},{5,6},{6,5},{7,4},{8,11},{9,10},{10,... | collective-permute-start | bytes 884744 | tf_op jit(solution)/shard_map/ppermute | solution.py:760
  697.8 13.5 %collective-permute-start.11 = (bf16[3,96,640]{2,1,0:T(8,128)(2,1)S(1)}, bf16[3,96,640]{2,1,0:T(8,128)(2,1)S(1)}, u32[]{:S(2)}, u32[]{:S(2)}) collective-permute-start(bf16[3,96,640]{2,1,0:T(8,128)(2,1)S(1)} %get-tuple-element.116), channel_id=1, source_target_pairs={{0,1},{1,0},{2,3},{3,2},{4,5},{5,4},{6,7},{7,6},{8,9},{9,8},{10,11... | collective-permute-start | bytes 1105928 | tf_op jit(solution)/shard_map/ppermute | solution.py:760
  698.2 20.4 %collective-permute-start.12 = (bf16[3,96,640]{2,1,0:T(8,128)(2,1)S(1)}, bf16[3,96,640]{2,1,0:T(8,128)(2,1)S(1)}, u32[]{:S(2)}, u32[]{:S(2)}) collective-permute-start(bf16[3,96,640]{2,1,0:T(8,128)(2,1)S(1)} %get-tuple-element.115), channel_id=1, source_target_pairs={{0,2},{1,3},{2,0},{3,1},{4,6},{5,7},{6,4},{7,5},{8,10},{9,11},{10,... | collective-permute-start | bytes 1105928 | tf_op jit(solution)/shard_map/ppermute | solution.py:760
  698.8 26.9 %collective-permute-start.13 = (bf16[3,96,640]{2,1,0:T(8,128)(2,1)S(1)}, bf16[3,96,640]{2,1,0:T(8,128)(2,1)S(1)}, u32[]{:S(2)}, u32[]{:S(2)}) collective-permute-start(bf16[3,96,640]{2,1,0:T(8,128)(2,1)S(1)} %get-tuple-element.114), channel_id=1, source_target_pairs={{0,3},{1,2},{2,1},{3,0},{4,7},{5,6},{6,5},{7,4},{8,11},{9,10},{10,... | collective-permute-start | bytes 1105928 | tf_op jit(solution)/shard_map/ppermute | solution.py:760
  (41 other events, 164.4 us)
Sparse Core Ops, SparseCore 0:
  117.3 113.1 all-gather.4
  232.7 123.5 all-gather.2
  358.6 84.1 reduce-scatter.2
  445.0 112.4 reduce-scatter.4

commit v3 on v2

--- a/solution.py
+++ b/solution.py
@@ -45,9 +45,12 @@
     return tuple(a for a in axes if sizes[a] > 1)
 
 
-def greet(axes, sizes):
+def greet(axes, sizes, diagonal=False):
     barrier = pltpu.get_barrier_semaphore()
     count = 0
+    if diagonal:
+        pl.semaphore_signal(barrier, inc=1, device_id=across(3), device_id_type=MESH)
+        count += 1
     for a in axes:
         me = lax.axis_index(a)
         for d in range(1, sizes[a]):
@@ -61,6 +64,61 @@
     pl.semaphore_wait(barrier, count)
 
 
+def across(d):
+    y, c = lax.axis_index("y"), lax.axis_index("c")
+    return {"y": 1 - y if d & 2 else y, "c": 1 - c if d & 1 else c}
+
+
+class Swap:
+    def __init__(self, x, out, send_sems, recv_sems, local_sem):
+        me = lax.axis_index("y") * 2 + lax.axis_index("c")
+        self.kept = pltpu.make_async_copy(x.at[:, me], out.at[:, me], local_sem)
+        self.copies = []
+        for d in range(1, 4):
+            to = across(d)
+            self.copies.append(
+                pltpu.make_async_remote_copy(
+                    src_ref=x.at[:, to["y"] * 2 + to["c"]],
+                    dst_ref=out.at[:, me],
+                    send_sem=send_sems.at[d - 1],
+                    recv_sem=recv_sems.at[d - 1],
+                    device_id=to,
+                    device_id_type=MESH,
+                )
+            )
+
+    def start(self):
+        for copy in self.copies:
+            copy.start()
+        self.kept.start()
+
+    def wait(self):
+        self.kept.wait()
+        for copy in self.copies:
+            copy.wait()
+
+
+def swap_scratch(swaps):
+    if not swaps:
+        return []
+    return [pltpu.SemaphoreType.DMA((3 * len(swaps),))] * 2 + [
+        pltpu.SemaphoreType.DMA((len(swaps),))
+    ]
+
+
+def swaps_of(xs, outs, sems):
+    return [
+        Swap(
+            x,
+            out,
+            sems[0].at[pl.ds(3 * i, 3)],
+            sems[1].at[pl.ds(3 * i, 3)],
+            sems[2].at[i],
+        )
+        for i, (x, out) in enumerate(zip(xs, outs))
+    ]
+
+
 def place_of(offsets, axes, sizes):
     value = 0
     for a in axes:
@@ -82,12 +140,16 @@
     )
 
 
-def gather_kernel(plans, sizes, *refs):
+def gather_kernel(plans, sizes, swap_count, *refs, ahead=None):
     count = max(p[0] for p in plans) + 1
-    xs, outs = refs[:count], refs[count : 2 * count]
-    send_sems, recv_sems, local_sems = refs[2 * count :]
+    xs, refs = refs[:count], refs[count:]
+    swap_xs, refs = refs[:swap_count], refs[swap_count:]
+    outs, refs = refs[:count], refs[count:]
+    swap_outs, refs = refs[:swap_count], refs[swap_count:]
+    send_sems, recv_sems, local_sems = refs[:3]
+    swaps = swaps_of(swap_xs, swap_outs, refs[3:])
     used = {a: (sizes[a] if any(a in p[3] for p in plans) else 1) for a in AXES}
-    greet(live(AXES, used), sizes)
+    greet(live(AXES, used), sizes, bool(swaps))
 
     def cut(ref, rows):
         return ref if rows is None else ref.at[pl.ds(*rows)]
@@ -132,15 +194,17 @@
                 queue.append((plan, later, p, sem))
                 sem += 1
         if at == len(plans):
-            for copy in kept:
+            if ahead is not None:
+                ahead()
+            for copy in kept + swaps:
                 copy.start()
-    for copy in kept:
+    for copy in kept + swaps:
         copy.wait()
     for copy in sends:
         copy.wait_send()
 
 
-def gather(arrays, plans, sizes, collective_id):
+def gather(arrays, plans, sizes, collective_id, swaps=()):
     plans = [
         (i, rows, live(layout, sizes), live(phases, sizes), split)
         for i, rows, layout, phases, split in plans
@@ -152,22 +216,105 @@
         n, split = next((c, p[4]) for c, p in zip(counts, plans) if p[0] == i)
         shapes.append(jax.ShapeDtypeStruct((n,) + (x.shape[1:] if split else x.shape), x.dtype))
     spec = pl.BlockSpec(memory_space=pltpu.VMEM)
+    far = pl.BlockSpec(memory_space=pl.ANY)
+    specs = [spec] * len(arrays) + [far] * len(swaps)
     moved = sum(int(np.prod(s.shape)) * s.dtype.itemsize for s in shapes)
     return pl.pallas_call(
-        functools.partial(gather_kernel, plans, sizes),
-        out_shape=shapes,
-        in_specs=[spec] * len(arrays),
-        out_specs=[spec] * len(arrays),
+        functools.partial(gather_kernel, plans, sizes, len(swaps)),
+        out_shape=shapes + [jax.ShapeDtypeStruct(x.shape, x.dtype) for x in swaps],
+        in_specs=specs,
+        out_specs=specs,
         scratch_shapes=[
             pltpu.SemaphoreType.DMA((total,)),
             pltpu.SemaphoreType.DMA((total,)),
             pltpu.SemaphoreType.DMA((len(plans),)),
-        ],
+        ]
+        + swap_scratch(swaps),
         compiler_params=pltpu.CompilerParams(
             collective_id=collective_id, has_side_effects=True, vmem_limit_bytes=VMEM_LIMIT
         ),
         cost_estimate=pl.CostEstimate(flops=0, bytes_accessed=20 * moved, transcendentals=0),
-    )(*arrays)
+    )(*arrays, *swaps)
+
+
+def front_kernel(plans, sizes, *refs):
+    q_ref, k_ref, v_ref, o_ref, hidden_ref, small_ref = refs[:6]
+    feeds, refs = refs[6:9], refs[9:]
+    outs, swapped, second_ref, refs = refs[:4], refs[4], refs[5], refs[6:]
+    halves_s, o_s, first_s = refs[:3]
+    heads = halves_s.shape[0]
+    q_cols, kv_cols = q_ref.shape[1] // heads, k_ref.shape[1] // heads
+    for i in range(heads):
+        halves_s[i, :, :q_cols] = q_ref[:, i * q_cols : (i + 1) * q_cols].astype(BF)
+        cols = slice(i * kv_cols, (i + 1) * kv_cols)
+        halves_s[i, :, q_cols : q_cols + kv_cols] = k_ref[:, cols].astype(BF)
+        halves_s[i, :, q_cols + kv_cols :] = v_ref[:, cols].astype(BF)
+    o_s[...] = o_ref[...].astype(BF)
+
+    def pack():
+        first, second = first_s.shape[-1], second_ref.shape[-1]
+        for m, feed_ref in enumerate(feeds):
+            rows, width = feed_ref.shape
+            for i in range(first_s.shape[1]):
+                low = i * (first + second)
+                for ref, n in ((first_s, first), (second_ref, second)):
+                    real = min(n, width - low)
+                    ref[m, i, :, :real] = feed_ref[:, low : low + real].astype(BF)
+                    if real < n:
+                        ref[m, i, :, real:] = jnp.zeros((rows, n - real), BF)
+                    low += n
+
+    gather_kernel(
+        plans,
+        sizes,
+        1,
+        halves_s,
+        hidden_ref,
+        small_ref,
+        o_s,
+        first_s,
+        *outs,
+        swapped,
+        *refs[3:],
+        ahead=pack,
+    )
+
+
+def front(weights, hidden, small, feeds, first, second, plans, sizes, collective_id):
+    plans = alive(plans, sizes)
+    heads, rows = sizes["head"], weights[0].shape[0]
+    halves = jax.ShapeDtypeStruct((heads, rows, sum(w.shape[1] for w in weights[:3]) // heads), BF)
+    out = jax.ShapeDtypeStruct(weights[3].shape, BF)
+    arrays = [halves, hidden, small, out]
+    counts = [int(np.prod([sizes[a] for a in p[2]])) for p in plans]
+    total = sum(counts) - len(counts)
+    shapes = [
+        jax.ShapeDtypeStruct((n,) + (x.shape[1:] if p[4] else x.shape), x.dtype)
+        for n, x, p in zip(counts, arrays, plans)
+    ]
+    ff_rows = feeds[0].shape[0]
+    blocks = [jax.ShapeDtypeStruct((3, 4, ff_rows, n), BF) for n in (first, second)]
+    spec = pl.BlockSpec(memory_space=pltpu.VMEM)
+    far = pl.BlockSpec(memory_space=pl.ANY)
+    return pl.pallas_call(
+        functools.partial(front_kernel, plans, sizes),
+        out_shape=shapes + blocks,
+        in_specs=[spec] * 9,
+        out_specs=[spec] * 4 + [far, spec],
+        scratch_shapes=[
+            pltpu.VMEM(halves.shape, BF),
+            pltpu.VMEM(out.shape, BF),
+            pltpu.VMEM(blocks[0].shape, BF),
+            pltpu.SemaphoreType.DMA((total,)),
+            pltpu.SemaphoreType.DMA((total,)),
+            pltpu.SemaphoreType.DMA((len(plans),)),
+        ]
+        + swap_scratch(blocks[:1]),
+        compiler_params=pltpu.CompilerParams(
+            collective_id=collective_id, has_side_effects=True, vmem_limit_bytes=VMEM_LIMIT
+        ),
+        cost_estimate=pl.CostEstimate(flops=0, bytes_accessed=100 * 2**20, transcendentals=0),
+    )(*weights, hidden, small, *feeds)
 
 
 def offset_keys(axes, sizes):
@@ -177,7 +324,7 @@
     return keys
 
 
-def scatter_kernel(plans, sizes, *refs, between=None):
+def scatter_kernel(plans, sizes, *refs, between=None, swaps=(), delays=None):
     count = max(p[0] for p in plans) + 1
     xs, outs = refs[:count], refs[count : 2 * count]
     at = 2 * count
@@ -191,7 +338,7 @@
         a: (sizes[a] if any(a in p[3] or (p[4] and a == "head") for p in plans) else 1)
         for a in AXES
     }
-    greet(live(AXES, used), sizes)
+    greet(live(AXES, used), sizes, bool(swaps))
     sem = 0
     sends = []
     arrivals = [dict() for _ in plans]
@@ -219,10 +366,12 @@
                 total = total + buf[...].astype(F32)
         return total
 
-    depth = max(len(p[3]) for p in plans)
-    for phase in range(depth):
+    delays = delays or [0] * len(plans)
+    depth = max(len(p[3]) + delay for p, delay in zip(plans, delays))
+    for step in range(depth):
         for j, (i, rows, layout, phases, swap) in enumerate(plans):
-            if phase >= len(phases):
+            phase = step - delays[j]
+            if phase < 0 or phase >= len(phases):
                 continue
             a, rest = phases[phase], phases[phase + 1 :]
             for d in range(1, sizes[a]):
@@ -241,9 +390,12 @@
                     sends.append(copy)
                     arrivals[j][(phase, d, where)] = sem
                     sem += 1
+        if step == min(2, depth - 1):
+            for item in swaps:
+                item.start()
         if between is not None:
-            between(phase)
-    swaps = []
+            between(step)
+    late = []
     for j, (i, rows, layout, phases, swap) in enumerate(plans):
         total = total_of(j, {}, len(phases))
         if swap:
@@ -252,7 +404,7 @@
             me = lax.axis_index("head")
             copy = pltpu.make_async_copy(hold.at[me], out.at[me], local_sems.at[j])
             copy.start()
-            swaps.append((copy, None))
+            late.append((copy, None))
             for d in range(1, sizes["head"]):
                 to = lax.rem(me + d, sizes["head"])
                 copy = remote(
@@ -260,17 +412,19 @@
                 )
                 copy.start()
                 sends.append(copy)
-                swaps.append((out.at[lax.rem(me + sizes["head"] - d, sizes["head"])], sem))
+                late.append((out.at[lax.rem(me + sizes["head"] - d, sizes["head"])], sem))
                 sem += 1
         elif rows is None:
             outs[i][...] = total.astype(outs[i].dtype)
         else:
             outs[i][pl.ds(*rows)] = total.astype(outs[i].dtype)
-    for item, s in swaps:
+    for item, s in late:
         if s is None:
             item.wait()
         else:
             remote(item, item, send_sems.at[s], recv_sems.at[s], "head", 0, sizes).wait_recv()
+    for item in swaps:
+        item.wait()
     for copy in sends:
         copy.wait_send()
 
@@ -307,27 +461,83 @@
     ]
 
 
-def scatter(arrays, plans, out_types, sizes, collective_id):
+def scatter_and_swap_kernel(plans, sizes, arrays, carried, swap_count, delays, *refs):
+    xs, refs = refs[:arrays], refs[arrays:]
+    swap_xs, refs = refs[:swap_count], refs[swap_count + carried :]
+    outs, refs = refs[:arrays], refs[arrays:]
+    swap_outs, refs = refs[:swap_count], refs[swap_count + carried :]
+    held = 3 if swap_count else 0
+    swaps = swaps_of(swap_xs, swap_outs, refs[len(refs) - held :])
+    rest = refs[: len(refs) - held]
+    scatter_kernel(plans, sizes, *xs, *outs, *rest, swaps=swaps, delays=delays)
+
+
+def scatter(arrays, plans, out_types, sizes, collective_id, swaps=(), carried=(), delays=None):
     plans = alive(plans, sizes)
     shapes = [jax.ShapeDtypeStruct(x.shape[1:], kind) for x, kind in zip(arrays, out_types)]
     spec = pl.BlockSpec(memory_space=pltpu.VMEM)
+    far = pl.BlockSpec(memory_space=pl.ANY)
+    specs = [spec] * len(arrays) + [far] * (len(swaps) + len(carried))
     moved = sum(int(np.prod(x.shape)) * x.dtype.itemsize for x in arrays)
     return pl.pallas_call(
-        functools.partial(scatter_kernel, plans, sizes),
-        out_shape=shapes,
-        in_specs=[spec] * len(arrays),
-        out_specs=[spec] * len(arrays),
-        scratch_shapes=scatter_scratch(arrays, plans, out_types, sizes),
+        functools.partial(
+            scatter_and_swap_kernel, plans, sizes, len(arrays), len(carried), len(swaps), delays
+        ),
+        out_shape=shapes + [jax.ShapeDtypeStruct(x.shape, x.dtype) for x in (*swaps, *carried)],
+        in_specs=specs,
+        out_specs=specs,
+        input_output_aliases={
+            len(arrays) + len(swaps) + i: len(arrays) + len(swaps) + i for i in range(len(carried))
+        },
+        scratch_shapes=scatter_scratch(arrays, plans, out_types, sizes) + swap_scratch(swaps),
         compiler_params=pltpu.CompilerParams(
             collective_id=collective_id, has_side_effects=True, vmem_limit_bytes=VMEM_LIMIT
         ),
         cost_estimate=pl.CostEstimate(flops=0, bytes_accessed=20 * moved, transcendentals=0),
-    )(*arrays)
-
-
-def feed_kernel(chunks, t_ref, c_ref, w_ref, *refs):
+    )(*arrays, *swaps, *carried)
+
+
+def finish_kernel(count, *refs):
+    xs, refs = refs[:count], refs[count + 1 :]
+    outs, got, sems = refs[:3], refs[3 : 3 + count], refs[3 + count :]
+    items = swaps_of(xs, got, sems)
+    greet(("y", "c"), {"y": 2, "c": 2}, True)
+    for item in items:
+        item.start()
+    width = outs[0].shape[1]
+    lanes = sum(x.shape[-1] for x in xs)
+    start = 0
+    for item, part in zip(items, got):
+        item.wait()
+        n = part.shape[-1]
+        for m, out in enumerate(outs):
+            for i in range(part.shape[1]):
+                low = i * lanes + start
+                high = min(low + n, width)
+                if high > low:
+                    out[:, low:high] = part[m, i, :, : high - low].astype(F32)
+        start += n
+
+
+def finish(xs, width, last, collective_id):
+    far = pl.BlockSpec(memory_space=pl.ANY)
+    spec = pl.BlockSpec(memory_space=pltpu.VMEM)
+    n = len(xs)
+    return pl.pallas_call(
+        functools.partial(finish_kernel, n),
+        out_shape=[jax.ShapeDtypeStruct((xs[0].shape[2], width), F32)] * 3,
+        in_specs=[far] * (n + 1),
+        out_specs=[spec] * 3,
+        scratch_shapes=[pltpu.VMEM(x.shape, x.dtype) for x in xs] + swap_scratch(xs),
+        compiler_params=pltpu.CompilerParams(
+            collective_id=collective_id, has_side_effects=True, vmem_limit_bytes=VMEM_LIMIT
+        ),
+    )(*xs, last)
+
+
+def feed_kernel(chunks, added, t_ref, c_ref, w_ref, *refs):
     act_ref, dgate_ref, dup_ref, branch_ref, dtok_ref = refs[-5:]
-    before = refs[:-5]
+    before = refs[:added]
     tokens, cot = t_ref[...], c_ref[...]
     places, _, rows, width = w_ref.shape
     per = max(1, LANES * 3 // rows)
@@ -365,22 +575,24 @@
         branch_ref[:, cols] = branch.astype(BF)
 
 
-def feed(tokens, cot, weights, *before):
+def feed(tokens, cot, weights, before=(), after=()):
     n, width, tile = tokens.shape[0], weights.shape[-1], 256
     chunks = [(i, min(256, width - i)) for i in range(0, width, 256)]
     wide = pl.BlockSpec((tile, D), lambda i: (i, 0))
     inner = pl.BlockSpec((tile, width), lambda i: (i, 0))
     return pl.pallas_call(
-        functools.partial(feed_kernel, chunks),
+        functools.partial(feed_kernel, chunks, len(before)),
         grid=(n // tile,),
-        in_specs=[wide, wide, pl.BlockSpec(memory_space=pltpu.VMEM)] + [wide] * len(before),
+        in_specs=[wide, wide, pl.BlockSpec(memory_space=pltpu.VMEM)]
+        + [wide] * len(before)
+        + [pl.BlockSpec(memory_space=pl.ANY)] * len(after),
         out_specs=[inner, inner, inner, wide, wide],
         out_shape=[jax.ShapeDtypeStruct((n, k), BF) for k in (width, width, width, D, D)],
         compiler_params=pltpu.CompilerParams(vmem_limit_bytes=VMEM_LIMIT),
         cost_estimate=pl.CostEstimate(
             flops=12 * n * D * width, bytes_accessed=40 * 2**20, transcendentals=n * width
         ),
-    )(tokens, cot, weights, *before)
+    )(tokens, cot, weights, *before, *after)
 
 
 def plain_grads_kernel(t_ref, c_ref, act_ref, dgate_ref, dup_ref, grad_ref):
@@ -572,7 +784,19 @@
 
 
 def backward_kernel(
-    heads, slots, tops, q_ref, kv_ref, do_ref, lse_ref, delta_ref, dq_ref, dkv_ref, dq_s, dkv_s
+    heads,
+    slots,
+    tops,
+    q_ref,
+    kv_ref,
+    do_ref,
+    lse_ref,
+    o_ref,
+    dq_ref,
+    dkv_ref,
+    dq_s,
+    dkv_s,
+    delta_s,
 ):
     dkv_s[...] = jnp.zeros(dkv_s.shape, F32)
     for a in range(2):
@@ -580,6 +804,10 @@
 
         def part(ref, h):
             return ref[a * BLOCK : (a + 1) * BLOCK, h * HEAD_DIM : (h + 1) * HEAD_DIM]
+
+        for h in range(heads):
+            product = part(do_ref, h).astype(F32) * part(o_ref, h)
+            delta_s[h : h + 1, :] = jnp.sum(product.T, axis=0, keepdims=True)
 
         def one(n, carry):
             slot = slots[n]
@@ -599,7 +827,7 @@
                     ready.append(products(h + ahead))
                 p = jnp.exp2(s * SCALE2 - lse_ref[a, h : h + 1, :])
                 dv = dv + dot_nn(p.astype(BF), part(do_ref, h))
-                ds = (p * (dp - delta_ref[a, h : h + 1, :])).astype(BF)
+                ds = (p * (dp - delta_s[h : h + 1, :])).astype(BF)
                 dk = dk + dot_nn(ds, part(q_ref, h))
                 dq_s[h] = dq_s[h] + dot_nn(keys_t, ds)
             dkv_s[slot, :, :HEAD_DIM] = dkv_s[slot, :, :HEAD_DIM] + dk
@@ -615,7 +843,7 @@
     dkv_ref[:, :, HEAD_DIM:] = dkv_s[:, :, HEAD_DIM:].astype(BF)
 
 
-def attend_back(slots, tops, q, kv, do, lse, delta):
+def attend_back(slots, tops, q, kv, do, lse, attended):
     heads = q.shape[1] // HEAD_DIM
     spec = pl.BlockSpec(memory_space=pltpu.VMEM)
     pairs = 33 * BLOCK * BLOCK * heads
@@ -629,6 +857,7 @@
             scratch_shapes=[
                 pltpu.VMEM((heads, HEAD_DIM, BLOCK), F32),
                 pltpu.VMEM(kv.shape, F32),
+                pltpu.VMEM((8, BLOCK), F32),
             ],
         ),
         out_shape=(
@@ -639,27 +868,180 @@
         cost_estimate=pl.CostEstimate(
             flops=pairs * 10 * HEAD_DIM, bytes_accessed=120 * 2**20, transcendentals=pairs
         ),
-    )(slots, tops, q, kv, do, lse, delta)
+    )(slots, tops, q, kv, do, lse, attended)
 
 
 def inverse_rms(value):
     return lax.rsqrt(jnp.mean(value * value, axis=-1, keepdims=True) + EPS)
 
 
-def rotate(value, cosine, sine):
-    rows, width = value.shape
-    half = HEAD_DIM // 2
-    parts = value.reshape(rows, width // HEAD_DIM, HEAD_DIM)
-    first, second = parts[..., :half], parts[..., half:]
-    cosine, sine = cosine[:, None, :], sine[:, None, :]
-    return jnp.concatenate(
-        [first * cosine - second * sine, second * cosine + first * sine], axis=-1
-    ).reshape(rows, width)
-
-
-def shift(value, axis, distance, sizes):
-    n = sizes[axis]
-    return lax.ppermute(value, axis, [(i, (i + distance) % n) for i in range(n)])
+def turned(value, cosine, sine):
+    return value * cosine + pltpu.roll(value, HEAD_DIM // 2, 1) * sine
+
+
+def project_kernel(x_ref, w_ref, gain_ref, bias_ref, cos_ref, sin_ref, q_ref, kv_ref, normed_ref):
+    x = x_ref[...].astype(F32)
+    normed_ref[...] = (x * inverse_rms(x) * gain_ref[...]).astype(BF)
+    cosine, sine = cos_ref[...], sin_ref[...]
+    heads = q_ref.shape[1] // HEAD_DIM
+
+    def product(low, n):
+        cols = slice(low * HEAD_DIM, (low + n) * HEAD_DIM)
+        return dot_nn(normed_ref[...], w_ref[:, cols]) + bias_ref[:, cols]
+
+    for low in range(0, heads, 2):
+        made = product(low, 2)
+        for i in range(2):
+            part = made[:, i * HEAD_DIM : (i + 1) * HEAD_DIM]
+            q_ref[:, (low + i) * HEAD_DIM : (low + i + 1) * HEAD_DIM] = turned(
+                part, cosine, sine
+            ).astype(BF)
+    made = product(heads, 2)
+    kv_ref[:, :HEAD_DIM] = turned(made[:, :HEAD_DIM], cosine, sine).astype(BF)
+    kv_ref[:, HEAD_DIM:] = made[:, HEAD_DIM:].astype(BF)
+
+
+def project(x, w, gain, bias, cosine, sine):
+    n, width = x.shape[0], w.shape[1]
+    spec = pl.BlockSpec(memory_space=pltpu.VMEM)
+    return pl.pallas_call(
+        project_kernel,
+        in_specs=[spec] * 6,
+        out_specs=[spec] * 3,
+        out_shape=[
+            jax.ShapeDtypeStruct((n, k), BF)
+            for k in (width - 2 * HEAD_DIM, 2 * HEAD_DIM, D)
+        ],
+        compiler_params=pltpu.CompilerParams(vmem_limit_bytes=VMEM_LIMIT),
+        cost_estimate=pl.CostEstimate(
+            flops=2 * n * D * width, bytes_accessed=12 * 2**20, transcendentals=0
+        ),
+    )(x, w, gain, bias, cosine, sine)
+
+
+def project_back_kernel(
+    dq_ref,
+    dkv_ref,
+    normed_ref,
+    x_ref,
+    w_ref,
+    cos_ref,
+    sin_ref,
+    grad_ref,
+    dnormed_ref,
+    gain_grad_ref,
+    bias_grad_ref,
+    dpre_s,
+):
+    cosine, sine = cos_ref[...], -sin_ref[...]
+    heads = dq_ref.shape[1] // HEAD_DIM
+    for h in range(heads + 1):
+        cols = slice(h * HEAD_DIM, (h + 1) * HEAD_DIM)
+        part = dq_ref[:, cols] if h < heads else dkv_ref[:, :HEAD_DIM]
+        dpre_s[:, cols] = turned(part.astype(F32), cosine, sine).astype(BF)
+    dpre_s[:, (heads + 1) * HEAD_DIM :] = dkv_ref[:, HEAD_DIM:]
+    bias_grad_ref[...] = jnp.sum(dpre_s[...].astype(F32), axis=0, keepdims=True)
+    x = x_ref[...].astype(F32)
+    scale = inverse_rms(x)
+    step = 2 * HEAD_DIM
+    for low in range(0, D, step):
+        cols = slice(low, low + step)
+        dnormed = dot_nt(dpre_s[...], w_ref[cols, :])
+        dnormed_ref[:, cols] = dnormed.astype(BF)
+        gain_grad_ref[:, cols] = jnp.sum(
+            dnormed * (x[:, cols] * scale), axis=0, keepdims=True
+        )
+        if len(grad_ref.shape) == 2:
+            grad_ref[cols, :] = dot_tn(normed_ref[:, cols], dpre_s[...]).astype(BF)
+    if len(grad_ref.shape) == 4:
+        blk, heads, rows, width = grad_ref.shape
+        step = 3 * LANES
+        for low in range(0, D, step):
+            made = dot_tn(normed_ref[:, low : low + step], dpre_s[...]).astype(BF)
+            half, start = divmod(low // rows, blk)
+            grad_ref[start : start + step // rows, half] = made.reshape(step // rows, rows, width)
+
+
+def project_back(dq, dkv, normed, x, w, cosine, sine, blk, rows):
+    n, width = x.shape[0], w.shape[1]
+    split = rows % 16 == 0
+    made = (blk, 2, rows, width) if split else (D, width)
+    spec = pl.BlockSpec(memory_space=pltpu.VMEM)
+    return pl.pallas_call(
+        project_back_kernel,
+        in_specs=[spec] * 7,
+        out_specs=[spec] * 4,
+        out_shape=[
+            jax.ShapeDtypeStruct(made, BF),
+            jax.ShapeDtypeStruct((n, D), BF),
+            jax.ShapeDtypeStruct((1, D), F32),
+            jax.ShapeDtypeStruct((1, width), F32),
+        ],
+        scratch_shapes=[pltpu.VMEM((n, width), BF)],
+        compiler_params=pltpu.CompilerParams(vmem_limit_bytes=VMEM_LIMIT),
+        cost_estimate=pl.CostEstimate(
+            flops=4 * n * D * width, bytes_accessed=16 * 2**20, transcendentals=0
+        ),
+    )(dq, dkv, normed, x, w, cosine, sine)
+
+
+def last_kernel(plans, sizes, delays, *refs):
+    xs, refs = refs[:4], refs[4:]
+    dmixed_ref, x_ref, mixed_ref, gain_ref, _ = refs[:5]
+    q_ref, k_ref, v_ref, small_ref, out_ref, hidden_ref = refs[5:11]
+    w_s, dnormed_s, branch_s = refs[11:14]
+    outs = (w_s, small_ref, dnormed_s, branch_s)
+    scatter_kernel(plans, sizes, *xs, *outs, *refs[14:], delays=delays)
+    heads = w_s.shape[0]
+    q_cols = q_ref.shape[1] // heads
+    for i in range(heads):
+        cols = slice(i * HEAD_DIM, (i + 1) * HEAD_DIM)
+        q_ref[:, i * q_cols : (i + 1) * q_cols] = w_s[i, :, :q_cols]
+        k_ref[:, cols] = w_s[i, :, q_cols : q_cols + HEAD_DIM]
+        v_ref[:, cols] = w_s[i, :, q_cols + HEAD_DIM :]
+    out_ref[...] = (mixed_ref[...] + branch_s[...]).astype(BF)
+    x = x_ref[...].astype(F32)
+    scale = inverse_rms(x)
+    z = x * scale
+    u = gain_ref[...] * dnormed_s[...]
+    hidden_ref[...] = (
+        dmixed_ref[...] + scale * (u - z * jnp.mean(z * u, axis=-1, keepdims=True))
+    ).astype(BF)
+
+
+def last_sums(arrays, plans, delays, dmixed, x, mixed, gain, after, sizes, collective_id):
+    plans = alive(plans, sizes)
+    kinds = [F32] * 4
+    spec = pl.BlockSpec(memory_space=pltpu.VMEM)
+    heads, rows, width = arrays[0].shape[1:]
+    q_cols = heads * (width - 2 * HEAD_DIM)
+    tok = x.shape[0]
+    shapes = [
+        ((rows, q_cols), F32),
+        ((rows, heads * HEAD_DIM), F32),
+        ((rows, heads * HEAD_DIM), F32),
+        (arrays[1].shape[1:], F32),
+        ((tok, D), BF),
+        ((tok, D), BF),
+    ]
+    return pl.pallas_call(
+        functools.partial(last_kernel, plans, sizes, delays),
+        out_shape=[jax.ShapeDtypeStruct(*s) for s in shapes],
+        in_specs=[spec] * 8 + [pl.BlockSpec(memory_space=pl.ANY)],
+        out_specs=[spec] * 6,
+        scratch_shapes=[
+            pltpu.VMEM((heads, rows, width), F32),
+            pltpu.VMEM((tok, D), F32),
+            pltpu.VMEM((tok, D), F32),
+        ]
+        + scatter_scratch(arrays, plans, kinds, sizes),
+        compiler_params=pltpu.CompilerParams(
+            collective_id=collective_id, has_side_effects=True, vmem_limit_bytes=VMEM_LIMIT
+        ),
+        cost_estimate=pl.CostEstimate(
+            flops=0, bytes_accessed=200 * 2**20, transcendentals=0
+        ),
+    )(*arrays, dmixed, x, mixed, gain, after)
 
 
 def small_rows(*rows):
@@ -703,38 +1085,45 @@
     frequency = THETA ** (-(jnp.arange(HEAD_DIM // 2, dtype=F32) * 2.0) / HEAD_DIM)
     angles = positions.astype(F32)[:, None] * frequency[None, :]
     cosine, sine = jnp.cos(angles), jnp.sin(angles)
+    cosine = jnp.concatenate([cosine, cosine], axis=1)
+    sine = jnp.concatenate([-sine, sine], axis=1)
 
     q_cols = D // 2
     kv_cols = HEAD_DIM
     rows = q_weight.shape[0]
-    halves = [
-        jnp.concatenate(
-            [
-                q_weight[:, i * q_cols : (i + 1) * q_cols],
-                k_weight[:, i * kv_cols : (i + 1) * kv_cols],
-                v_weight[:, i * kv_cols : (i + 1) * kv_cols],
-            ],
-            axis=1,
-        ).astype(BF)
-        for i in range(2)
-    ]
     small = small_rows(
         *[v.astype(BF) for v in (norm1, norm2, q_bias, k_bias, v_bias)]
     )
-    w_qkv, x_pair, small_all, w_out = gather(
-        [jnp.stack(halves), hidden, small, o_weight.astype(BF)],
+    parts = sizes["y"] * sizes["c"]
+    width = gate_weight.shape[1]
+    lanes = -(-width // (LANES * parts)) * LANES
+    first = lanes * 6 // 9 // LANES * LANES
+    ff_rows = gate_weight.shape[0]
+
+    def along_z(part):
+        part = part.reshape(1, 3, parts * ff_rows, part.shape[-1])
+        return lax.all_gather(part, live(("g", "z"), sizes), axis=0, tiled=True)
+
+    w_qkv, x_pair, small_all, w_out, mine_one, packed_two = front(
+        (q_weight, k_weight, v_weight, o_weight),
+        hidden,
+        small,
+        (down_weight, gate_weight, up_weight),
+        first,
+        lanes - first,
         [
             (0, None, AXES, AXES, True),
             (1, None, ("head",), ("head",), False),
             (2, None, AXES, AXES, False),
-            (3, None, BLK, BLK, False),
+            (3, None, BLK, ("y", "z", "g", "c"), False),
         ],
         sizes,
         1,
     )
+    w_feed_one = along_z(mine_one)
     w_out = w_out.reshape(q_cols, D)
     w_qkv = w_qkv.reshape(D, q_cols + 2 * kv_cols)
-    x_pair = x_pair.reshape(pair, D).astype(F32)
+    x_pair = x_pair.reshape(pair, D)
     gain_one = small_all[:, 0, :rows].reshape(D)
     gain_two = small_all[:, 1, :rows].reshape(D)
     bias_q = lax.dynamic_slice_in_dim(small_all[:, 2, :rows].reshape(D), head * q_cols, q_cols)
@@ -745,84 +1134,49 @@
         for i in (3, 4)
     )
 
-    near = ("y", "c")
-    parts = sizes["y"] * sizes["c"]
-    width = gate_weight.shape[1]
-    lanes = -(-width // (LANES * parts)) * LANES
-    wide = lanes * parts
-    corner = place_of({}, near, sizes)
-    ff_rows = gate_weight.shape[0]
-
-    def corner_send(blocks):
-        got = [lax.dynamic_index_in_dim(blocks, corner, 0, keepdims=False)]
-        for d in range(1, parts):
-            piece = lax.dynamic_index_in_dim(blocks, corner ^ d, 0, keepdims=False)
-            got.append(lax.ppermute(piece, near, [(i, i ^ d) for i in range(parts)]))
-        return got
-
-    def corner_sort(got):
-        held = jnp.stack(got)
-        return [lax.dynamic_index_in_dim(held, corner ^ i, 0, keepdims=False) for i in range(parts)]
-
-    def quarters(weight):
-        padded = jnp.pad(weight.astype(BF), ((0, 0), (0, wide - width)))
-        return padded.reshape(ff_rows, parts, lanes).transpose(1, 0, 2)
-
-    packed = jnp.stack([quarters(w) for w in (down_weight, gate_weight, up_weight)], axis=1)
-    mine = jnp.stack(corner_sort(corner_send(packed)), axis=1)
-    mine = mine.reshape(1, 3, parts * ff_rows, lanes)
-    first = lanes * 4 // 9 // LANES * LANES
-
-    def along_z(part, zero):
-        part = (part.astype(F32) + zero).astype(BF)
-        return lax.all_gather(part, live(("g", "z"), sizes), axis=0, tiled=True)
-
-    w_feed_one = along_z(mine[..., :first], small_all[0, 7, 0])
-
-    def halved(value, axis, dim, kind=BF):
-        me = lax.axis_index(axis)
-        away = lax.dynamic_index_in_dim(value, 1 - me, dim, keepdims=False)
-        keep = lax.dynamic_index_in_dim(value, me, dim, keepdims=False)
-        return (keep.astype(F32) + shift(away, axis, 1, sizes).astype(F32)).astype(kind)
-
-    def group_sum(value, kind):
-        near_sum = halved(value.reshape(2, 2, 2, tok, D), "c", 2)
-        one = halved(near_sum[:, :, :half], "head", 0)
-        two = halved(near_sum[:, :, half:], "y", 1)
-        return jnp.concatenate([halved(one, "y", 0, kind), halved(two, "head", 0, kind)])
-
-    scale_one = inverse_rms(x_pair)
-    normed = (x_pair * scale_one * gain_one).astype(BF)
-    qkv = dot_nn(normed, w_qkv)
-    queries = rotate(qkv[:, :q_cols] + bias_q, cosine, sine).astype(BF)
-    keys = rotate(qkv[:, q_cols : q_cols + kv_cols] + bias_k, cosine, sine).astype(BF)
-    values = (qkv[:, q_cols + kv_cols :] + bias_v).astype(BF)
+    queries, kv_local, normed = project(
+        x_pair,
+        w_qkv,
+        gain_one[None],
+        jnp.concatenate([bias_q, bias_k, bias_v])[None],
+        cosine,
+        sine,
+    )
     group = ("head", "y", "c")
     half = tok // 2
     crossed = [
         ((0, half), group, ("head", "y", "c"), False),
         ((half, half), group, ("y", "head", "c"), False),
     ]
-    kv, cot_all = gather(
-        [jnp.concatenate([keys, values], axis=1), cotangent],
+    summed = [
+        ((0, half), group, ("c", "head", "y"), False),
+        ((half, half), group, ("c", "y", "head"), False),
+    ]
+    kv, cot_all, mine_two = gather(
+        [kv_local, cotangent],
         [
             (0, None, place_axes, place_axes, False),
             (1, None, group, ("y", "head", "c"), False),
         ],
         sizes,
         2,
+        [packed_two],
     )
     cot_all = cot_all.reshape(-1, D)
     kv = kv.reshape(2 * SEQ_SPAN, tok, 2 * HEAD_DIM)
     attended, lse = attend(slots, tops, queries, kv)
-    w_feed_two = along_z(mine[..., first:], lse[0, 7, 0])
+    w_feed_two = along_z((mine_two.astype(F32) + lse[0, 7, 0]).astype(BF))
     attn_local = attended.astype(BF)
-    inputs = lax.dynamic_slice_in_dim(x_pair, head * tok, tok)
-    mixed_part = dot_nn(attn_local, w_out).astype(BF).reshape(2, tok, D)
-    (mixed_sum,) = scatter(
-        [mixed_part], [(0, None, ("head",), ("head",), False)], [F32], sizes, 3
-    )
-    mixed = inputs + mixed_sum
+    inputs = hidden.astype(F32)
+    mixed_part = dot_nn(attn_local, w_out).reshape(2, tok, D)
+    (mixed_got,) = gather(
+        [mixed_part.astype(BF)], [(0, None, ("head",), ("head",), True)], sizes, 3
+    )
+    mixed = (
+        inputs
+        + lax.dynamic_index_in_dim(mixed_part, head, 0, keepdims=False)
+        + lax.dynamic_index_in_dim(mixed_got, 1 - head, 0, keepdims=False).astype(F32)
+    )
     scale_two = inverse_rms(mixed)
     normed_two = (mixed * scale_two * gain_two).astype(BF)
     (tokens,) = gather([normed_two], [(0,) + c for c in crossed], sizes, 4)
@@ -831,7 +1185,9 @@
     places = w_feed_one.shape[0]
     act, dgate, dup, branch, dtokens = feed(tokens, cot_all, w_feed_one)
     parts_one = plain_grads(tokens, cot_all, act, dgate, dup, places)
-    act, dgate, dup, branch, dtokens = feed(tokens, cot_all, w_feed_two, branch, dtokens)
+    act, dgate, dup, branch, dtokens = feed(
+        tokens, cot_all, w_feed_two, (branch, dtokens), (parts_one,)
+    )
     dnormed_two, parts_two = feed_grads(
         dtokens.reshape(-1, tok, D),
         tokens,
@@ -840,28 +1196,15 @@
         dgate,
         dup,
         places,
-        [
-            (0, (0, half), group, ("c", "head", "y"), False),
-            (0, (half, half), group, ("c", "y", "head"), False),
-        ],
+        [(0,) + c for c in summed],
         sizes,
         5,
     )
-    branch_sum = group_sum(branch, F32)
-    output = (mixed + branch_sum).astype(BF)
-
     def collect(grad):
         total = lax.psum_scatter(grad, live(("g", "z"), sizes), scatter_dimension=0, tiled=True)
-        total = total.reshape(3, parts, ff_rows, grad.shape[-1])
-        return corner_sort(corner_send(total.transpose(1, 0, 2, 3)))
-
-    back = list(zip(collect(parts_one), collect(parts_two)))
-    d_down, d_gate, d_up = (
-        jnp.concatenate([half[m] for pair_ in back for half in pair_], axis=1)[:, :width].astype(
-            F32
-        )
-        for m in range(3)
-    )
+        return total.reshape(3, parts, ff_rows, grad.shape[-1])
+
+    back_one = collect(parts_one)
 
     z_two = mixed * scale_two
     u_two = gain_two * dnormed_two
@@ -873,29 +1216,28 @@
     (dproj_pair,) = gather([dproj], [(0, None, ("head",), ("head",), False)], sizes, 6)
     dproj_pair = dproj_pair.reshape(pair, D)
     dout = dot_nt(dproj_pair, w_out).astype(BF)
-    delta = jnp.sum(
-        (dout.astype(F32) * attended).reshape(2, tok, q_cols // HEAD_DIM, HEAD_DIM), axis=-1
-    ).transpose(0, 2, 1)
-    delta = jnp.pad(delta, ((0, 0), (0, 8 - delta.shape[1]), (0, 0)))
-
     o_part = dot_tn(attn_local, dproj_pair).astype(BF)
 
-    dq, dkv_parts = attend_back(slots, tops, queries, kv, dout, lse, delta)
-    (dkv,) = scatter(
-        [dkv_parts.reshape(SEQ_SPAN, pair, 2 * HEAD_DIM)],
-        [(0, None, place_axes, place_axes[::-1], False)],
-        [BF],
+    dq, dkv_parts = attend_back(slots, tops, queries, kv, dout, lse, attended)
+    dkv, d_out_weight, parts_two = scatter(
+        [dkv_parts.reshape(SEQ_SPAN, pair, 2 * HEAD_DIM), o_part.reshape(blk, -1, D)],
+        [
+            (0, None, place_axes, place_axes[::-1], False),
+            (1, None, BLK, BLK[::-1], False),
+        ],
+        [BF, F32],
         sizes,
         7,
-    )
-    dq_pre = rotate(dq.astype(F32), cosine, -sine).astype(BF)
-    dk_pre = rotate(dkv[:, :HEAD_DIM].astype(F32), cosine, -sine).astype(BF)
-    dv = dkv[:, HEAD_DIM:]
-    dpre = jnp.concatenate([dq_pre, dk_pre, dv], axis=1)
-    w_part = dot_tn(normed, dpre).astype(BF)
-    bias_part = jnp.sum(dpre.astype(F32), axis=0)
-    dnormed = dot_nt(dpre, w_qkv)
-    norm1_part = jnp.sum(dnormed * (x_pair * scale_one), axis=0)
+        [],
+        [parts_two],
+    )
+    back_two = collect(parts_two)
+    w_part, dnormed, norm1_part, bias_part = project_back(
+        dq, dkv, normed, x_pair, w_qkv, cosine, sine, blk, rows
+    )
+    if w_part.ndim == 2:
+        w_part = w_part.reshape(2, blk, rows, -1).transpose(1, 0, 2, 3)
+    norm1_part, bias_part = norm1_part[0], bias_part[0]
     own = (jnp.arange(2) == head).astype(F32)[:, None]
 
     def owners(vector):
@@ -919,39 +1261,39 @@
         axis=2,
     )
     small_grads = small_grads.transpose(1, 0, 2, 3).reshape(2 * blk, 8, LANES)
-    w_grads, small_sum, dnormed_sum, d_out_weight = scatter(
+    d_query, d_key, d_value, small_sum, output, hidden_grad = last_sums(
         [
-            w_part.reshape(2, blk, rows, -1).transpose(1, 0, 2, 3),
+            w_part,
             small_grads,
-            dnormed.astype(BF).reshape(2, tok, D),
-            o_part.reshape(blk, -1, D),
+            dnormed.reshape(2, tok, D),
+            branch.reshape(-1, tok, D),
         ],
         [
             (0, None, BLK, BLK[::-1], True),
             (1, None, AXES, AXES[::-1], False),
             (2, None, ("head",), ("head",), False),
-            (3, None, BLK, BLK[::-1], False),
-        ],
-        [F32, F32, F32, F32],
+        ]
+        + [(3,) + c for c in summed],
+        [0, 0, 0, 0, 0],
+        dmixed,
+        hidden,
+        mixed,
+        gain_one[None],
+        back_one,
         sizes,
         8,
     )
-    own_scale = lax.dynamic_slice_in_dim(scale_one, head * tok, tok)
-    z_one = inputs * own_scale
-    u_one = gain_one * dnormed_sum
-    hidden_grad = (
-        dmixed + own_scale * (u_one - z_one * jnp.mean(z_one * u_one, axis=-1, keepdims=True))
-    ).astype(BF)
+    d_down, d_gate, d_up = finish([back_one, back_two], width, d_query, 9)
     kn = k_bias.shape[0]
     return (
         output,
         hidden_grad,
         small_sum[0, :rows],
-        jnp.concatenate([w_grads[0, :, :q_cols], w_grads[1, :, :q_cols]], axis=1),
+        d_query,
         small_sum[2, :rows],
-        jnp.concatenate([w_grads[i, :, q_cols : q_cols + kv_cols] for i in range(2)], axis=1),
+        d_key,
         small_sum[3, :kn],
-        jnp.concatenate([w_grads[i, :, q_cols + kv_cols :] for i in range(2)], axis=1),
+        d_value,
         small_sum[4, :kn],
         d_out_weight,
         small_sum[1, :rows],

time: 747 us -> 666 us (0.89)
  Pallas kernels: 498 us -> 593 us
  waiting for transfers between devices: 55.6 us -> 0.11 us
  local copies, waits for them, and re-layouts: 68.6 us -> 19.4 us
  other arithmetic: 64.2 us -> 19.7 us
  matrix products: 24.4 us -> 10.2 us
  starting transfers between devices: 11.7 us -> 0.78 us
    pallas_call x9 -> x12, Pallas kernels: 372 us -> 461 us  [the longest x4 142 us: gather(): pl.pallas_call(functools.partial(gather_kernel, plans, sizes, len(swaps))...]
    ppermute x14 -> x0, waiting for transfers between devices: 41.1 us -> none  [the longest x9 20.8 us: corner_send(): got.append(lax.ppermute(piece, near, [(i, i ^ d) for i in range(parts)]))]
    dynamic_slice x7 -> x0, local copies, waits for them, and re-layouts: 22.7 us -> none  [the longest x3 9.37 us: corner_send(): got = [lax.dynamic_index_in_dim(blocks, corner, 0, keepdims=False)]]
    convert_element_type x17 -> x2, other arithmetic: 23.7 us -> 3.38 us  [the longest x1 1.75 us: shards(): w_feed_two = along_z((mine_two.astype(F32) + lse[0, 7, 0]).astype(BF))]
    another operation x13 -> x0, other arithmetic: 15.5 us -> none  [the longest x3 7.73 us: corner_sort(): held = jnp.stack(got)]
    all_gather x2, waiting for transfers between devices: 14.4 us -> 0.04 us  [along_z(): return lax.all_gather(part, live(('g', 'z'), sizes), axis=0, tiled=True)]
    ppermute x14 -> x0, starting transfers between devices: 11.4 us -> none  [the longest x9 6.93 us: corner_send(): got.append(lax.ppermute(piece, near, [(i, i ^ d) for i in range(parts)]))]
    reshape x6 -> x0, local copies, waits for them, and re-layouts: 9.36 us -> none  [the longest x1 3.04 us: shards(): (dout.astype(F32) * attended).reshape(2, tok, q_cols // HEAD_DIM, HEAD_DIM)]
  transfers between devices with their start and end apart: 18 -> 4, of which waited for: 8 -> 0; matrix products, arithmetic and copies ran while one was open for 15% -> 5% of each run, Pallas kernels for 68% -> 77%
where the time goes in v3:
time: 666 us; the launch traced here: 658 us
  Pallas kernels  593 us (89%)
  other arithmetic  19.7 us (3%)
  local copies, waits for them, and re-layouts  19.4 us (3%)
  between operations  14.4 us (2%)
  matrix products  10.2 us (2%)
    pallas_call x4, Pallas kernels, gather(): pl.pallas_call(functools.partial(gather_kernel, plans, sizes, len(swaps))...  142 us
    pallas_call x2, Pallas kernels, feed(): pl.pallas_call(functools.partial(feed_kernel, chunks, len(before)), grid=...  71.9 us
    pallas_call x1, Pallas kernels, scatter(): pl.pallas_call(functools.partial(scatter_and_swap_kernel, plans, sizes, l...  71.1 us
    pallas_call x1, Pallas kernels, last_sums(): pl.pallas_call(functools.partial(last_kernel, plans, sizes, delays), out_...  70.7 us
    pallas_call x1, Pallas kernels, front(): pl.pallas_call(functools.partial(front_kernel, plans, sizes), out_shape=s...  56.2 us
    pallas_call x1, Pallas kernels, attend_back(): pl.pallas_call(functools.partial(backward_kernel, heads), grid_spec=pltpu...  44.4 us
    pallas_call x1, Pallas kernels, feed_grads(): pl.pallas_call(functools.partial(grads_kernel, plans, sizes), out_shape=[...  38.5 us
    pallas_call x1, Pallas kernels, finish(): pl.pallas_call(functools.partial(finish_kernel, n), out_shape=[jax.ShapeD...  33.5 us
  transfers between devices with their start and end apart: 4, of which 0 were waited for; matrix products, arithmetic and copies ran while one was open for 5% of the time, Pallas kernels for 77%

profile of v3, /device:TPU:0, one launch (start us, length us, event | category | flops | bytes accessed | tf_op | source)
XLA Modules:
  0.0 657.5 jit_solution(1441050189382531812)
XLA Ops:
  11.2 56.2 %shard_map.254 = (bf16[32,48,1024]{2,1,0:T(8,128)(2,1)}, bf16[2,256,1536]{2,1,0:T(8,128)(2,1)}, f32[32,8,128]{2,1,0:T(8,128)}, bf16[16,48,1536]{2,1,0:T(8,128)(2...) custom-call(f32[48,1536]{1,0:T(8,128)} %refs_0_.1, f32[48,256]{1,0:T(8,128)} %refs_1_.2, ...), custom_call_target="tpu_custom_call" | custom-call | bytes 104857600 | tf_op jit(solution)/shard_map/pallas_call | solution.py:299
  74.6 6.6 %shard_map.255 = (bf16[512,768]{1,0:T(8,128)(2,1)}, bf16[512,256]{1,0:T(8,128)(2,1)}, bf16[512,1536]{1,0:T(8,128)(2,1)}) custom-call(bf16[512,1536]{1,0:T(8,128)(2,1)} %bitcast.117, bf16[1536,1024]{1,0:T(8,128)(2,1)} %bitcast.115, f32[1,1536]{1,0:T(1,128)} %broadcast_in_dim_reshape_squeeze.2.gain_ref.refs_7_, f32[1,1024]{1,0:T(1,128)} %bitcast.107, ...), custom_call_target="tpu_custom_call" | custom-call | flops 1610612736 | bytes 12582912 | tf_op jit(solution)/shard_map/pallas_call | solution.py:907
  81.2 64.0 %shard_map.256 = (bf16[16,512,256]{2,1,0:T(8,128)(2,1)}, bf16[8,256,1536]{2,1,0:T(8,128)(2,1)}, bf16[3,4,96,384]{3,2,1,0:T(8,128)(2,1)}) custom-call(bf16[512,256]{1,0:T(8,128)(2,1)} %get-tuple-element.64.refs_0_, bf16[256,1536]{1,0:T(8,128)(2,1)} %refs_1_.3, bf16[3,4,96,384]{3,2,1,0:T(8,128)(2,1)} %get-tuple-element.65.refs_2_), custom_call_target="tpu_custom_call" | custom-call | bytes 209715200 | tf_op jit(solution)/shard_map/pallas_call | solution.py:222
  145.2 27.7 %shard_map.257 = (f32[512,768]{1,0:T(8,128)}, f32[2,8,256]{2,1,0:T(8,128)}) custom-call(s32[32]{0:T(128)} %get-tuple-element.59.slots, s32[2]{0:T(128)} %get-tuple-element.118.tops, bf16[512,768]{1,0:T(8,128)(2,1)} %get-tuple-element.63.q_ref, bf16[32,256,256]{2,1,0:T(8,128)(2,1)} %bitcast.113), custom_call_target="tpu_custom_call" | custom-call | flops 6643777536 | bytes 83886080 | tf_op jit(solution)/shard_map/pallas_call | solution.py:762
  174.0 1.7 add_convert_fusion
  176.0 1.6 convert_element_type.96
  177.9 3.6 fusion.4
  181.5 22.5 %shard_map.258 = bf16[2,256,1536]{2,1,0:T(8,128)(2,1)} custom-call(bf16[2,256,1536]{2,1,0:T(8,128)(2,1)} %get-tuple-element.129.refs_0_), custom_call_target="tpu_custom_call" | custom-call | bytes 31457280 | tf_op jit(solution)/shard_map/pallas_call | solution.py:222
  204.1 2.0 multiply_reduce_fusion.2
  207.4 34.1 %shard_map.259 = bf16[8,256,1536]{2,1,0:T(8,128)(2,1)} custom-call(bf16[256,1536]{1,0:T(8,128)(2,1)} %multiply_convert_fusion.refs_0_), custom_call_target="tpu_custom_call" | custom-call | bytes 125829120 | tf_op jit(solution)/shard_map/pallas_call | solution.py:222
  241.5 43.2 %shard_map.260 = (bf16[2048,768]{1,0:T(8,128)(2,1)}, bf16[2048,768]{1,0:T(8,128)(2,1)}, bf16[2048,768]{1,0:T(8,128)(2,1)}, bf16[2048,1536]{1,0:T(8,128)(2,1)}, bf16[2048,1536]{1,0:T(8,128)(2,1)}) custom-call(bf16[2048,1536]{1,0:T(8,128)(2,1)} %bitcast.83, bf16[2048,1536]{1,0:T(8,128)(2,1)} %bitcast.109, ...), custom_call_target="tpu_custom_call" | custom-call | flops 28991029248 | bytes 41943040 | tf_op jit(solution)/shard_map/pallas_call | solution.py:583
  284.8 21.5 %shard_map.261.refs_2_ = bf16[4,3,384,768]{3,2,1,0:T(8,128)(2,1)} custom-call(bf16[2048,1536]{1,0:T(8,128)(2,1)} %bitcast.84, bf16[2048,1536]{1,0:T(8,128)(2,1)} %bitcast.110, bf16[2048,768]{1,0:T(8,128)(2,1)} %get-tuple-element.75.act_ref, bf16[2048,768]{1,0:T(8,128)(2,1)} %get-tuple-element.76.dgate_ref, bf16[2048,768]{1,0:T(8,128)(2,1)} %get-tuple-element.77.dup_ref), custom_call_target="tpu_custom_call" | custom-call | flops 14495514624 | bytes 41943040 | tf_op jit(solution)/shard_map/pallas_call | solution.py:611
  306.8 28.6 %shard_map.262 = (bf16[2048,384]{1,0:T(8,128)(2,1)}, bf16[2048,384]{1,0:T(8,128)(2,1)}, bf16[2048,384]{1,0:T(8,128)(2,1)}, bf16[2048,1536]{1,0:T(8,128)(2,1)}, bf16[2048,1536]{1,0:T(8,128)(2,1)}) custom-call(bf16[2048,1536]{1,0:T(8,128)(2,1)} %bitcast.85, bf16[2048,1536]{1,0:T(8,128)(2,1)} %bitcast.111, ...), custom_call_target="tpu_custom_call" | custom-call | flops 14495514624 | bytes 41943040 | tf_op jit(solution)/shard_map/pallas_call | solution.py:583
  335.4 38.5 %shard_map.263 = (f32[256,1536]{1,0:T(8,128)}, bf16[4,3,384,384]{3,2,1,0:T(8,128)(2,1)}) custom-call(bf16[8,256,1536]{2,1,0:T(8,128)(2,1)} %bitcast.119, bf16[2048,1536]{1,0:T(8,128)(2,1)} %bitcast.86, bf16[2048,1536]{1,0:T(8,128)(2,1)} %bitcast.112, bf16[2048,384]{1,0:T(8,128)(2,1)} %get-tuple-element.79.act_hbm, ...), custom_call_target="tpu_custom_call" | custom-call | flops 7247757312 | bytes 104857600 | tf_op jit(solution)/shard_map/pallas_call | solution.py:686
  373.9 2.0 multiply_reduce_fusion
  375.9 1.9 fusion.2
  377.8 21.6 %shard_map.264 = bf16[2,256,1536]{2,1,0:T(8,128)(2,1)} custom-call(bf16[256,1536]{1,0:T(8,128)(2,1)} %get-tuple-element.113.refs_0_), custom_call_target="tpu_custom_call" | custom-call | bytes 31457280 | tf_op jit(solution)/shard_map/pallas_call | solution.py:222
  399.5 4.3 convolution_convert_fusion
  403.8 2.3 convolution_convert_fusion.1.do_ref
  406.1 44.4 %shard_map.265 = (bf16[512,768]{1,0:T(8,128)(2,1)}, bf16[32,256,256]{2,1,0:T(8,128)(2,1)}) custom-call(s32[32]{0:T(128)} %get-tuple-element.59.slots, s32[2]{0:T(128)} %get-tuple-element.118.tops, bf16[512,768]{1,0:T(8,128)(2,1)} %get-tuple-element.63.q_ref, bf16[32,256,256]{2,1,0:T(8,128)(2,1)} %bitcast.114, ...), custom_call_target="tpu_custom_call" | custom-call | flops 16609443840 | bytes 125829120 | tf_op jit(solution)/shard_map/pallas_call | solution.py:850
  450.5 71.1 %shard_map.266 = (bf16[512,256]{1,0:T(8,128)(2,1)}, f32[48,1536]{1,0:T(8,128)}, bf16[4,3,384,384]{3,2,1,0:T(8,128)(2,1)}) custom-call(bf16[16,512,256]{2,1,0:T(8,128)(2,1)} %bitcast.87, bf16[16,48,1536]{2,1,0:T(8,128)(2,1)} %bitcast.90, bf16[4,3,384,384]{3,2,1,0:T(8,128)(2,1)} %get-tuple-element.85.refs_2_), custom_call_target="tpu_custom_call", output_to_operand_aliasing={{2}: (2, {})} | custom-call | bytes 131072000 | tf_op jit(solution)/shard_map/pallas_call | solution.py:482
  521.6 8.9 %shard_map.267 = (bf16[16,2,48,1024]{3,2,1,0:T(8,128)(2,1)}, bf16[512,1536]{1,0:T(8,128)(2,1)}, f32[1,1536]{1,0:T(1,128)}, f32[1,1024]{1,0:T(1,128)}) custom-call(bf16[512,768]{1,0:T(8,128)(2,1)} %get-tuple-element.83.dq_ref, bf16[512,256]{1,0:T(8,128)(2,1)} %get-tuple-element.86.dkv_ref, bf16[512,1536]{1,0:T(8,128)(2,1)} %get-tuple-element.87.normed_ref, ...), custom_call_target="tpu_custom_call" | custom-call | flops 3221225472 | bytes 16777216 | tf_op jit(solution)/shard_map/pallas_call | solution.py:970
  534.1 70.7 %shard_map.268 = (f32[48,1536]{1,0:T(8,128)}, f32[48,256]{1,0:T(8,128)}, f32[48,256]{1,0:T(8,128)}, f32[8,128]{1,0:T(8,128)}, bf16[256,1536]{1,0:T(8,128)(2,1)}, /*index=5*/bf16[256,1536]{1,0:T(8,128)(2,1)}) custom-call(bf16[16,2,48,1024]{3,2,1,0:T(8,128)(2,1)} %get-tuple-element.88.refs_0_, f32[32,8,128]{2,1,0:T(8,128)} %bitcast.98, ...), custom_call_target="tpu_custom_call" | custom-call | bytes 209715200 | tf_op jit(solution)/shard_map/pallas_call | solution.py:1027
  607.4 33.5 %shard_map.269 = (f32[96,4480]{1,0:T(8,128)}, f32[96,4480]{1,0:T(8,128)}, f32[96,4480]{1,0:T(8,128)}) custom-call(bf16[3,4,96,768]{3,2,1,0:T(8,128)(2,1)} %bitcast.81, bf16[3,4,96,384]{3,2,1,0:T(8,128)(2,1)} %bitcast.97, f32[48,1536]{1,0:T(8,128)} %get-tuple-element.154.refs_2_), custom_call_target="tpu_custom_call" | custom-call | tf_op jit(solution)/shard_map/pallas_call | solution.py:526
  (114 shorter events, 30.6 us)
Async XLA Ops:
  7.2 234.4 %all-gather.5.cloned.1.call-start = ((), (), s32[]{:S(2)}) async-start(), calls=%async_computation.3 | async-start | bytes 8847360 | tf_op jit(solution)/shard_map/all_gather | solution.py:1105
  67.4 0.9 copy-start.15
  67.4 1.5 copy-start.18
  67.4 239.3 %all-gather.3.cloned.1.call-start = ((), (), s32[]{:S(2)}) async-start(), calls=%async_computation.2 | async-start | bytes 4423680 | tf_op jit(solution)/shard_map/all_gather | solution.py:1105
  145.1 28.9 %copy-start.11 = (bf16[3,4,96,384]{3,2,1,0:T(8,128)(2,1)S(1)}, bf16[3,4,96,384]{3,2,1,0:T(8,128)(2,1)}, u32[]{:S(2)}) copy-start(bf16[3,4,96,384]{3,2,1,0:T(8,128)(2,1)} %get-tuple-element.70) | copy-start | bytes 2654212
  175.8 2.1 copy-start.4
  175.8 358.3 %reduce-scatter.3.cloned.1.call-start = ((), (), s32[]{:S(2)}) async-start(), calls=%async_computation.4 | async-start | bytes 8847360 | tf_op jit(solution)/shard_map/reduce_scatter | solution.py:1204
  181.5 22.6 %copy-start.1 = (bf16[256,1536]{1,0:T(8,128)(2,1)S(1)}, bf16[256,1536]{1,0:T(8,128)(2,1)}, u32[]{:S(2)}) copy-start(bf16[256,1536]{1,0:T(8,128)(2,1)} %refs_5_.1) | copy-start | bytes 2359300
  206.1 169.8 %copy-start = (f32[256,1536]{1,0:T(8,128)}, f32[256,1536]{1,0:T(8,128)S(1)}, u32[]{:S(2)}) copy-start(f32[256,1536]{1,0:T(8,128)S(1)} %get-tuple-element.116.refs_6_) | copy-start | bytes 4718596
  306.3 301.1 %reduce-scatter.5.cloned.1.call-start = ((), (), s32[]{:S(2)}) async-start(), calls=%async_computation.5 | async-start | bytes 4423680 | tf_op jit(solution)/shard_map/reduce_scatter | solution.py:1204
  373.9 2.1 copy-start.2
  373.9 2.1 copy-start.3
  399.5 4.4 copy-start.5
  399.5 4.4 copy-start.9
  604.8 36.1 %copy-start.13 = (bf16[256,1536]{1,0:T(8,128)(2,1)S(1)}, bf16[256,1536]{1,0:T(8,128)(2,1)}, u32[]{:S(2)}) copy-start(bf16[256,1536]{1,0:T(8,128)(2,1)} %get-tuple-element.151) | copy-start | bytes 2359300
  607.4 34.5 %copy-start.12 = (bf16[256,1536]{1,0:T(8,128)(2,1)S(1)}, bf16[256,1536]{1,0:T(8,128)(2,1)}, u32[]{:S(2)}) copy-start(bf16[256,1536]{1,0:T(8,128)(2,1)} %get-tuple-element.152) | copy-start | bytes 2359300
  640.9 1.8 copy-start.10
  640.9 2.5 copy-start.17
  640.9 3.1 copy-start.16
  640.9 3.7 copy-start.14
  641.8 3.6 copy-start.8
  645.4 2.1 copy-start.7
  647.5 2.1 copy-start.6
Sparse Core Ops, SparseCore 0:
  67.5 152.7 all-gather.4
  221.9 68.1 all-gather.2
  306.4 144.9 reduce-scatter.2
  521.7 80.0 reduce-scatter.4

commit v4 on v3

--- a/solution.py
+++ b/solution.py
@@ -140,15 +140,17 @@
     )
 
 
-def gather_kernel(plans, sizes, swap_count, *refs, ahead=None):
+def gather_kernel(plans, sizes, swap_count, waited, carried, *refs, ahead=None):
     count = max(p[0] for p in plans) + 1
     xs, refs = refs[:count], refs[count:]
-    swap_xs, refs = refs[:swap_count], refs[swap_count:]
+    swap_xs, refs = refs[:swap_count], refs[swap_count + waited :]
     outs, refs = refs[:count], refs[count:]
-    swap_outs, refs = refs[:swap_count], refs[swap_count:]
+    swap_outs, refs = refs[:swap_count], refs[swap_count + carried :]
     send_sems, recv_sems, local_sems = refs[:3]
     swaps = swaps_of(swap_xs, swap_outs, refs[3:])
     used = {a: (sizes[a] if any(a in p[3] for p in plans) else 1) for a in AXES}
+    if swaps:
+        used.update(y=sizes["y"], c=sizes["c"])
     greet(live(AXES, used), sizes, bool(swaps))
 
     def cut(ref, rows):
@@ -204,7 +206,7 @@
         copy.wait_send()
 
 
-def gather(arrays, plans, sizes, collective_id, swaps=()):
+def gather(arrays, plans, sizes, collective_id, swaps=(), after=(), carried=()):
     plans = [
         (i, rows, live(layout, sizes), live(phases, sizes), split)
         for i, rows, layout, phases, split in plans
@@ -220,10 +222,15 @@
     specs = [spec] * len(arrays) + [far] * len(swaps)
     moved = sum(int(np.prod(s.shape)) * s.dtype.itemsize for s in shapes)
     return pl.pallas_call(
-        functools.partial(gather_kernel, plans, sizes, len(swaps)),
-        out_shape=shapes + [jax.ShapeDtypeStruct(x.shape, x.dtype) for x in swaps],
-        in_specs=specs,
-        out_specs=specs,
+        functools.partial(
+            gather_kernel, plans, sizes, len(swaps), len(after) + len(carried), len(carried)
+        ),
+        out_shape=shapes + [jax.ShapeDtypeStruct(x.shape, x.dtype) for x in (*swaps, *carried)],
+        in_specs=specs + [far] * (len(after) + len(carried)),
+        out_specs=specs + [far] * len(carried),
+        input_output_aliases={
+            len(specs) + len(after) + i: len(specs) + i for i in range(len(carried))
+        },
         scratch_shapes=[
             pltpu.SemaphoreType.DMA((total,)),
             pltpu.SemaphoreType.DMA((total,)),
@@ -234,14 +241,14 @@
             collective_id=collective_id, has_side_effects=True, vmem_limit_bytes=VMEM_LIMIT
         ),
         cost_estimate=pl.CostEstimate(flops=0, bytes_accessed=20 * moved, transcendentals=0),
-    )(*arrays, *swaps)
+    )(*arrays, *swaps, *after, *carried)
 
 
 def front_kernel(plans, sizes, *refs):
     q_ref, k_ref, v_ref, o_ref, hidden_ref, small_ref = refs[:6]
     feeds, refs = refs[6:9], refs[9:]
-    outs, swapped, second_ref, refs = refs[:4], refs[4], refs[5], refs[6:]
-    halves_s, o_s, first_s = refs[:3]
+    outs, first_ref, second_ref, refs = refs[:4], refs[4], refs[5], refs[6:]
+    halves_s, o_s = refs[:2]
     heads = halves_s.shape[0]
     q_cols, kv_cols = q_ref.shape[1] // heads, k_ref.shape[1] // heads
     for i in range(heads):
@@ -252,12 +259,12 @@
     o_s[...] = o_ref[...].astype(BF)
 
     def pack():
-        first, second = first_s.shape[-1], second_ref.shape[-1]
+        first, second = first_ref.shape[-1], second_ref.shape[-1]
         for m, feed_ref in enumerate(feeds):
             rows, width = feed_ref.shape
-            for i in range(first_s.shape[1]):
+            for i in range(first_ref.shape[1]):
                 low = i * (first + second)
-                for ref, n in ((first_s, first), (second_ref, second)):
+                for ref, n in ((first_ref, first), (second_ref, second)):
                     real = min(n, width - low)
                     ref[m, i, :, :real] = feed_ref[:, low : low + real].astype(BF)
                     if real < n:
@@ -267,15 +274,15 @@
     gather_kernel(
         plans,
         sizes,
-        1,
+        0,
+        0,
+        0,
         halves_s,
         hidden_ref,
         small_ref,
         o_s,
-        first_s,
         *outs,
-        swapped,
-        *refs[3:],
+        *refs[2:],
         ahead=pack,
     )
 
@@ -295,21 +302,18 @@
     ff_rows = feeds[0].shape[0]
     blocks = [jax.ShapeDtypeStruct((3, 4, ff_rows, n), BF) for n in (first, second)]
     spec = pl.BlockSpec(memory_space=pltpu.VMEM)
-    far = pl.BlockSpec(memory_space=pl.ANY)
     return pl.pallas_call(
         functools.partial(front_kernel, plans, sizes),
         out_shape=shapes + blocks,
         in_specs=[spec] * 9,
-        out_specs=[spec] * 4 + [far, spec],
+        out_specs=[spec] * 6,
         scratch_shapes=[
             pltpu.VMEM(halves.shape, BF),
             pltpu.VMEM(out.shape, BF),
-            pltpu.VMEM(blocks[0].shape, BF),
             pltpu.SemaphoreType.DMA((total,)),
             pltpu.SemaphoreType.DMA((total,)),
             pltpu.SemaphoreType.DMA((len(plans),)),
-        ]
-        + swap_scratch(blocks[:1]),
+        ],
         compiler_params=pltpu.CompilerParams(
             collective_id=collective_id, has_side_effects=True, vmem_limit_bytes=VMEM_LIMIT
         ),
@@ -324,7 +328,7 @@
     return keys
 
 
-def scatter_kernel(plans, sizes, *refs, between=None, swaps=(), delays=None):
+def scatter_kernel(plans, sizes, *refs, between=None):
     count = max(p[0] for p in plans) + 1
     xs, outs = refs[:count], refs[count : 2 * count]
     at = 2 * count
@@ -338,7 +342,7 @@
         a: (sizes[a] if any(a in p[3] or (p[4] and a == "head") for p in plans) else 1)
         for a in AXES
     }
-    greet(live(AXES, used), sizes, bool(swaps))
+    greet(live(AXES, used), sizes)
     sem = 0
     sends = []
     arrivals = [dict() for _ in plans]
@@ -366,12 +370,10 @@
                 total = total + buf[...].astype(F32)
         return total
 
-    delays = delays or [0] * len(plans)
-    depth = max(len(p[3]) + delay for p, delay in zip(plans, delays))
-    for step in range(depth):
+    depth = max(len(p[3]) for p in plans)
+    for phase in range(depth):
         for j, (i, rows, layout, phases, swap) in enumerate(plans):
-            phase = step - delays[j]
-            if phase < 0 or phase >= len(phases):
+            if phase >= len(phases):
                 continue
             a, rest = phases[phase], phases[phase + 1 :]
             for d in range(1, sizes[a]):
@@ -390,11 +392,8 @@
                     sends.append(copy)
                     arrivals[j][(phase, d, where)] = sem
                     sem += 1
-        if step == min(2, depth - 1):
-            for item in swaps:
-                item.start()
         if between is not None:
-            between(step)
+            between(phase)
     late = []
     for j, (i, rows, layout, phases, swap) in enumerate(plans):
         total = total_of(j, {}, len(phases))
@@ -423,8 +422,6 @@
             item.wait()
         else:
             remote(item, item, send_sems.at[s], recv_sems.at[s], "head", 0, sizes).wait_recv()
-    for item in swaps:
-        item.wait()
     for copy in sends:
         copy.wait_send()
 
@@ -461,78 +458,115 @@
     ]
 
 
-def scatter_and_swap_kernel(plans, sizes, arrays, carried, swap_count, delays, *refs):
-    xs, refs = refs[:arrays], refs[arrays:]
-    swap_xs, refs = refs[:swap_count], refs[swap_count + carried :]
-    outs, refs = refs[:arrays], refs[arrays:]
-    swap_outs, refs = refs[:swap_count], refs[swap_count + carried :]
-    held = 3 if swap_count else 0
-    swaps = swaps_of(swap_xs, swap_outs, refs[len(refs) - held :])
-    rest = refs[: len(refs) - held]
-    scatter_kernel(plans, sizes, *xs, *outs, *rest, swaps=swaps, delays=delays)
-
-
-def scatter(arrays, plans, out_types, sizes, collective_id, swaps=(), carried=(), delays=None):
+def scatter_and_wait_kernel(plans, sizes, arrays, waited, carried, *refs):
+    xs, refs = refs[:arrays], refs[arrays + waited :]
+    scatter_kernel(plans, sizes, *xs, *refs[:arrays], *refs[arrays + carried :])
+
+
+def scatter(arrays, plans, out_types, sizes, collective_id, after=(), carried=()):
     plans = alive(plans, sizes)
     shapes = [jax.ShapeDtypeStruct(x.shape[1:], kind) for x, kind in zip(arrays, out_types)]
     spec = pl.BlockSpec(memory_space=pltpu.VMEM)
     far = pl.BlockSpec(memory_space=pl.ANY)
-    specs = [spec] * len(arrays) + [far] * (len(swaps) + len(carried))
     moved = sum(int(np.prod(x.shape)) * x.dtype.itemsize for x in arrays)
     return pl.pallas_call(
         functools.partial(
-            scatter_and_swap_kernel, plans, sizes, len(arrays), len(carried), len(swaps), delays
-        ),
-        out_shape=shapes + [jax.ShapeDtypeStruct(x.shape, x.dtype) for x in (*swaps, *carried)],
-        in_specs=specs,
-        out_specs=specs,
+            scatter_and_wait_kernel,
+            plans,
+            sizes,
+            len(arrays),
+            len(after) + len(carried),
+            len(carried),
+        ),
+        out_shape=shapes + [jax.ShapeDtypeStruct(x.shape, x.dtype) for x in carried],
+        in_specs=[spec] * len(arrays) + [far] * (len(after) + len(carried)),
+        out_specs=[spec] * len(arrays) + [far] * len(carried),
         input_output_aliases={
-            len(arrays) + len(swaps) + i: len(arrays) + len(swaps) + i for i in range(len(carried))
+            len(arrays) + len(after) + i: len(arrays) + i for i in range(len(carried))
         },
-        scratch_shapes=scatter_scratch(arrays, plans, out_types, sizes) + swap_scratch(swaps),
+        scratch_shapes=scatter_scratch(arrays, plans, out_types, sizes),
         compiler_params=pltpu.CompilerParams(
             collective_id=collective_id, has_side_effects=True, vmem_limit_bytes=VMEM_LIMIT
         ),
         cost_estimate=pl.CostEstimate(flops=0, bytes_accessed=20 * moved, transcendentals=0),
-    )(*arrays, *swaps, *carried)
-
-
-def finish_kernel(count, *refs):
-    xs, refs = refs[:count], refs[count + 1 :]
-    outs, got, sems = refs[:3], refs[3 : 3 + count], refs[3 + count :]
-    items = swaps_of(xs, got, sems)
+    )(*arrays, *after, *carried)
+
+
+def swap_kernel(count, *refs):
+    items = swaps_of(refs[:count], refs[count + 1 : 2 * count + 1], refs[2 * count + 1 :])
     greet(("y", "c"), {"y": 2, "c": 2}, True)
     for item in items:
         item.start()
-    width = outs[0].shape[1]
-    lanes = sum(x.shape[-1] for x in xs)
-    start = 0
-    for item, part in zip(items, got):
+    for item in items:
         item.wait()
-        n = part.shape[-1]
-        for m, out in enumerate(outs):
-            for i in range(part.shape[1]):
-                low = i * lanes + start
-                high = min(low + n, width)
-                if high > low:
-                    out[:, low:high] = part[m, i, :, : high - low].astype(F32)
-        start += n
-
-
-def finish(xs, width, last, collective_id):
+
+
+def swap(xs, last, collective_id):
     far = pl.BlockSpec(memory_space=pl.ANY)
-    spec = pl.BlockSpec(memory_space=pltpu.VMEM)
     n = len(xs)
     return pl.pallas_call(
-        functools.partial(finish_kernel, n),
-        out_shape=[jax.ShapeDtypeStruct((xs[0].shape[2], width), F32)] * 3,
+        functools.partial(swap_kernel, n),
+        out_shape=[jax.ShapeDtypeStruct(x.shape, x.dtype) for x in xs],
         in_specs=[far] * (n + 1),
-        out_specs=[spec] * 3,
-        scratch_shapes=[pltpu.VMEM(x.shape, x.dtype) for x in xs] + swap_scratch(xs),
+        out_specs=[far] * n,
+        scratch_shapes=swap_scratch(xs),
         compiler_params=pltpu.CompilerParams(
             collective_id=collective_id, has_side_effects=True, vmem_limit_bytes=VMEM_LIMIT
         ),
     )(*xs, last)
+
+
+def outputs_kernel(*refs):
+    w_ref, dnormed_ref, branch_ref, dmixed_ref, x_ref, mixed_ref, gain_ref = refs[:7]
+    parts, refs = refs[7:9], refs[9:]
+    q_ref, k_ref, v_ref, out_ref, hidden_ref = refs[:5]
+    feeds = refs[5:]
+    heads = w_ref.shape[0]
+    q_cols = q_ref.shape[1] // heads
+    for i in range(heads):
+        cols = slice(i * HEAD_DIM, (i + 1) * HEAD_DIM)
+        q_ref[:, i * q_cols : (i + 1) * q_cols] = w_ref[i, :, :q_cols]
+        k_ref[:, cols] = w_ref[i, :, q_cols : q_cols + HEAD_DIM]
+        v_ref[:, cols] = w_ref[i, :, q_cols + HEAD_DIM :]
+    out_ref[...] = (mixed_ref[...] + branch_ref[...]).astype(BF)
+    x = x_ref[...].astype(F32)
+    scale = inverse_rms(x)
+    z = x * scale
+    u = gain_ref[...] * dnormed_ref[...]
+    hidden_ref[...] = (
+        dmixed_ref[...] + scale * (u - z * jnp.mean(z * u, axis=-1, keepdims=True))
+    ).astype(BF)
+    width = feeds[0].shape[1]
+    lanes = sum(part.shape[-1] for part in parts)
+    for m, feed_ref in enumerate(feeds):
+        for i in range(parts[0].shape[1]):
+            low = i * lanes
+            for part in parts:
+                n = part.shape[-1]
+                real = min(n, width - low)
+                if real > 0:
+                    feed_ref[:, low : low + real] = part[m, i, :, :real].astype(F32)
+                low += n
+
+
+def write_outputs(w, dnormed, branch, dmixed, x, mixed, gain, parts, width):
+    spec = pl.BlockSpec(memory_space=pltpu.VMEM)
+    heads, rows, inner = w.shape
+    kinds = [
+        ((rows, heads * (inner - 2 * HEAD_DIM)), F32),
+        ((rows, heads * HEAD_DIM), F32),
+        ((rows, heads * HEAD_DIM), F32),
+        (x.shape, BF),
+        (x.shape, BF),
+    ] + [((parts[0].shape[2], width), F32)] * 3
+    return pl.pallas_call(
+        outputs_kernel,
+        out_shape=[jax.ShapeDtypeStruct(*k) for k in kinds],
+        in_specs=[spec] * 9,
+        out_specs=[spec] * len(kinds),
+        compiler_params=pltpu.CompilerParams(vmem_limit_bytes=VMEM_LIMIT),
+        cost_estimate=pl.CostEstimate(flops=0, bytes_accessed=20 * 2**20, transcendentals=0),
+    )(w, dnormed, branch, dmixed, x, mixed, gain, *parts)
 
 
 def feed_kernel(chunks, added, t_ref, c_ref, w_ref, *refs):
@@ -985,65 +1019,6 @@
     )(dq, dkv, normed, x, w, cosine, sine)
 
 
-def last_kernel(plans, sizes, delays, *refs):
-    xs, refs = refs[:4], refs[4:]
-    dmixed_ref, x_ref, mixed_ref, gain_ref, _ = refs[:5]
-    q_ref, k_ref, v_ref, small_ref, out_ref, hidden_ref = refs[5:11]
-    w_s, dnormed_s, branch_s = refs[11:14]
-    outs = (w_s, small_ref, dnormed_s, branch_s)
-    scatter_kernel(plans, sizes, *xs, *outs, *refs[14:], delays=delays)
-    heads = w_s.shape[0]
-    q_cols = q_ref.shape[1] // heads
-    for i in range(heads):
-        cols = slice(i * HEAD_DIM, (i + 1) * HEAD_DIM)
-        q_ref[:, i * q_cols : (i + 1) * q_cols] = w_s[i, :, :q_cols]
-        k_ref[:, cols] = w_s[i, :, q_cols : q_cols + HEAD_DIM]
-        v_ref[:, cols] = w_s[i, :, q_cols + HEAD_DIM :]
-    out_ref[...] = (mixed_ref[...] + branch_s[...]).astype(BF)
-    x = x_ref[...].astype(F32)
-    scale = inverse_rms(x)
-    z = x * scale
-    u = gain_ref[...] * dnormed_s[...]
-    hidden_ref[...] = (
-        dmixed_ref[...] + scale * (u - z * jnp.mean(z * u, axis=-1, keepdims=True))
-    ).astype(BF)
-
-
-def last_sums(arrays, plans, delays, dmixed, x, mixed, gain, after, sizes, collective_id):
-    plans = alive(plans, sizes)
-    kinds = [F32] * 4
-    spec = pl.BlockSpec(memory_space=pltpu.VMEM)
-    heads, rows, width = arrays[0].shape[1:]
-    q_cols = heads * (width - 2 * HEAD_DIM)
-    tok = x.shape[0]
-    shapes = [
-        ((rows, q_cols), F32),
-        ((rows, heads * HEAD_DIM), F32),
-        ((rows, heads * HEAD_DIM), F32),
-        (arrays[1].shape[1:], F32),
-        ((tok, D), BF),
-        ((tok, D), BF),
-    ]
-    return pl.pallas_call(
-        functools.partial(last_kernel, plans, sizes, delays),
-        out_shape=[jax.ShapeDtypeStruct(*s) for s in shapes],
-        in_specs=[spec] * 8 + [pl.BlockSpec(memory_space=pl.ANY)],
-        out_specs=[spec] * 6,
-        scratch_shapes=[
-            pltpu.VMEM((heads, rows, width), F32),
-            pltpu.VMEM((tok, D), F32),
-            pltpu.VMEM((tok, D), F32),
-        ]
-        + scatter_scratch(arrays, plans, kinds, sizes),
-        compiler_params=pltpu.CompilerParams(
-            collective_id=collective_id, has_side_effects=True, vmem_limit_bytes=VMEM_LIMIT
-        ),
-        cost_estimate=pl.CostEstimate(
-            flops=0, bytes_accessed=200 * 2**20, transcendentals=0
-        ),
-    )(*arrays, dmixed, x, mixed, gain, after)
-
-
 def small_rows(*rows):
     return jnp.stack(
         [jnp.pad(r.astype(F32), ((0, LANES - r.shape[0]),)) for r in rows]
@@ -1104,7 +1079,7 @@
         part = part.reshape(1, 3, parts * ff_rows, part.shape[-1])
         return lax.all_gather(part, live(("g", "z"), sizes), axis=0, tiled=True)
 
-    w_qkv, x_pair, small_all, w_out, mine_one, packed_two = front(
+    w_qkv, x_pair, small_all, w_out, packed_one, packed_two = front(
         (q_weight, k_weight, v_weight, o_weight),
         hidden,
         small,
@@ -1120,7 +1095,6 @@
         sizes,
         1,
     )
-    w_feed_one = along_z(mine_one)
     w_out = w_out.reshape(q_cols, D)
     w_qkv = w_qkv.reshape(D, q_cols + 2 * kv_cols)
     x_pair = x_pair.reshape(pair, D)
@@ -1152,26 +1126,36 @@
         ((0, half), group, ("c", "head", "y"), False),
         ((half, half), group, ("c", "y", "head"), False),
     ]
-    kv, cot_all, mine_two = gather(
-        [kv_local, cotangent],
-        [
-            (0, None, place_axes, place_axes, False),
-            (1, None, group, ("y", "head", "c"), False),
-        ],
+    far_axes, near_axes = place_axes[:2], place_axes[2:]
+    cot_all = lax.all_gather(cotangent, group, axis=0, tiled=True)
+    kv, mine_one = gather(
+        [kv_local],
+        [(0, None, far_axes, far_axes, False)],
         sizes,
         2,
-        [packed_two],
-    )
-    cot_all = cot_all.reshape(-1, D)
+        [packed_one],
+        [cot_all],
+    )
+    w_feed_one = along_z(mine_one)
+    if near_axes:
+        (kv,) = gather([kv], [(0, None, near_axes, near_axes, False)], sizes, 10)
+    near_count = int(np.prod([sizes[a] for a in near_axes], dtype=int))
+    far_count = SEQ_SPAN // near_count
+    where = slots // 2
+    slots = ((where % near_count) * far_count + where // near_count) * 2 + slots % 2
     kv = kv.reshape(2 * SEQ_SPAN, tok, 2 * HEAD_DIM)
     attended, lse = attend(slots, tops, queries, kv)
-    w_feed_two = along_z((mine_two.astype(F32) + lse[0, 7, 0]).astype(BF))
     attn_local = attended.astype(BF)
     inputs = hidden.astype(F32)
     mixed_part = dot_nn(attn_local, w_out).reshape(2, tok, D)
-    (mixed_got,) = gather(
-        [mixed_part.astype(BF)], [(0, None, ("head",), ("head",), True)], sizes, 3
-    )
+    mixed_got, mine_two = gather(
+        [mixed_part.astype(BF)],
+        [(0, None, ("head",), ("head",), True)],
+        sizes,
+        3,
+        [packed_two],
+    )
+    w_feed_two = along_z(mine_two)
     mixed = (
         inputs
         + lax.dynamic_index_in_dim(mixed_part, head, 0, keepdims=False)
@@ -1222,14 +1206,13 @@
     dkv, d_out_weight, parts_two = scatter(
         [dkv_parts.reshape(SEQ_SPAN, pair, 2 * HEAD_DIM), o_part.reshape(blk, -1, D)],
         [
-            (0, None, place_axes, place_axes[::-1], False),
+            (0, None, near_axes + far_axes, place_axes[::-1], False),
             (1, None, BLK, BLK[::-1], False),
         ],
         [BF, F32],
         sizes,
         7,
-        [],
-        [parts_two],
+        carried=[parts_two],
     )
     back_two = collect(parts_two)
     w_part, dnormed, norm1_part, bias_part = project_back(
@@ -1261,7 +1244,7 @@
         axis=2,
     )
     small_grads = small_grads.transpose(1, 0, 2, 3).reshape(2 * blk, 8, LANES)
-    d_query, d_key, d_value, small_sum, output, hidden_grad = last_sums(
+    w_grads, small_sum, dnormed_sum, branch_sum = scatter(
         [
             w_part,
             small_grads,
@@ -1274,16 +1257,22 @@
             (2, None, ("head",), ("head",), False),
         ]
         + [(3,) + c for c in summed],
-        [0, 0, 0, 0, 0],
+        [F32] * 4,
+        sizes,
+        8,
+        [back_one],
+    )
+    d_query, d_key, d_value, output, hidden_grad, d_down, d_gate, d_up = write_outputs(
+        w_grads,
+        dnormed_sum,
+        branch_sum,
         dmixed,
         hidden,
         mixed,
         gain_one[None],
-        back_one,
-        sizes,
-        8,
-    )
-    d_down, d_gate, d_up = finish([back_one, back_two], width, d_query, 9)
+        swap([back_one, back_two], w_grads, 9),
+        width,
+    )
     kn = k_bias.shape[0]
     return (
         output,

time: 666 us -> 642 us (0.964)
  Pallas kernels: 593 us -> 570 us
  waiting for transfers between devices: 0.11 us -> 9.03 us
  local copies, waits for them, and re-layouts: 19.4 us -> 10.6 us
    pallas_call x7 -> x9, Pallas kernels: 317 us -> 290 us  [the longest x5 133 us: gather(): pl.pallas_call(functools.partial(gather_kernel, plans, sizes, len(swaps),...]
    unnamed x48 -> x20, local copies, waits for them, and re-layouts: 10.9 us -> 1.26 us
    all_gather x2, waiting for transfers between devices: 0.04 us -> 8.27 us  [along_z(): return lax.all_gather(part, live(('g', 'z'), sizes), axis=0, tiled=True)]
  transfers between devices with their start and end apart: 4 -> 5, of which waited for: 0 -> 2; matrix products, arithmetic and copies ran while one was open for 5% -> 6% of each run, Pallas kernels for 77% -> 80%
where the time goes in v4:
time: 642 us; the launch traced here: 634 us
  Pallas kernels  570 us (89%)
  other arithmetic  18.5 us (3%)
  between operations  14.3 us (2%)
  local copies, waits for them, and re-layouts  10.6 us (2%)
  matrix products  10.2 us (2%)
  waiting for transfers between devices  9.03 us (1%)
    pallas_call x5, Pallas kernels, gather(): pl.pallas_call(functools.partial(gather_kernel, plans, sizes, len(swaps),...  133 us
    pallas_call x2, Pallas kernels, scatter(): pl.pallas_call(functools.partial(scatter_and_wait_kernel, plans, sizes, l...  118 us
    pallas_call x2, Pallas kernels, feed(): pl.pallas_call(functools.partial(feed_kernel, chunks, len(before)), grid=...  71.8 us
    pallas_call x1, Pallas kernels, front(): pl.pallas_call(functools.partial(front_kernel, plans, sizes), out_shape=s...  61.5 us
    pallas_call x1, Pallas kernels, attend_back(): pl.pallas_call(functools.partial(backward_kernel, heads), grid_spec=pltpu...  44.5 us
    pallas_call x1, Pallas kernels, feed_grads(): pl.pallas_call(functools.partial(grads_kernel, plans, sizes), out_shape=[...  38.1 us
    pallas_call x1, Pallas kernels, swap(): pl.pallas_call(functools.partial(swap_kernel, n), out_shape=[jax.ShapeDty...  31.3 us
    pallas_call x1, Pallas kernels, attend(): pl.pallas_call(functools.partial(forward_kernel, heads), grid_spec=pltpu....  27.5 us
  transfers between devices with their start and end apart: 5, of which 2 were waited for; matrix products, arithmetic and copies ran while one was open for 6% of the time, Pallas kernels for 80%

profile of v4, /device:TPU:0, one launch (start us, length us, event | category | flops | bytes accessed | tf_op | source)
XLA Modules:
  0.0 633.6 jit_solution(6590093706594361784)
XLA Ops:
  11.9 61.5 %shard_map.254 = (bf16[32,48,1024]{2,1,0:T(8,128)(2,1)}, bf16[2,256,1536]{2,1,0:T(8,128)(2,1)}, f32[32,8,128]{2,1,0:T(8,128)}, bf16[16,48,1536]{2,1,0:T(8,128)(2...) custom-call(f32[48,1536]{1,0:T(8,128)} %refs_0_.1, f32[48,256]{1,0:T(8,128)} %refs_1_.1, ...), custom_call_target="tpu_custom_call" | custom-call | bytes 104857600 | tf_op jit(solution)/shard_map/pallas_call | solution.py:305
  80.2 6.2 shard_map.255
  86.4 24.0 %shard_map.256 = (bf16[4,512,256]{2,1,0:T(8,128)(2,1)}, bf16[3,4,96,768]{3,2,1,0:T(8,128)(2,1)}) custom-call(bf16[512,256]{1,0:T(8,128)(2,1)} %get-tuple-element.70.refs_0_, bf16[3,4,96,768]{3,2,1,0:T(8,128)(2,1)} %get-tuple-element.71.refs_1_, bf16[2048,1536]{1,0:T(8,128)(2,1)} %all-gather.4.cloned.1.call-done.refs_2_.c_ref.c_hbm), custom_call_target="tpu_custom_call" | custom-call | bytes 20971520 | tf_op jit(solution)/shard_map/pallas_call | solution.py:224
  112.6 31.0 %shard_map.257 = bf16[4,4,512,256]{3,2,1,0:T(8,128)(2,1)} custom-call(bf16[4,512,256]{2,1,0:T(8,128)(2,1)} %get-tuple-element.72.refs_0_), custom_call_target="tpu_custom_call" | custom-call | bytes 83886080 | tf_op jit(solution)/shard_map/pallas_call | solution.py:224
  143.6 27.5 %shard_map.258 = (f32[512,768]{1,0:T(8,128)}, f32[2,8,256]{2,1,0:T(8,128)}) custom-call(s32[32]{0:T(128)} %fusion.1.slots, s32[2]{0:T(128)} %get-tuple-element.130.tops, bf16[512,768]{1,0:T(8,128)(2,1)} %get-tuple-element.69.q_ref, bf16[32,256,256]{2,1,0:T(8,128)(2,1)} %bitcast.85), custom_call_target="tpu_custom_call" | custom-call | flops 6643777536 | bytes 83886080 | tf_op jit(solution)/shard_map/pallas_call | solution.py:796
  173.3 3.6 fusion.7
  176.9 22.7 %shard_map.259 = (bf16[2,256,1536]{2,1,0:T(8,128)(2,1)}, bf16[3,4,96,384]{3,2,1,0:T(8,128)(2,1)}) custom-call(bf16[2,256,1536]{2,1,0:T(8,128)(2,1)} %get-tuple-element.141.refs_0_, bf16[3,4,96,384]{3,2,1,0:T(8,128)(2,1)} %get-tuple-element.75.refs_1_), custom_call_target="tpu_custom_call" | custom-call | bytes 31457280 | tf_op jit(solution)/shard_map/pallas_call | solution.py:224
  199.9 2.0 multiply_reduce_fusion.2
  203.3 34.0 %shard_map.260 = bf16[8,256,1536]{2,1,0:T(8,128)(2,1)} custom-call(bf16[256,1536]{1,0:T(8,128)(2,1)} %multiply_convert_fusion.refs_0_), custom_call_target="tpu_custom_call" | custom-call | bytes 125829120 | tf_op jit(solution)/shard_map/pallas_call | solution.py:224
  237.3 3.6 all-gather.8.cloned.1.call-done.w_ref
  240.9 43.2 %shard_map.261 = (bf16[2048,768]{1,0:T(8,128)(2,1)}, bf16[2048,768]{1,0:T(8,128)(2,1)}, bf16[2048,768]{1,0:T(8,128)(2,1)}, bf16[2048,1536]{1,0:T(8,128)(2,1)}, bf16[2048,1536]{1,0:T(8,128)(2,1)}) custom-call(bf16[2048,1536]{1,0:T(8,128)(2,1)} %bitcast.81, bf16[2048,1536]{1,0:T(8,128)(2,1)} %all-gather.4.cloned.1.call-done.refs_2_.c_ref.c_hbm, ...), custom_call_target="tpu_custom_call" | custom-call | flops 28991029248 | bytes 41943040 | tf_op jit(solution)/shard_map/pallas_call | solution.py:617
  284.1 21.5 %shard_map.262.refs_2_ = bf16[4,3,384,768]{3,2,1,0:T(8,128)(2,1)} custom-call(bf16[2048,1536]{1,0:T(8,128)(2,1)} %bitcast.82, bf16[2048,1536]{1,0:T(8,128)(2,1)} %all-gather.4.cloned.1.call-done.refs_2_.c_ref.c_hbm, bf16[2048,768]{1,0:T(8,128)(2,1)} %get-tuple-element.81.act_ref, bf16[2048,768]{1,0:T(8,128)(2,1)} %get-tuple-element.82.dgate_ref, ...), custom_call_target="tpu_custom_call" | custom-call | flops 14495514624 | bytes 41943040 | tf_op jit(solution)/shard_map/pallas_call | solution.py:645
  306.1 4.6 all-gather.6.cloned.1.call-done.w_ref
  310.8 28.6 %shard_map.263 = (bf16[2048,384]{1,0:T(8,128)(2,1)}, bf16[2048,384]{1,0:T(8,128)(2,1)}, bf16[2048,384]{1,0:T(8,128)(2,1)}, bf16[2048,1536]{1,0:T(8,128)(2,1)}, bf16[2048,1536]{1,0:T(8,128)(2,1)}) custom-call(bf16[2048,1536]{1,0:T(8,128)(2,1)} %bitcast.83, bf16[2048,1536]{1,0:T(8,128)(2,1)} %all-gather.4.cloned.1.call-done.refs_2_.c_ref.c_hbm, ...), custom_call_target="tpu_custom_call" | custom-call | flops 14495514624 | bytes 41943040 | tf_op jit(solution)/shard_map/pallas_call | solution.py:617
  339.4 38.1 %shard_map.264 = (f32[256,1536]{1,0:T(8,128)}, bf16[4,3,384,384]{3,2,1,0:T(8,128)(2,1)}) custom-call(bf16[8,256,1536]{2,1,0:T(8,128)(2,1)} %bitcast.113, bf16[2048,1536]{1,0:T(8,128)(2,1)} %bitcast.84, bf16[2048,1536]{1,0:T(8,128)(2,1)} %all-gather.4.cloned.1.call-done.refs_2_.c_ref.c_hbm, bf16[2048,384]{1,0:T(8,128)(2,1)} %get-tuple-element.85.act_hbm, ...), custom_call_target="tpu_custom_call" | custom-call | flops 7247757312 | bytes 104857600 | tf_op jit(solution)/shard_map/pallas_call | solution.py:720
  381.5 21.3 %shard_map.265 = bf16[2,256,1536]{2,1,0:T(8,128)(2,1)} custom-call(bf16[256,1536]{1,0:T(8,128)(2,1)} %get-tuple-element.125.refs_0_), custom_call_target="tpu_custom_call" | custom-call | bytes 31457280 | tf_op jit(solution)/shard_map/pallas_call | solution.py:224
  402.8 4.4 convolution_convert_fusion
  407.2 2.3 convolution_convert_fusion.1.do_ref
  409.5 44.5 %shard_map.266 = (bf16[512,768]{1,0:T(8,128)(2,1)}, bf16[32,256,256]{2,1,0:T(8,128)(2,1)}) custom-call(s32[32]{0:T(128)} %fusion.1.slots, s32[2]{0:T(128)} %get-tuple-element.130.tops, bf16[512,768]{1,0:T(8,128)(2,1)} %get-tuple-element.69.q_ref, bf16[32,256,256]{2,1,0:T(8,128)(2,1)} %bitcast.86, bf16[512,768]{1,0:T(8,128)(2,1)} %convolution_convert_fusion.1.do_ref, ...), custom_call_target="tpu_custom_call" | custom-call | flops 16609443840 | bytes 125829120 | tf_op jit(solution)/shard_map/pallas_call | solution.py:884
  454.0 49.0 %shard_map.267 = (bf16[512,256]{1,0:T(8,128)(2,1)}, f32[48,1536]{1,0:T(8,128)}, bf16[4,3,384,384]{3,2,1,0:T(8,128)(2,1)}) custom-call(bf16[16,512,256]{2,1,0:T(8,128)(2,1)} %bitcast.87, bf16[16,48,1536]{2,1,0:T(8,128)(2,1)} %bitcast.89, bf16[4,3,384,384]{3,2,1,0:T(8,128)(2,1)} %get-tuple-element.92.refs_2_), custom_call_target="tpu_custom_call", output_to_operand_aliasing={{2}: (2, {})} | custom-call | bytes 131072000 | tf_op jit(solution)/shard_map/pallas_call | solution.py:472
  503.0 9.0 %shard_map.268 = (bf16[16,2,48,1024]{3,2,1,0:T(8,128)(2,1)}, bf16[512,1536]{1,0:T(8,128)(2,1)}, f32[1,1536]{1,0:T(1,128)}, f32[1,1024]{1,0:T(1,128)}) custom-call(bf16[512,768]{1,0:T(8,128)(2,1)} %get-tuple-element.90.dq_ref, bf16[512,256]{1,0:T(8,128)(2,1)} %get-tuple-element.93.dkv_ref, bf16[512,1536]{1,0:T(8,128)(2,1)} %get-tuple-element.94.normed_ref, ...), custom_call_target="tpu_custom_call" | custom-call | flops 3221225472 | bytes 16777216 | tf_op jit(solution)/shard_map/pallas_call | solution.py:1004
  515.6 69.1 %shard_map.269 = (f32[2,48,1024]{2,1,0:T(8,128)}, f32[8,128]{1,0:T(8,128)}, f32[256,1536]{1,0:T(8,128)}, f32[256,1536]{1,0:T(8,128)}) custom-call(bf16[16,2,48,1024]{3,2,1,0:T(8,128)(2,1)} %get-tuple-element.95.refs_0_, f32[32,8,128]{2,1,0:T(8,128)} %bitcast.98, bf16[2,256,1536]{2,1,0:T(8,128)(2,1)} %bitcast.93, bf16[8,256,1536]{2,1,0:T(8,128)(2,1)} %bitcast.80, ...), custom_call_target="tpu_custom_call" | custom-call | bytes 222822400 | tf_op jit(solution)/shard_map/pallas_call | solution.py:472
  587.3 31.3 %shard_map.270 = (bf16[3,4,96,768]{3,2,1,0:T(8,128)(2,1)}, bf16[3,4,96,384]{3,2,1,0:T(8,128)(2,1)}) custom-call(bf16[3,4,96,768]{3,2,1,0:T(8,128)(2,1)} %bitcast.79, bf16[3,4,96,384]{3,2,1,0:T(8,128)(2,1)} %bitcast.96, f32[2,48,1024]{2,1,0:T(8,128)} %get-tuple-element.100.refs_2_.refs_0_), custom_call_target="tpu_custom_call" | custom-call | tf_op jit(solution)/shard_map/pallas_call | solution.py:507
  618.6 7.5 %shard_map.271 = (f32[48,1536]{1,0:T(8,128)}, f32[48,256]{1,0:T(8,128)}, f32[48,256]{1,0:T(8,128)}, bf16[256,1536]{1,0:T(8,128)(2,1)}, bf16[256,1536]{1,0:T(8,12...) custom-call(f32[2,48,1024]{2,1,0:T(8,128)} %get-tuple-element.100.refs_2_.refs_0_, ...), custom_call_target="tpu_custom_call" | custom-call | bytes 20971520 | tf_op jit(solution)/shard_map/pallas_call | solution.py:562
  (90 shorter events, 28.6 us)
Async XLA Ops:
  7.2 79.2 %all-gather.4.cloned.1.call-start = ((), (), s32[]{:S(2)}) async-start(), calls=%async_computation.2 | async-start | bytes 7077888 | tf_op jit(solution)/shard_map/all_gather | solution.py:1130
  7.9 233.0 %all-gather.8.cloned.1.call-start = ((), (), s32[]{:S(2)}) async-start(), calls=%async_computation.4 | async-start | bytes 8847360 | tf_op jit(solution)/shard_map/all_gather | solution.py:1080
  11.9 64.2 %copy-start.8 = (s32[1,32]{1,0:T(1,128)S(1)}, s32[1,32]{1,0:T(1,128)}, u32[]{:S(2)}) copy-start(s32[1,32]{1,0:T(1,128)} %param.17) | copy-start | bytes 388
  110.4 200.4 %all-gather.6.cloned.1.call-start = ((), (), s32[]{:S(2)}) async-start(), calls=%async_computation.3 | async-start | bytes 4423680 | tf_op jit(solution)/shard_map/all_gather | solution.py:1080
  171.2 2.1 copy-start.4
  176.9 23.0 %copy-start.1 = (bf16[256,1536]{1,0:T(8,128)(2,1)S(1)}, bf16[256,1536]{1,0:T(8,128)(2,1)}, u32[]{:S(2)}) copy-start(bf16[256,1536]{1,0:T(8,128)(2,1)} %refs_4_.3) | copy-start | bytes 2359300
  199.6 316.0 %reduce-scatter.3.cloned.1.call-start = ((), (), s32[]{:S(2)}) async-start(), calls=%async_computation.5 | async-start | bytes 8847360 | tf_op jit(solution)/shard_map/reduce_scatter | solution.py:1188
  202.0 177.6 %copy-start = (f32[256,1536]{1,0:T(8,128)}, f32[256,1536]{1,0:T(8,128)S(1)}, u32[]{:S(2)}) copy-start(f32[256,1536]{1,0:T(8,128)S(1)} %get-tuple-element.128.refs_5_) | copy-start | bytes 4718596
  305.7 281.6 %reduce-scatter.5.cloned.1.call-start = ((), (), s32[]{:S(2)}) async-start(), calls=%async_computation.6 | async-start | bytes 4423680 | tf_op jit(solution)/shard_map/reduce_scatter | solution.py:1188
  377.5 2.1 copy-start.2
  377.5 2.1 copy-start.3
  402.8 4.4 copy-start.5
  402.8 4.4 copy-start.6
  618.6 7.5 %copy-start.7 = (f32[48,1536]{1,0:T(8,128)S(1)}, f32[48,1536]{1,0:T(8,128)}, u32[]{:S(2)}) copy-start(f32[48,1536]{1,0:T(8,128)} %get-tuple-element.172) | copy-start | bytes 884740
Sparse Core Ops, SparseCore 0:
  9.9 63.7 all-gather.3
  110.5 130.3 all-gather.7
  242.5 68.2 all-gather.5
  312.9 122.0 reduce-scatter.2
  503.1 80.2 reduce-scatter.4

commit v5 on v4

--- a/solution.py
+++ b/solution.py
@@ -140,7 +140,7 @@
     )
 
 
-def gather_kernel(plans, sizes, swap_count, waited, carried, *refs, ahead=None):
+def gather_kernel(plans, sizes, swap_count, waited, carried, *refs, ahead=None, behind=None):
     count = max(p[0] for p in plans) + 1
     xs, refs = refs[:count], refs[count:]
     swap_xs, refs = refs[:swap_count], refs[swap_count + waited :]
@@ -160,6 +160,10 @@
         i, rows, layout, phases, split = plan
         return cut(xs[i].at[place] if split else xs[i], rows)
 
+    def landed(slot, number):
+        axis = plans[0][3][0]
+        return remote(slot, slot, send_sems.at[number], recv_sems.at[number], axis, 0, sizes)
+
     sends, kept, queue = [], [], []
     sem = 0
     for j, plan in enumerate(plans):
@@ -170,6 +174,7 @@
         queue.append((plan, {}, -1, None))
         kept.append(copy)
     at = 0
+    ends = []
     while at < len(queue):
         plan, offsets, phase, arrived = queue[at]
         at += 1
@@ -179,9 +184,7 @@
             src = source(plan, lax.axis_index(phases[0]))
         else:
             src = slot
-            remote(
-                slot, slot, send_sems.at[arrived], recv_sems.at[arrived], phases[0], 0, sizes
-            ).wait_recv()
+            landed(slot, arrived).wait_recv()
         for p in range(phase + 1, len(phases)):
             a = phases[p]
             for d in range(1, sizes[a]):
@@ -193,13 +196,20 @@
                 sends.append(copy)
                 later = dict(offsets)
                 later[a] = sizes[a] - d
-                queue.append((plan, later, p, sem))
+                if p + 1 < len(phases):
+                    queue.append((plan, later, p, sem))
+                else:
+                    ends.append((plan, later, sem))
                 sem += 1
         if at == len(plans):
             if ahead is not None:
                 ahead()
             for copy in kept + swaps:
                 copy.start()
+            if behind is not None:
+                behind()
+    for (i, rows, layout, phases, split), offsets, arrived in ends:
+        landed(cut(outs[i].at[place_of(offsets, layout, sizes)], rows), arrived).wait_recv()
     for copy in kept + swaps:
         copy.wait()
     for copy in sends:
@@ -655,8 +665,10 @@
     )(tokens, cot, act, dgate, dup)
 
 
-def grads_kernel(plans, sizes, dtok_ref, t_hbm, c_hbm, act_hbm, dgate_hbm, dup_hbm, *refs):
-    sum_ref, grad_hbm, left_s, right_s, made_s, load_sems, made_sems = refs[:7]
+def grads_kernel(plans, sizes, dtok_ref, mixed_ref, cot_ref, gain_ref, *refs):
+    t_hbm, c_hbm, act_hbm, dgate_hbm, dup_hbm = refs[:5]
+    dmixed_ref, dproj_ref, gain_grad_ref, grad_hbm = refs[5:9]
+    sum_ref, left_s, right_s, made_s, load_sems, made_sems = refs[9:15]
     per, rows = made_s.shape[1:3]
     cols = per * rows
     loads = [
@@ -705,12 +717,22 @@
             loads[4].wait()
             some(2, 0, chunks, 1, 0, False)
 
-    scatter_kernel(plans, sizes, dtok_ref, sum_ref, *refs[7:], between=between)
+    scatter_kernel(plans, sizes, dtok_ref, sum_ref, *refs[15:], between=between)
+    mixed, dnormed = mixed_ref[...], sum_ref[...]
+    scale = inverse_rms(mixed)
+    z = mixed * scale
+    u = gain_ref[...] * dnormed
+    gain_grad_ref[...] = jnp.sum(dnormed * z, axis=0, keepdims=True)
+    dmixed = cot_ref[...].astype(F32) + scale * (
+        u - z * jnp.mean(z * u, axis=-1, keepdims=True)
+    )
+    dmixed_ref[...] = dmixed
+    dproj_ref[...] = dmixed.astype(BF)
     for slot in range(2):
         stored(2, slot, slot).wait()
 
 
-def feed_grads(dtok, tokens, cot, act, dgate, dup, places, plans, sizes, collective_id):
+def feed_grads(dtok, mixed, cot_own, gain, tokens, cot, act, dgate, dup, places, plans, sizes, collective_id):
     plans = alive(plans, sizes)
     n, width = act.shape
     rows = D // places
@@ -721,11 +743,14 @@
         functools.partial(grads_kernel, plans, sizes),
         out_shape=[
             jax.ShapeDtypeStruct(dtok.shape[1:], F32),
+            jax.ShapeDtypeStruct(dtok.shape[1:], BF),
+            jax.ShapeDtypeStruct((1, D), F32),
             jax.ShapeDtypeStruct((places, 3, rows, width), BF),
         ],
-        in_specs=[spec] + [far] * 5,
-        out_specs=[spec, far],
+        in_specs=[spec] * 4 + [far] * 5,
+        out_specs=[spec] * 3 + [far],
         scratch_shapes=[
+            pltpu.VMEM(dtok.shape[1:], F32),
             pltpu.VMEM((2, n, D), BF),
             pltpu.VMEM((2, n, width), BF),
             pltpu.VMEM((2, per, rows, width), BF),
@@ -739,7 +764,7 @@
         cost_estimate=pl.CostEstimate(
             flops=6 * n * D * width, bytes_accessed=100 * 2**20, transcendentals=0
         ),
-    )(dtok, tokens, cot, act, dgate, dup)
+    )(dtok, mixed, cot_own, gain, tokens, cot, act, dgate, dup)
 
 
 def forward_kernel(heads, slots, tops, q_ref, kv_ref, o_ref, lse_ref, top_s, sum_s, acc_s):
@@ -913,7 +938,8 @@
     return value * cosine + pltpu.roll(value, HEAD_DIM // 2, 1) * sine
 
 
-def project_kernel(x_ref, w_ref, gain_ref, bias_ref, cos_ref, sin_ref, q_ref, kv_ref, normed_ref):
+def project_kernel(plans, sizes, x_ref, w_ref, gain_ref, bias_ref, cos_ref, sin_ref, *refs):
+    packed_ref, _, kv_all_ref, swapped_ref, q_ref, normed_ref, kv_s = refs[:7]
     x = x_ref[...].astype(F32)
     normed_ref[...] = (x * inverse_rms(x) * gain_ref[...]).astype(BF)
     cosine, sine = cos_ref[...], sin_ref[...]
@@ -923,34 +949,53 @@
         cols = slice(low * HEAD_DIM, (low + n) * HEAD_DIM)
         return dot_nn(normed_ref[...], w_ref[:, cols]) + bias_ref[:, cols]
 
-    for low in range(0, heads, 2):
-        made = product(low, 2)
-        for i in range(2):
-            part = made[:, i * HEAD_DIM : (i + 1) * HEAD_DIM]
-            q_ref[:, (low + i) * HEAD_DIM : (low + i + 1) * HEAD_DIM] = turned(
-                part, cosine, sine
-            ).astype(BF)
     made = product(heads, 2)
-    kv_ref[:, :HEAD_DIM] = turned(made[:, :HEAD_DIM], cosine, sine).astype(BF)
-    kv_ref[:, HEAD_DIM:] = made[:, HEAD_DIM:].astype(BF)
-
-
-def project(x, w, gain, bias, cosine, sine):
+    kv_s[:, :HEAD_DIM] = turned(made[:, :HEAD_DIM], cosine, sine).astype(BF)
+    kv_s[:, HEAD_DIM:] = made[:, HEAD_DIM:].astype(BF)
+
+    def queries():
+        for low in range(0, heads, 2):
+            made = product(low, 2)
+            for i in range(2):
+                part = made[:, i * HEAD_DIM : (i + 1) * HEAD_DIM]
+                q_ref[:, (low + i) * HEAD_DIM : (low + i + 1) * HEAD_DIM] = turned(
+                    part, cosine, sine
+                ).astype(BF)
+
+    gather_kernel(
+        plans, sizes, 1, 0, 0, kv_s, packed_ref, kv_all_ref, swapped_ref, *refs[7:], behind=queries
+    )
+
+
+def project(x, w, gain, bias, cosine, sine, packed, after, plans, sizes, collective_id):
+    plans = alive(plans, sizes)
     n, width = x.shape[0], w.shape[1]
     spec = pl.BlockSpec(memory_space=pltpu.VMEM)
+    far = pl.BlockSpec(memory_space=pl.ANY)
+    count = int(np.prod([sizes[a] for a in plans[0][2]]))
+    kv = (n, 2 * HEAD_DIM)
     return pl.pallas_call(
-        project_kernel,
-        in_specs=[spec] * 6,
-        out_specs=[spec] * 3,
+        functools.partial(project_kernel, plans, sizes),
+        in_specs=[spec] * 6 + [far] * 2,
+        out_specs=[spec, far, spec, spec],
         out_shape=[
-            jax.ShapeDtypeStruct((n, k), BF)
-            for k in (width - 2 * HEAD_DIM, 2 * HEAD_DIM, D)
+            jax.ShapeDtypeStruct(s, BF)
+            for s in ((count,) + kv, packed.shape, (n, width - 2 * HEAD_DIM), (n, D))
         ],
-        compiler_params=pltpu.CompilerParams(vmem_limit_bytes=VMEM_LIMIT),
+        scratch_shapes=[
+            pltpu.VMEM(kv, BF),
+            pltpu.SemaphoreType.DMA((count - 1,)),
+            pltpu.SemaphoreType.DMA((count - 1,)),
+            pltpu.SemaphoreType.DMA((1,)),
+        ]
+        + swap_scratch([packed]),
+        compiler_params=pltpu.CompilerParams(
+            collective_id=collective_id, has_side_effects=True, vmem_limit_bytes=VMEM_LIMIT
+        ),
         cost_estimate=pl.CostEstimate(
-            flops=2 * n * D * width, bytes_accessed=12 * 2**20, transcendentals=0
-        ),
-    )(x, w, gain, bias, cosine, sine)
+            flops=2 * n * D * width, bytes_accessed=80 * 2**20, transcendentals=0
+        ),
+    )(x, w, gain, bias, cosine, sine, packed, after)
 
 
 def project_back_kernel(
@@ -961,12 +1006,18 @@
     w_ref,
     cos_ref,
     sin_ref,
+    back_ref,
     grad_ref,
     dnormed_ref,
     gain_grad_ref,
     bias_grad_ref,
+    swapped_ref,
     dpre_s,
+    *sems,
 ):
+    (item,) = swaps_of([back_ref], [swapped_ref], sems)
+    greet(("y", "c"), {"y": 2, "c": 2}, True)
+    item.start()
     cosine, sine = cos_ref[...], -sin_ref[...]
     heads = dq_ref.shape[1] // HEAD_DIM
     for h in range(heads + 1):
@@ -994,36 +1045,96 @@
             made = dot_tn(normed_ref[:, low : low + step], dpre_s[...]).astype(BF)
             half, start = divmod(low // rows, blk)
             grad_ref[start : start + step // rows, half] = made.reshape(step // rows, rows, width)
-
-
-def project_back(dq, dkv, normed, x, w, cosine, sine, blk, rows):
+    item.wait()
+
+
+def project_back(dq, dkv, normed, x, w, cosine, sine, back, blk, rows, collective_id):
     n, width = x.shape[0], w.shape[1]
     split = rows % 16 == 0
     made = (blk, 2, rows, width) if split else (D, width)
     spec = pl.BlockSpec(memory_space=pltpu.VMEM)
+    far = pl.BlockSpec(memory_space=pl.ANY)
     return pl.pallas_call(
         project_back_kernel,
-        in_specs=[spec] * 7,
-        out_specs=[spec] * 4,
+        in_specs=[spec] * 7 + [far],
+        out_specs=[spec] * 4 + [far],
         out_shape=[
             jax.ShapeDtypeStruct(made, BF),
             jax.ShapeDtypeStruct((n, D), BF),
             jax.ShapeDtypeStruct((1, D), F32),
             jax.ShapeDtypeStruct((1, width), F32),
+            jax.ShapeDtypeStruct(back.shape, back.dtype),
         ],
-        scratch_shapes=[pltpu.VMEM((n, width), BF)],
-        compiler_params=pltpu.CompilerParams(vmem_limit_bytes=VMEM_LIMIT),
+        scratch_shapes=[pltpu.VMEM((n, width), BF)] + swap_scratch([back]),
+        compiler_params=pltpu.CompilerParams(
+            collective_id=collective_id, has_side_effects=True, vmem_limit_bytes=VMEM_LIMIT
+        ),
         cost_estimate=pl.CostEstimate(
             flops=4 * n * D * width, bytes_accessed=16 * 2**20, transcendentals=0
         ),
-    )(dq, dkv, normed, x, w, cosine, sine)
-
-
-def small_rows(*rows):
-    return jnp.stack(
-        [jnp.pad(r.astype(F32), ((0, LANES - r.shape[0]),)) for r in rows]
-        + [jnp.zeros((LANES,), F32)] * (8 - len(rows))
-    )
+    )(dq, dkv, normed, x, w, cosine, sine, back)
+
+
+def exchange_back_kernel(sizes, dproj_ref, w_ref, attn_ref, dout_ref, o_ref, pair_s, sum_s, *sems):
+    send_sems, recv_sems = sems
+    greet(("head",), sizes)
+    me, count = lax.axis_index("head"), sizes["head"]
+    tok = dproj_ref.shape[0]
+    copies = []
+    for d in range(1, count):
+        copy = remote(
+            dproj_ref, pair_s.at[me], send_sems.at[d - 1], recv_sems.at[d - 1], "head", d, sizes
+        )
+        copy.start()
+        copies.append(copy)
+    cols = 2 * LANES
+
+    def use(place, grads, fresh, last):
+        rows = pl.ds(pl.multiple_of(place * tok, tok), tok)
+        for low in range(0, w_ref.shape[0], cols):
+            part = slice(low, low + cols)
+            dout_ref[rows, part] = dot_nt(grads, w_ref[part, :]).astype(BF)
+            made = dot_tn(attn_ref[rows, part], grads)
+            if not fresh:
+                made = made + sum_s[part, :]
+            if last:
+                o_ref[part, :] = made.astype(BF)
+            else:
+                sum_s[part, :] = made
+
+    use(me, dproj_ref[...], True, count == 1)
+    for d in range(1, count):
+        copies[d - 1].wait_recv()
+        place = lax.rem(me + count - d, count)
+        use(place, pair_s[place], False, d == count - 1)
+    for copy in copies:
+        copy.wait_send()
+
+
+def exchange_back(dproj, w, attn, sizes, collective_id):
+    spec = pl.BlockSpec(memory_space=pltpu.VMEM)
+    count = sizes["head"]
+    return pl.pallas_call(
+        functools.partial(exchange_back_kernel, sizes),
+        in_specs=[spec] * 3,
+        out_specs=[spec] * 2,
+        out_shape=[
+            jax.ShapeDtypeStruct(attn.shape, BF),
+            jax.ShapeDtypeStruct(w.shape, BF),
+        ],
+        scratch_shapes=[
+            pltpu.VMEM((count,) + dproj.shape, BF),
+            pltpu.VMEM(w.shape, F32),
+            pltpu.SemaphoreType.DMA((count - 1,)),
+            pltpu.SemaphoreType.DMA((count - 1,)),
+        ],
+        compiler_params=pltpu.CompilerParams(
+            collective_id=collective_id, has_side_effects=True, vmem_limit_bytes=VMEM_LIMIT
+        ),
+        cost_estimate=pl.CostEstimate(
+            flops=4 * w.size * attn.shape[0], bytes_accessed=40 * 2**20, transcendentals=0
+        ),
+    )(dproj, w, attn)
 
 
 def shards(
@@ -1066,9 +1177,8 @@
     q_cols = D // 2
     kv_cols = HEAD_DIM
     rows = q_weight.shape[0]
-    small = small_rows(
-        *[v.astype(BF) for v in (norm1, norm2, q_bias, k_bias, v_bias)]
-    )
+    small = jnp.concatenate([v.astype(BF) for v in (norm1, norm2, q_bias, k_bias, v_bias)])
+    small = jnp.pad(small.astype(F32), (0, 8 * LANES - small.shape[0])).reshape(8, LANES)
     parts = sizes["y"] * sizes["c"]
     width = gate_weight.shape[1]
     lanes = -(-width // (LANES * parts)) * LANES
@@ -1098,25 +1208,34 @@
     w_out = w_out.reshape(q_cols, D)
     w_qkv = w_qkv.reshape(D, q_cols + 2 * kv_cols)
     x_pair = x_pair.reshape(pair, D)
-    gain_one = small_all[:, 0, :rows].reshape(D)
-    gain_two = small_all[:, 1, :rows].reshape(D)
-    bias_q = lax.dynamic_slice_in_dim(small_all[:, 2, :rows].reshape(D), head * q_cols, q_cols)
-    bias_k, bias_v = (
-        lax.dynamic_slice_in_dim(
-            small_all[:, i, : k_bias.shape[0]].reshape(2 * kv_cols), head * kv_cols, kv_cols
-        )
-        for i in (3, 4)
-    )
-
-    queries, kv_local, normed = project(
+    small_all = small_all.reshape(-1, 8 * LANES)
+    kn = k_bias.shape[0]
+    long = small_all[:, : 3 * rows].reshape(-1, 3, rows).transpose(1, 0, 2).reshape(3, D)
+    short = small_all[:, 3 * rows : 3 * rows + 2 * kn].reshape(-1, 2, kn)
+    short = short.transpose(1, 0, 2).reshape(2, 2 * kv_cols)
+    gain_one, gain_two = long[:1], long[1:2]
+    bias = jnp.concatenate(
+        [
+            lax.dynamic_slice_in_dim(v, head * n, n)
+            for v, n in ((long[2], q_cols), (short[0], kv_cols), (short[1], kv_cols))
+        ]
+    )[None]
+    far_axes, near_axes = place_axes[:2], place_axes[2:]
+    group = ("head", "y", "c")
+    cot_all = lax.all_gather(cotangent, group, axis=0, tiled=True)
+    kv, mine_one, queries, normed = project(
         x_pair,
         w_qkv,
-        gain_one[None],
-        jnp.concatenate([bias_q, bias_k, bias_v])[None],
+        gain_one,
+        bias,
         cosine,
         sine,
-    )
-    group = ("head", "y", "c")
+        packed_one,
+        cot_all,
+        [(0, None, far_axes, far_axes, False)],
+        sizes,
+        2,
+    )
     half = tok // 2
     crossed = [
         ((0, half), group, ("head", "y", "c"), False),
@@ -1126,16 +1245,6 @@
         ((0, half), group, ("c", "head", "y"), False),
         ((half, half), group, ("c", "y", "head"), False),
     ]
-    far_axes, near_axes = place_axes[:2], place_axes[2:]
-    cot_all = lax.all_gather(cotangent, group, axis=0, tiled=True)
-    kv, mine_one = gather(
-        [kv_local],
-        [(0, None, far_axes, far_axes, False)],
-        sizes,
-        2,
-        [packed_one],
-        [cot_all],
-    )
     w_feed_one = along_z(mine_one)
     if near_axes:
         (kv,) = gather([kv], [(0, None, near_axes, near_axes, False)], sizes, 10)
@@ -1172,8 +1281,11 @@
     act, dgate, dup, branch, dtokens = feed(
         tokens, cot_all, w_feed_two, (branch, dtokens), (parts_one,)
     )
-    dnormed_two, parts_two = feed_grads(
+    dmixed, dproj, norm2_part, parts_two = feed_grads(
         dtokens.reshape(-1, tok, D),
+        mixed,
+        cotangent,
+        gain_two,
         tokens,
         cot_all,
         act,
@@ -1190,17 +1302,7 @@
 
     back_one = collect(parts_one)
 
-    z_two = mixed * scale_two
-    u_two = gain_two * dnormed_two
-    norm2_part = jnp.sum(dnormed_two * z_two, axis=0)
-    dmixed = cotangent.astype(F32) + scale_two * (
-        u_two - z_two * jnp.mean(z_two * u_two, axis=-1, keepdims=True)
-    )
-    dproj = dmixed.astype(BF)
-    (dproj_pair,) = gather([dproj], [(0, None, ("head",), ("head",), False)], sizes, 6)
-    dproj_pair = dproj_pair.reshape(pair, D)
-    dout = dot_nt(dproj_pair, w_out).astype(BF)
-    o_part = dot_tn(attn_local, dproj_pair).astype(BF)
+    dout, o_part = exchange_back(dproj, w_out, attn_local, sizes, 6)
 
     dq, dkv_parts = attend_back(slots, tops, queries, kv, dout, lse, attended)
     dkv, d_out_weight, parts_two = scatter(
@@ -1215,8 +1317,8 @@
         carried=[parts_two],
     )
     back_two = collect(parts_two)
-    w_part, dnormed, norm1_part, bias_part = project_back(
-        dq, dkv, normed, x_pair, w_qkv, cosine, sine, blk, rows
+    w_part, dnormed, norm1_part, bias_part, back_one = project_back(
+        dq, dkv, normed, x_pair, w_qkv, cosine, sine, back_one, blk, rows, 11
     )
     if w_part.ndim == 2:
         w_part = w_part.reshape(2, blk, rows, -1).transpose(1, 0, 2, 3)
@@ -1234,7 +1336,7 @@
             jnp.pad(part, ((0, 0), (0, 0), (0, LANES - part.shape[2])))
             for part in (
                 owners(norm1_part),
-                owners(norm2_part),
+                owners(norm2_part[0]),
                 owned(bias_part[:q_cols]),
                 owned(bias_part[q_cols : q_cols + kv_cols]),
                 owned(bias_part[q_cols + kv_cols :]),
@@ -1260,7 +1362,6 @@
         [F32] * 4,
         sizes,
         8,
-        [back_one],
     )
     d_query, d_key, d_value, output, hidden_grad, d_down, d_gate, d_up = write_outputs(
         w_grads,
@@ -1269,11 +1370,10 @@
         dmixed,
         hidden,
         mixed,
-        gain_one[None],
-        swap([back_one, back_two], w_grads, 9),
+        gain_one,
+        [back_one] + list(swap([back_two], w_grads, 9)),
         width,
     )
-    kn = k_bias.shape[0]
     return (
         output,
         hidden_grad,

time: 642 us -> 626 us (0.975)
  matrix products: 10.2 us -> 3.57 us
    pallas_call x2 -> x3, Pallas kernels: 15.2 us -> 79.2 us  [the longest x1 27.6 us: project(): pl.pallas_call(functools.partial(project_kernel, plans, sizes), in_specs=...]
    pallas_call x5 -> x3, Pallas kernels: 133 us -> 87.8 us  [gather(): pl.pallas_call(functools.partial(gather_kernel, plans, sizes, len(swaps),...]
    pallas_call x1, Pallas kernels: 31.3 us -> 12.3 us  [swap(): pl.pallas_call(functools.partial(swap_kernel, n), out_shape=[jax.ShapeDty...]
    pallas_call x2, Pallas kernels: 118 us -> 111 us  [scatter(): pl.pallas_call(functools.partial(scatter_and_wait_kernel, plans, sizes, l...]
    dot_general x2 -> x0, matrix products: 6.67 us -> none  [the longest x1 4.37 us: dot_tn(): lax.dot_general(a, b, (((0,), (0,)), ((), ())), preferred_element_type=F32)]
  transfers between devices with their start and end apart: 5 -> 5, of which waited for: 2 -> 2; matrix products, arithmetic and copies ran while one was open for 6% -> 4% of each run, Pallas kernels for 80% -> 84%
where the time goes in v5:
time: 626 us; the launch traced here: 618 us
  Pallas kernels  565 us (90%)
  other arithmetic  15.1 us (2%)
  between operations  14.3 us (2%)
  local copies, waits for them, and re-layouts  10.6 us (2%)
  waiting for transfers between devices  8.38 us (1%)
    pallas_call x2, Pallas kernels, scatter(): pl.pallas_call(functools.partial(scatter_and_wait_kernel, plans, sizes, l...  111 us
    pallas_call x3, Pallas kernels, gather(): pl.pallas_call(functools.partial(gather_kernel, plans, sizes, len(swaps),...  87.8 us
    pallas_call x2, Pallas kernels, feed(): pl.pallas_call(functools.partial(feed_kernel, chunks, len(before)), grid=...  71.8 us
    pallas_call x1, Pallas kernels, front(): pl.pallas_call(functools.partial(front_kernel, plans, sizes), out_shape=s...  61.6 us
    pallas_call x1, Pallas kernels, attend_back(): pl.pallas_call(functools.partial(backward_kernel, heads), grid_spec=pltpu...  44.7 us
    pallas_call x1, Pallas kernels, feed_grads(): pl.pallas_call(functools.partial(grads_kernel, plans, sizes), out_shape=[...  39.9 us
    pallas_call x1, Pallas kernels, project(): pl.pallas_call(functools.partial(project_kernel, plans, sizes), in_specs=...  27.6 us
    pallas_call x1, Pallas kernels, attend(): pl.pallas_call(functools.partial(forward_kernel, heads), grid_spec=pltpu....  27.5 us
  transfers between devices with their start and end apart: 5, of which 2 were waited for; matrix products, arithmetic and copies ran while one was open for 4% of the time, Pallas kernels for 84%

profile of v5, /device:TPU:0, one launch (start us, length us, event | category | flops | bytes accessed | tf_op | source)
XLA Modules:
  0.0 617.5 jit_solution(12600297063506092111)
XLA Ops:
  12.0 61.6 %shard_map.254 = (bf16[32,48,1024]{2,1,0:T(8,128)(2,1)}, bf16[2,256,1536]{2,1,0:T(8,128)(2,1)}, f32[32,8,128]{2,1,0:T(8,128)}, bf16[16,48,1536]{2,1,0:T(8,128)(2...) custom-call(f32[48,1536]{1,0:T(8,128)} %refs_0_.1, f32[48,256]{1,0:T(8,128)} %refs_1_.1, ...), custom_call_target="tpu_custom_call" | custom-call | bytes 104857600 | tf_op jit(solution)/shard_map/pallas_call | solution.py:315
  79.4 27.6 %shard_map.255 = (bf16[4,512,256]{2,1,0:T(8,128)(2,1)}, bf16[3,4,96,768]{3,2,1,0:T(8,128)(2,1)}, bf16[512,768]{1,0:T(8,128)(2,1)}, bf16[512,1536]{1,0:T(8,128)(2,1)}) custom-call(bf16[512,1536]{1,0:T(8,128)(2,1)} %bitcast.85, bf16[1536,1024]{1,0:T(8,128)(2,1)} %bitcast.78, f32[1,1536]{1,0:T(1,128)} %slice.59.gain_ref.refs_6_, f32[1,1024]{1,0:T(1,128)} %bitcast.104, ...), custom_call_target="tpu_custom_call" | custom-call | flops 1610612736 | bytes 83886080 | tf_op jit(solution)/shard_map/pallas_call | solution.py:977
  107.2 1.6 sort.17
  109.3 31.0 %shard_map.256 = bf16[4,4,512,256]{3,2,1,0:T(8,128)(2,1)} custom-call(bf16[4,512,256]{2,1,0:T(8,128)(2,1)} %get-tuple-element.73.refs_0_), custom_call_target="tpu_custom_call" | custom-call | bytes 83886080 | tf_op jit(solution)/shard_map/pallas_call | solution.py:234
  140.3 27.5 %shard_map.257 = (f32[512,768]{1,0:T(8,128)}, f32[2,8,256]{2,1,0:T(8,128)}) custom-call(s32[32]{0:T(128)} %fusion.1.slots, s32[2]{0:T(128)} %get-tuple-element.128.tops, bf16[512,768]{1,0:T(8,128)(2,1)} %get-tuple-element.72.q_ref, bf16[32,256,256]{2,1,0:T(8,128)(2,1)} %bitcast.75), custom_call_target="tpu_custom_call" | custom-call | flops 6643777536 | bytes 83886080 | tf_op jit(solution)/shard_map/pallas_call | solution.py:821
  167.8 1.6 convert_element_type.68.attn_ref
  170.0 3.6 fusion.7
  173.5 22.7 %shard_map.258 = (bf16[2,256,1536]{2,1,0:T(8,128)(2,1)}, bf16[3,4,96,384]{3,2,1,0:T(8,128)(2,1)}) custom-call(bf16[2,256,1536]{2,1,0:T(8,128)(2,1)} %get-tuple-element.142.refs_0_, bf16[3,4,96,384]{3,2,1,0:T(8,128)(2,1)} %get-tuple-element.76.refs_1_), custom_call_target="tpu_custom_call" | custom-call | bytes 31457280 | tf_op jit(solution)/shard_map/pallas_call | solution.py:234
  196.6 2.0 multiply_reduce_fusion
  199.9 34.1 %shard_map.259 = bf16[8,256,1536]{2,1,0:T(8,128)(2,1)} custom-call(bf16[256,1536]{1,0:T(8,128)(2,1)} %multiply_convert_fusion.refs_0_), custom_call_target="tpu_custom_call" | custom-call | bytes 125829120 | tf_op jit(solution)/shard_map/pallas_call | solution.py:234
  234.0 3.6 all-gather.8.cloned.1.call-done.w_ref
  237.6 43.2 %shard_map.260 = (bf16[2048,768]{1,0:T(8,128)(2,1)}, bf16[2048,768]{1,0:T(8,128)(2,1)}, bf16[2048,768]{1,0:T(8,128)(2,1)}, bf16[2048,1536]{1,0:T(8,128)(2,1)}, bf16[2048,1536]{1,0:T(8,128)(2,1)}) custom-call(bf16[2048,1536]{1,0:T(8,128)(2,1)} %bitcast.70, bf16[2048,1536]{1,0:T(8,128)(2,1)} %all-gather.4.cloned.1.call-done.refs_1_.c_ref, ...), custom_call_target="tpu_custom_call" | custom-call | flops 28991029248 | bytes 41943040 | tf_op jit(solution)/shard_map/pallas_call | solution.py:627
  280.8 21.5 %shard_map.261.refs_2_ = bf16[4,3,384,768]{3,2,1,0:T(8,128)(2,1)} custom-call(bf16[2048,1536]{1,0:T(8,128)(2,1)} %bitcast.71, bf16[2048,1536]{1,0:T(8,128)(2,1)} %all-gather.4.cloned.1.call-done.refs_1_.c_ref, bf16[2048,768]{1,0:T(8,128)(2,1)} %get-tuple-element.82.act_ref, bf16[2048,768]{1,0:T(8,128)(2,1)} %get-tuple-element.83.dgate_ref, ...), custom_call_target="tpu_custom_call" | custom-call | flops 14495514624 | bytes 41943040 | tf_op jit(solution)/shard_map/pallas_call | solution.py:655
  303.5 4.0 all-gather.6.cloned.1.call-done.w_ref
  307.5 28.6 %shard_map.262 = (bf16[2048,384]{1,0:T(8,128)(2,1)}, bf16[2048,384]{1,0:T(8,128)(2,1)}, bf16[2048,384]{1,0:T(8,128)(2,1)}, bf16[2048,1536]{1,0:T(8,128)(2,1)}, bf16[2048,1536]{1,0:T(8,128)(2,1)}) custom-call(bf16[2048,1536]{1,0:T(8,128)(2,1)} %bitcast.72, bf16[2048,1536]{1,0:T(8,128)(2,1)} %all-gather.4.cloned.1.call-done.refs_1_.c_ref, ...), custom_call_target="tpu_custom_call" | custom-call | flops 14495514624 | bytes 41943040 | tf_op jit(solution)/shard_map/pallas_call | solution.py:627
  336.1 39.9 %shard_map.263 = (f32[256,1536]{1,0:T(8,128)}, bf16[256,1536]{1,0:T(8,128)(2,1)}, f32[1,1536]{1,0:T(1,128)}, bf16[4,3,384,384]{3,2,1,0:T(8,128)(2,1)}) custom-call(bf16[8,256,1536]{2,1,0:T(8,128)(2,1)} %bitcast.108, f32[256,1536]{1,0:T(8,128)} %copy-done, bf16[256,1536]{1,0:T(8,128)(2,1)} %cot_ref.1, f32[1,1536]{1,0:T(1,128)} %slice.65.gain_ref, ...), custom_call_target="tpu_custom_call" | custom-call | flops 7247757312 | bytes 104857600 | tf_op jit(solution)/shard_map/pallas_call | solution.py:742
  376.0 24.3 %shard_map.264 = (bf16[512,768]{1,0:T(8,128)(2,1)}, bf16[768,1536]{1,0:T(8,128)(2,1)}) custom-call(bf16[256,1536]{1,0:T(8,128)(2,1)} %get-tuple-element.89.dproj_ref, bf16[768,1536]{1,0:T(8,128)(2,1)} %bitcast.82, bf16[512,768]{1,0:T(8,128)(2,1)} %copy-done.2), custom_call_target="tpu_custom_call" | custom-call | flops 2415919104 | bytes 41943040 | tf_op jit(solution)/shard_map/pallas_call | solution.py:1117
  400.3 44.7 %shard_map.265 = (bf16[512,768]{1,0:T(8,128)(2,1)}, bf16[32,256,256]{2,1,0:T(8,128)(2,1)}) custom-call(s32[32]{0:T(128)} %fusion.1.slots, s32[2]{0:T(128)} %get-tuple-element.128.tops, bf16[512,768]{1,0:T(8,128)(2,1)} %get-tuple-element.72.q_ref, bf16[32,256,256]{2,1,0:T(8,128)(2,1)} %bitcast.76, bf16[512,768]{1,0:T(8,128)(2,1)} %get-tuple-element.90.do_ref, ...), custom_call_target="tpu_custom_call" | custom-call | flops 16609443840 | bytes 125829120 | tf_op jit(solution)/shard_map/pallas_call | solution.py:909
  445.0 48.5 %shard_map.266 = (bf16[512,256]{1,0:T(8,128)(2,1)}, f32[48,1536]{1,0:T(8,128)}, bf16[4,3,384,384]{3,2,1,0:T(8,128)(2,1)}) custom-call(bf16[16,512,256]{2,1,0:T(8,128)(2,1)} %bitcast.77, bf16[16,48,1536]{2,1,0:T(8,128)(2,1)} %bitcast.81, bf16[4,3,384,384]{3,2,1,0:T(8,128)(2,1)} %get-tuple-element.95.refs_2_), custom_call_target="tpu_custom_call", output_to_operand_aliasing={{2}: (2, {})} | custom-call | bytes 131072000 | tf_op jit(solution)/shard_map/pallas_call | solution.py:482
  494.3 27.3 %shard_map.267 = (bf16[16,2,48,1024]{3,2,1,0:T(8,128)(2,1)}, bf16[512,1536]{1,0:T(8,128)(2,1)}, f32[1,1536]{1,0:T(1,128)}, f32[1,1024]{1,0:T(1,128)}, bf16[3,4,96,768]{3,2,1,0:T(8,128)(2,1)}) custom-call(bf16[512,768]{1,0:T(8,128)(2,1)} %get-tuple-element.92.dq_ref, bf16[512,256]{1,0:T(8,128)(2,1)} %get-tuple-element.96.dkv_ref, ...), custom_call_target="tpu_custom_call" | custom-call | flops 3221225472 | bytes 16777216 | tf_op jit(solution)/shard_map/pallas_call | solution.py:1057
  525.1 62.6 %shard_map.268 = (f32[2,48,1024]{2,1,0:T(8,128)}, f32[8,128]{1,0:T(8,128)}, f32[256,1536]{1,0:T(8,128)}, f32[256,1536]{1,0:T(8,128)}) custom-call(bf16[16,2,48,1024]{3,2,1,0:T(8,128)(2,1)} %get-tuple-element.98.refs_0_, f32[32,8,128]{2,1,0:T(8,128)} %bitcast.90, bf16[2,256,1536]{2,1,0:T(8,128)(2,1)} %bitcast.87, bf16[8,256,1536]{2,1,0:T(8,128)(2,1)} %bitcast.74), custom_call_target="tpu_custom_call" | custom-call | bytes 222822400 | tf_op jit(solution)/shard_map/pallas_call | solution.py:482
  589.0 1.3 slice_bitcast_fusion
  590.3 12.3 %shard_map.269.refs_8_ = bf16[3,4,96,384]{3,2,1,0:T(8,128)(2,1)} custom-call(bf16[3,4,96,384]{3,2,1,0:T(8,128)(2,1)} %bitcast.89, f32[2,48,1024]{2,1,0:T(8,128)} %get-tuple-element.104.refs_1_.refs_0_), custom_call_target="tpu_custom_call" | custom-call | tf_op jit(solution)/shard_map/pallas_call | solution.py:517
  602.6 7.5 %shard_map.270 = (f32[48,1536]{1,0:T(8,128)}, f32[48,256]{1,0:T(8,128)}, f32[48,256]{1,0:T(8,128)}, bf16[256,1536]{1,0:T(8,128)(2,1)}, bf16[256,1536]{1,0:T(8,12...) custom-call(f32[2,48,1024]{2,1,0:T(8,128)} %get-tuple-element.104.refs_1_.refs_0_, ...), custom_call_target="tpu_custom_call" | custom-call | bytes 20971520 | tf_op jit(solution)/shard_map/pallas_call | solution.py:572
  (85 shorter events, 20.7 us)
Async XLA Ops:
  7.2 72.3 %all-gather.4.cloned.1.call-start = ((), (), s32[]{:S(2)}) async-start(), calls=%async_computation.2 | async-start | bytes 7077888 | tf_op jit(solution)/shard_map/all_gather | solution.py:1225
  7.9 229.7 %all-gather.8.cloned.1.call-start = ((), (), s32[]{:S(2)}) async-start(), calls=%async_computation.4 | async-start | bytes 8847360 | tf_op jit(solution)/shard_map/all_gather | solution.py:1190
  11.9 63.5 %copy-start.6 = (s32[1,32]{1,0:T(1,128)S(1)}, s32[1,32]{1,0:T(1,128)}, u32[]{:S(2)}) copy-start(s32[1,32]{1,0:T(1,128)} %param.17) | copy-start | bytes 388
  107.1 200.3 %all-gather.6.cloned.1.call-start = ((), (), s32[]{:S(2)}) async-start(), calls=%async_computation.3 | async-start | bytes 4423680 | tf_op jit(solution)/shard_map/all_gather | solution.py:1190
  167.8 2.1 copy-start.3
  169.5 4.1 copy-start.2
  173.5 23.1 %copy-start.1 = (bf16[256,1536]{1,0:T(8,128)(2,1)S(1)}, bf16[256,1536]{1,0:T(8,128)(2,1)}, u32[]{:S(2)}) copy-start(bf16[256,1536]{1,0:T(8,128)(2,1)} %refs_4_.3) | copy-start | bytes 2359300
  196.2 298.1 %reduce-scatter.3.cloned.1.call-start = ((), (), s32[]{:S(2)}) async-start(), calls=%async_computation.5 | async-start | bytes 8847360 | tf_op jit(solution)/shard_map/reduce_scatter | solution.py:1300
  198.6 35.3 %copy-start = (f32[256,1536]{1,0:T(8,128)}, f32[256,1536]{1,0:T(8,128)S(1)}, u32[]{:S(2)}) copy-start(f32[256,1536]{1,0:T(8,128)S(1)} %get-tuple-element.126.mixed_ref.refs_5_) | copy-start | bytes 4718596
  302.3 287.9 %reduce-scatter.5.cloned.1.call-start = ((), (), s32[]{:S(2)}) async-start(), calls=%async_computation.6 | async-start | bytes 4423680 | tf_op jit(solution)/shard_map/reduce_scatter | solution.py:1300
  493.5 0.7 copy-start.5
  602.6 7.5 %copy-start.4 = (f32[48,1536]{1,0:T(8,128)S(1)}, f32[48,1536]{1,0:T(8,128)}, u32[]{:S(2)}) copy-start(f32[48,1536]{1,0:T(8,128)} %get-tuple-element.169) | copy-start | bytes 884740
Sparse Core Ops, SparseCore 0:
  9.9 63.6 all-gather.3
  107.2 130.3 all-gather.7
  239.2 68.2 all-gather.5
  309.6 122.0 reduce-scatter.2
  493.7 80.2 reduce-scatter.4

commit v6 on v5

--- a/solution.py
+++ b/solution.py
@@ -258,7 +258,12 @@
     q_ref, k_ref, v_ref, o_ref, hidden_ref, small_ref = refs[:6]
     feeds, refs = refs[6:9], refs[9:]
     outs, first_ref, second_ref, refs = refs[:4], refs[4], refs[5], refs[6:]
-    halves_s, o_s = refs[:2]
+    halves_s, o_s, feed_s, feed_sems = refs[:4]
+    loads = [
+        pltpu.make_async_copy(feeds[m], feed_s.at[m], feed_sems.at[m]) for m in range(len(feeds))
+    ]
+    for copy in loads:
+        copy.start()
     heads = halves_s.shape[0]
     q_cols, kv_cols = q_ref.shape[1] // heads, k_ref.shape[1] // heads
     for i in range(heads):
@@ -270,13 +275,14 @@
 
     def pack():
         first, second = first_ref.shape[-1], second_ref.shape[-1]
-        for m, feed_ref in enumerate(feeds):
-            rows, width = feed_ref.shape
+        for m in range(len(feeds)):
+            loads[m].wait()
+            rows, width = feed_s.shape[1:]
             for i in range(first_ref.shape[1]):
                 low = i * (first + second)
                 for ref, n in ((first_ref, first), (second_ref, second)):
                     real = min(n, width - low)
-                    ref[m, i, :, :real] = feed_ref[:, low : low + real].astype(BF)
+                    ref[m, i, :, :real] = feed_s[m, :, low : low + real].astype(BF)
                     if real < n:
                         ref[m, i, :, real:] = jnp.zeros((rows, n - real), BF)
                     low += n
@@ -292,7 +298,7 @@
         small_ref,
         o_s,
         *outs,
-        *refs[2:],
+        *refs[4:],
         ahead=pack,
     )
 
@@ -315,11 +321,13 @@
     return pl.pallas_call(
         functools.partial(front_kernel, plans, sizes),
         out_shape=shapes + blocks,
-        in_specs=[spec] * 9,
+        in_specs=[spec] * 6 + [pl.BlockSpec(memory_space=pl.ANY)] * 3,
         out_specs=[spec] * 6,
         scratch_shapes=[
             pltpu.VMEM(halves.shape, BF),
             pltpu.VMEM(out.shape, BF),
+            pltpu.VMEM((3,) + feeds[0].shape, F32),
+            pltpu.SemaphoreType.DMA((3,)),
             pltpu.SemaphoreType.DMA((total,)),
             pltpu.SemaphoreType.DMA((total,)),
             pltpu.SemaphoreType.DMA((len(plans),)),
@@ -338,9 +346,10 @@
     return keys
 
 
-def scatter_kernel(plans, sizes, *refs, between=None):
+def scatter_kernel(plans, sizes, *refs, between=None, held=None, held_sems=None):
     count = max(p[0] for p in plans) + 1
     xs, outs = refs[:count], refs[count : 2 * count]
+    held = held or {}
     at = 2 * count
     bufs = []
     for _, _, _, phases, swap in plans:
@@ -352,6 +361,18 @@
         a: (sizes[a] if any(a in p[3] or (p[4] and a == "head") for p in plans) else 1)
         for a in AXES
     }
+    loads = {}
+    for j, (i, rows, layout, phases, swap) in enumerate(plans):
+        if i not in held:
+            continue
+        for key in offset_keys(phases[1:], sizes):
+            place = place_of(key, layout, sizes)
+            src, dst = xs[i].at[place], held[i].at[place]
+            if rows is not None:
+                src, dst = src.at[pl.ds(*rows)], dst.at[pl.ds(*rows)]
+            copy = pltpu.make_async_copy(src, dst, held_sems.at[len(loads)])
+            copy.start()
+            loads[j, tuple(key.get(a, 0) for a in phases[1:])] = copy
     greet(live(AXES, used), sizes)
     sem = 0
     sends = []
@@ -363,14 +384,16 @@
             value = value * sizes[a] + offsets.get(a, 0)
         return value
 
-    def block_of(j, offsets):
+    def block_of(j, offsets, near=False):
         i, rows, layout, phases, swap = plans[j]
-        block = xs[i].at[place_of(offsets, layout, sizes)]
+        block = (held.get(i, xs[i]) if near else xs[i]).at[place_of(offsets, layout, sizes)]
         return block if rows is None else block.at[pl.ds(*rows)]
 
     def total_of(j, offsets, phase):
         phases = plans[j][3]
-        total = block_of(j, offsets)[...].astype(F32)
+        if plans[j][0] in held:
+            loads[j, tuple(offsets.get(a, 0) for a in phases[1:])].wait()
+        total = block_of(j, offsets, True)[...].astype(F32)
         for q in range(phase):
             rest = phases[q + 1 :]
             for d in range(1, sizes[phases[q]]):
@@ -461,6 +484,16 @@
     ]
 
 
+def held_scratch(arrays, plans, far, sizes):
+    count = 0
+    for i, _, _, phases, _ in plans:
+        if i in far:
+            count += int(np.prod([sizes[a] for a in phases[1:]], dtype=int))
+    return [pltpu.VMEM(arrays[i].shape, arrays[i].dtype) for i in far] + [
+        pltpu.SemaphoreType.DMA((count,))
+    ]
+
+
 def alive(plans, sizes):
     return [
         (i, rows, live(layout, sizes), live(phases, sizes), flag)
@@ -468,9 +501,15 @@
     ]
 
 
-def scatter_and_wait_kernel(plans, sizes, arrays, waited, carried, *refs):
+def scatter_and_wait_kernel(plans, sizes, arrays, waited, carried, far, *refs):
     xs, refs = refs[:arrays], refs[arrays + waited :]
-    scatter_kernel(plans, sizes, *xs, *refs[:arrays], *refs[arrays + carried :])
+    outs, refs, held = refs[:arrays], refs[arrays + carried :], {}
+    if far:
+        held = dict(zip(far, refs[-len(far) - 1 : -1]))
+        refs, held_sems = refs[: -len(far) - 1], refs[-1]
+        scatter_kernel(plans, sizes, *xs, *outs, *refs, held=held, held_sems=held_sems)
+    else:
+        scatter_kernel(plans, sizes, *xs, *outs, *refs)
 
 
 def scatter(arrays, plans, out_types, sizes, collective_id, after=(), carried=()):
@@ -478,6 +517,7 @@
     shapes = [jax.ShapeDtypeStruct(x.shape[1:], kind) for x, kind in zip(arrays, out_types)]
     spec = pl.BlockSpec(memory_space=pltpu.VMEM)
     far = pl.BlockSpec(memory_space=pl.ANY)
+    big = tuple(i for i, x in enumerate(arrays) if x.dtype == BF)
     moved = sum(int(np.prod(x.shape)) * x.dtype.itemsize for x in arrays)
     return pl.pallas_call(
         functools.partial(
@@ -487,14 +527,16 @@
             len(arrays),
             len(after) + len(carried),
             len(carried),
+            big,
         ),
         out_shape=shapes + [jax.ShapeDtypeStruct(x.shape, x.dtype) for x in carried],
-        in_specs=[spec] * len(arrays) + [far] * (len(after) + len(carried)),
+        in_specs=[far if i in big else spec for i in range(len(arrays))] + [far] * (len(after) + len(carried)),
         out_specs=[spec] * len(arrays) + [far] * len(carried),
         input_output_aliases={
             len(arrays) + len(after) + i: len(arrays) + i for i in range(len(carried))
         },
-        scratch_shapes=scatter_scratch(arrays, plans, out_types, sizes),
+        scratch_shapes=scatter_scratch(arrays, plans, out_types, sizes)
+        + (held_scratch(arrays, plans, big, sizes) if big else []),
         compiler_params=pltpu.CompilerParams(
             collective_id=collective_id, has_side_effects=True, vmem_limit_bytes=VMEM_LIMIT
         ),
@@ -560,20 +602,30 @@
 
 
 def write_outputs(w, dnormed, branch, dmixed, x, mixed, gain, parts, width):
-    spec = pl.BlockSpec(memory_space=pltpu.VMEM)
     heads, rows, inner = w.shape
+    tok, ff_rows = x.shape[0], parts[0].shape[2]
+    steps = 2 if rows % 16 == 0 and ff_rows % 32 == 0 else 1
+
+    def rows_of(shape, dim):
+        block = tuple(n // steps if i == dim else n for i, n in enumerate(shape))
+        return pl.BlockSpec(block, lambda i: tuple(i if k == dim else 0 for k in range(len(shape))))
+
     kinds = [
         ((rows, heads * (inner - 2 * HEAD_DIM)), F32),
         ((rows, heads * HEAD_DIM), F32),
         ((rows, heads * HEAD_DIM), F32),
         (x.shape, BF),
         (x.shape, BF),
-    ] + [((parts[0].shape[2], width), F32)] * 3
+    ] + [((ff_rows, width), F32)] * 3
     return pl.pallas_call(
         outputs_kernel,
+        grid=(steps,),
         out_shape=[jax.ShapeDtypeStruct(*k) for k in kinds],
-        in_specs=[spec] * 9,
-        out_specs=[spec] * len(kinds),
+        in_specs=[rows_of(w.shape, 1)]
+        + [rows_of(x.shape, 0)] * 5
+        + [pl.BlockSpec(gain.shape, lambda i: (0, 0))]
+        + [rows_of(part.shape, 2) for part in parts],
+        out_specs=[rows_of(shape, 0) for shape, _ in kinds],
         compiler_params=pltpu.CompilerParams(vmem_limit_bytes=VMEM_LIMIT),
         cost_estimate=pl.CostEstimate(flops=0, bytes_accessed=20 * 2**20, transcendentals=0),
     )(w, dnormed, branch, dmixed, x, mixed, gain, *parts)
@@ -669,6 +721,7 @@
     t_hbm, c_hbm, act_hbm, dgate_hbm, dup_hbm = refs[:5]
     dmixed_ref, dproj_ref, gain_grad_ref, grad_hbm = refs[5:9]
     sum_ref, left_s, right_s, made_s, load_sems, made_sems = refs[9:15]
+    held, held_sems = {0: refs[-2]}, refs[-1]
     per, rows = made_s.shape[1:3]
     cols = per * rows
     loads = [
@@ -717,7 +770,16 @@
             loads[4].wait()
             some(2, 0, chunks, 1, 0, False)
 
-    scatter_kernel(plans, sizes, dtok_ref, sum_ref, *refs[15:], between=between)
+    scatter_kernel(
+        plans,
+        sizes,
+        dtok_ref,
+        sum_ref,
+        *refs[15:-2],
+        between=between,
+        held=held,
+        held_sems=held_sems,
+    )
     mixed, dnormed = mixed_ref[...], sum_ref[...]
     scale = inverse_rms(mixed)
     z = mixed * scale
@@ -747,7 +809,7 @@
             jax.ShapeDtypeStruct((1, D), F32),
             jax.ShapeDtypeStruct((places, 3, rows, width), BF),
         ],
-        in_specs=[spec] * 4 + [far] * 5,
+        in_specs=[far] + [spec] * 3 + [far] * 5,
         out_specs=[spec] * 3 + [far],
         scratch_shapes=[
             pltpu.VMEM(dtok.shape[1:], F32),
@@ -757,7 +819,8 @@
             pltpu.SemaphoreType.DMA((5,)),
             pltpu.SemaphoreType.DMA((2,)),
         ]
-        + scatter_scratch([dtok], plans, [F32], sizes),
+        + scatter_scratch([dtok], plans, [F32], sizes)
+        + held_scratch([dtok], plans, (0,), sizes),
         compiler_params=pltpu.CompilerParams(
             collective_id=collective_id, has_side_effects=True, vmem_limit_bytes=VMEM_LIMIT
         ),
@@ -1177,8 +1240,8 @@
     q_cols = D // 2
     kv_cols = HEAD_DIM
     rows = q_weight.shape[0]
-    small = jnp.concatenate([v.astype(BF) for v in (norm1, norm2, q_bias, k_bias, v_bias)])
-    small = jnp.pad(small.astype(F32), (0, 8 * LANES - small.shape[0])).reshape(8, LANES)
+    small = lax.reduce_precision(jnp.concatenate([norm1, norm2, q_bias, k_bias, v_bias]), 8, 7)
+    small = jnp.pad(small, (0, 8 * LANES - small.shape[0])).reshape(8, LANES)
     parts = sizes["y"] * sizes["c"]
     width = gate_weight.shape[1]
     lanes = -(-width // (LANES * parts)) * LANES

time: 626 us -> 618 us (0.987)
  Pallas kernels: 565 us -> 558 us
where the time goes in v6:
time: 618 us; the launch traced here: 609 us
  Pallas kernels  558 us (90%)
  between operations  14.3 us (2%)
  local copies, waits for them, and re-layouts  11.9 us (2%)
  other arithmetic  11.2 us (2%)
  waiting for transfers between devices  8.52 us (1%)
    pallas_call x2, Pallas kernels, scatter(): pl.pallas_call(functools.partial(scatter_and_wait_kernel, plans, sizes, l...  109 us
    pallas_call x3, Pallas kernels, gather(): pl.pallas_call(functools.partial(gather_kernel, plans, sizes, len(swaps),...  88.5 us
    pallas_call x2, Pallas kernels, feed(): pl.pallas_call(functools.partial(feed_kernel, chunks, len(before)), grid=...  71.8 us
    pallas_call x1, Pallas kernels, front(): pl.pallas_call(functools.partial(front_kernel, plans, sizes), out_shape=s...  57.1 us
    pallas_call x1, Pallas kernels, attend_back(): pl.pallas_call(functools.partial(backward_kernel, heads), grid_spec=pltpu...  44.5 us
    pallas_call x1, Pallas kernels, feed_grads(): pl.pallas_call(functools.partial(grads_kernel, plans, sizes), out_shape=[...  38.4 us
    pallas_call x1, Pallas kernels, project(): pl.pallas_call(functools.partial(project_kernel, plans, sizes), in_specs=...  29.5 us
    pallas_call x1, Pallas kernels, attend(): pl.pallas_call(functools.partial(forward_kernel, heads), grid_spec=pltpu....  27.6 us
  transfers between devices with their start and end apart: 5, of which 2 were waited for; matrix products, arithmetic and copies ran while one was open for 4% of the time, Pallas kernels for 84%

profile of v6, /device:TPU:0, one launch (start us, length us, event | category | flops | bytes accessed | tf_op | source)
XLA Modules:
  0.0 608.8 jit_solution(7994375475016779370)
XLA Ops:
  9.4 57.1 %shard_map.254 = (bf16[32,48,1024]{2,1,0:T(8,128)(2,1)}, bf16[2,256,1536]{2,1,0:T(8,128)(2,1)}, f32[32,8,128]{2,1,0:T(8,128)}, bf16[16,48,1536]{2,1,0:T(8,128)(2...) custom-call(f32[48,1536]{1,0:T(8,128)} %refs_0_.1, f32[48,256]{1,0:T(8,128)} %refs_1_.1, ...), custom_call_target="tpu_custom_call" | custom-call | bytes 104857600 | tf_op jit(solution)/shard_map/pallas_call | solution.py:321
  72.5 29.5 %shard_map.255 = (bf16[4,512,256]{2,1,0:T(8,128)(2,1)}, bf16[3,4,96,768]{3,2,1,0:T(8,128)(2,1)}, bf16[512,768]{1,0:T(8,128)(2,1)}, bf16[512,1536]{1,0:T(8,128)(2,1)}) custom-call(bf16[512,1536]{1,0:T(8,128)(2,1)} %bitcast.84, bf16[1536,1024]{1,0:T(8,128)(2,1)} %bitcast.77, f32[1,1536]{1,0:T(1,128)} %slice.59.gain_ref.refs_6_, f32[1,1024]{1,0:T(1,128)} %bitcast.103, ...), custom_call_target="tpu_custom_call" | custom-call | flops 1610612736 | bytes 83886080 | tf_op jit(solution)/shard_map/pallas_call | solution.py:1040
  102.1 1.6 sort.17
  104.3 30.9 %shard_map.256 = bf16[4,4,512,256]{3,2,1,0:T(8,128)(2,1)} custom-call(bf16[4,512,256]{2,1,0:T(8,128)(2,1)} %get-tuple-element.73.refs_0_), custom_call_target="tpu_custom_call" | custom-call | bytes 83886080 | tf_op jit(solution)/shard_map/pallas_call | solution.py:234
  135.2 27.6 %shard_map.257 = (f32[512,768]{1,0:T(8,128)}, f32[2,8,256]{2,1,0:T(8,128)}) custom-call(s32[32]{0:T(128)} %fusion.1.slots, s32[2]{0:T(128)} %get-tuple-element.128.tops, bf16[512,768]{1,0:T(8,128)(2,1)} %get-tuple-element.72.q_ref, bf16[32,256,256]{2,1,0:T(8,128)(2,1)} %bitcast.74), custom_call_target="tpu_custom_call" | custom-call | flops 6643777536 | bytes 83886080 | tf_op jit(solution)/shard_map/pallas_call | solution.py:884
  162.8 1.6 convert_element_type.47.attn_ref
  165.0 3.6 fusion.7
  168.5 23.1 %shard_map.258 = (bf16[2,256,1536]{2,1,0:T(8,128)(2,1)}, bf16[3,4,96,384]{3,2,1,0:T(8,128)(2,1)}) custom-call(bf16[2,256,1536]{2,1,0:T(8,128)(2,1)} %get-tuple-element.142.refs_0_, bf16[3,4,96,384]{3,2,1,0:T(8,128)(2,1)} %get-tuple-element.76.refs_1_), custom_call_target="tpu_custom_call" | custom-call | bytes 31457280 | tf_op jit(solution)/shard_map/pallas_call | solution.py:234
  192.0 2.0 multiply_reduce_fusion
  195.3 34.5 %shard_map.259 = bf16[8,256,1536]{2,1,0:T(8,128)(2,1)} custom-call(bf16[256,1536]{1,0:T(8,128)(2,1)} %multiply_convert_fusion.refs_0_), custom_call_target="tpu_custom_call" | custom-call | bytes 125829120 | tf_op jit(solution)/shard_map/pallas_call | solution.py:234
  229.8 3.8 all-gather.8.cloned.1.call-done.w_ref
  233.6 43.2 %shard_map.260 = (bf16[2048,768]{1,0:T(8,128)(2,1)}, bf16[2048,768]{1,0:T(8,128)(2,1)}, bf16[2048,768]{1,0:T(8,128)(2,1)}, bf16[2048,1536]{1,0:T(8,128)(2,1)}, bf16[2048,1536]{1,0:T(8,128)(2,1)}) custom-call(bf16[2048,1536]{1,0:T(8,128)(2,1)} %bitcast.69, bf16[2048,1536]{1,0:T(8,128)(2,1)} %all-gather.4.cloned.1.call-done.refs_1_.c_ref, ...), custom_call_target="tpu_custom_call" | custom-call | flops 28991029248 | bytes 41943040 | tf_op jit(solution)/shard_map/pallas_call | solution.py:679
  276.7 21.5 %shard_map.261.refs_2_ = bf16[4,3,384,768]{3,2,1,0:T(8,128)(2,1)} custom-call(bf16[2048,1536]{1,0:T(8,128)(2,1)} %bitcast.70, bf16[2048,1536]{1,0:T(8,128)(2,1)} %all-gather.4.cloned.1.call-done.refs_1_.c_ref, bf16[2048,768]{1,0:T(8,128)(2,1)} %get-tuple-element.82.act_ref, bf16[2048,768]{1,0:T(8,128)(2,1)} %get-tuple-element.83.dgate_ref, ...), custom_call_target="tpu_custom_call" | custom-call | flops 14495514624 | bytes 41943040 | tf_op jit(solution)/shard_map/pallas_call | solution.py:707
  299.4 4.0 all-gather.6.cloned.1.call-done.w_ref
  303.4 28.6 %shard_map.262 = (bf16[2048,384]{1,0:T(8,128)(2,1)}, bf16[2048,384]{1,0:T(8,128)(2,1)}, bf16[2048,384]{1,0:T(8,128)(2,1)}, bf16[2048,1536]{1,0:T(8,128)(2,1)}, bf16[2048,1536]{1,0:T(8,128)(2,1)}) custom-call(bf16[2048,1536]{1,0:T(8,128)(2,1)} %bitcast.71, bf16[2048,1536]{1,0:T(8,128)(2,1)} %all-gather.4.cloned.1.call-done.refs_1_.c_ref, ...), custom_call_target="tpu_custom_call" | custom-call | flops 14495514624 | bytes 41943040 | tf_op jit(solution)/shard_map/pallas_call | solution.py:679
  332.0 38.4 %shard_map.263 = (f32[256,1536]{1,0:T(8,128)}, bf16[256,1536]{1,0:T(8,128)(2,1)}, f32[1,1536]{1,0:T(1,128)}, bf16[4,3,384,384]{3,2,1,0:T(8,128)(2,1)}) custom-call(bf16[8,256,1536]{2,1,0:T(8,128)(2,1)} %bitcast.107, f32[256,1536]{1,0:T(8,128)} %copy-done, bf16[256,1536]{1,0:T(8,128)(2,1)} %cot_ref.1, f32[1,1536]{1,0:T(1,128)} %slice.65.gain_ref, ...), custom_call_target="tpu_custom_call" | custom-call | flops 7247757312 | bytes 104857600 | tf_op jit(solution)/shard_map/pallas_call | solution.py:804
  370.4 24.4 %shard_map.264 = (bf16[512,768]{1,0:T(8,128)(2,1)}, bf16[768,1536]{1,0:T(8,128)(2,1)}) custom-call(bf16[256,1536]{1,0:T(8,128)(2,1)} %get-tuple-element.89.dproj_ref, bf16[768,1536]{1,0:T(8,128)(2,1)} %bitcast.81, bf16[512,768]{1,0:T(8,128)(2,1)} %copy-done.2), custom_call_target="tpu_custom_call" | custom-call | flops 2415919104 | bytes 41943040 | tf_op jit(solution)/shard_map/pallas_call | solution.py:1180
  394.8 44.5 %shard_map.265 = (bf16[512,768]{1,0:T(8,128)(2,1)}, bf16[32,256,256]{2,1,0:T(8,128)(2,1)}) custom-call(s32[32]{0:T(128)} %fusion.1.slots, s32[2]{0:T(128)} %get-tuple-element.128.tops, bf16[512,768]{1,0:T(8,128)(2,1)} %get-tuple-element.72.q_ref, bf16[32,256,256]{2,1,0:T(8,128)(2,1)} %bitcast.75, bf16[512,768]{1,0:T(8,128)(2,1)} %get-tuple-element.90.do_ref, ...), custom_call_target="tpu_custom_call" | custom-call | flops 16609443840 | bytes 125829120 | tf_op jit(solution)/shard_map/pallas_call | solution.py:972
  439.3 46.1 %shard_map.266 = (bf16[512,256]{1,0:T(8,128)(2,1)}, f32[48,1536]{1,0:T(8,128)}, bf16[4,3,384,384]{3,2,1,0:T(8,128)(2,1)}) custom-call(bf16[16,512,256]{2,1,0:T(8,128)(2,1)} %bitcast.76, bf16[16,48,1536]{2,1,0:T(8,128)(2,1)} %bitcast.80, bf16[4,3,384,384]{3,2,1,0:T(8,128)(2,1)} %get-tuple-element.95.refs_2_), custom_call_target="tpu_custom_call", output_to_operand_aliasing={{2}: (2, {})} | custom-call | bytes 131072000 | tf_op jit(solution)/shard_map/pallas_call | solution.py:522
  486.3 27.3 %shard_map.267 = (bf16[16,2,48,1024]{3,2,1,0:T(8,128)(2,1)}, bf16[512,1536]{1,0:T(8,128)(2,1)}, f32[1,1536]{1,0:T(1,128)}, f32[1,1024]{1,0:T(1,128)}, bf16[3,4,96,768]{3,2,1,0:T(8,128)(2,1)}) custom-call(bf16[512,768]{1,0:T(8,128)(2,1)} %get-tuple-element.92.dq_ref, bf16[512,256]{1,0:T(8,128)(2,1)} %get-tuple-element.96.dkv_ref, ...), custom_call_target="tpu_custom_call" | custom-call | flops 3221225472 | bytes 16777216 | tf_op jit(solution)/shard_map/pallas_call | solution.py:1120
  517.0 62.7 %shard_map.268 = (f32[2,48,1024]{2,1,0:T(8,128)}, f32[8,128]{1,0:T(8,128)}, f32[256,1536]{1,0:T(8,128)}, f32[256,1536]{1,0:T(8,128)}) custom-call(bf16[16,2,48,1024]{3,2,1,0:T(8,128)(2,1)} %get-tuple-element.98.refs_0_, f32[32,8,128]{2,1,0:T(8,128)} %bitcast.89, bf16[2,256,1536]{2,1,0:T(8,128)(2,1)} %bitcast.86, bf16[8,256,1536]{2,1,0:T(8,128)(2,1)} %bitcast.73), custom_call_target="tpu_custom_call" | custom-call | bytes 222822400 | tf_op jit(solution)/shard_map/pallas_call | solution.py:522
  581.0 1.3 slice_bitcast_fusion
  582.3 12.3 %shard_map.269.refs_8_ = bf16[3,4,96,384]{3,2,1,0:T(8,128)(2,1)} custom-call(bf16[3,4,96,384]{3,2,1,0:T(8,128)(2,1)} %bitcast.88, f32[2,48,1024]{2,1,0:T(8,128)} %get-tuple-element.104.refs_1_.refs_0_), custom_call_target="tpu_custom_call" | custom-call | tf_op jit(solution)/shard_map/pallas_call | solution.py:559
  594.6 6.8 %shard_map.270 = (f32[48,1536]{1,0:T(8,128)}, f32[48,256]{1,0:T(8,128)}, f32[48,256]{1,0:T(8,128)}, bf16[256,1536]{1,0:T(8,128)(2,1)}, bf16[256,1536]{1,0:T(8,12...) custom-call(f32[2,48,1024]{2,1,0:T(8,128)} %get-tuple-element.104.refs_1_.refs_0_, ...), custom_call_target="tpu_custom_call" | custom-call | bytes 20971520 | tf_op jit(solution)/shard_map/pallas_call | solution.py:620
  (81 shorter events, 18.2 us)
Async XLA Ops:
  7.2 65.3 %all-gather.4.cloned.1.call-start = ((), (), s32[]{:S(2)}) async-start(), calls=%async_computation.2 | async-start | bytes 7077888 | tf_op jit(solution)/shard_map/all_gather | solution.py:1288
  7.9 225.6 %all-gather.8.cloned.1.call-start = ((), (), s32[]{:S(2)}) async-start(), calls=%async_computation.4 | async-start | bytes 8847360 | tf_op jit(solution)/shard_map/all_gather | solution.py:1253
  9.4 59.1 %copy-start.6 = (s32[1,32]{1,0:T(1,128)S(1)}, s32[1,32]{1,0:T(1,128)}, u32[]{:S(2)}) copy-start(s32[1,32]{1,0:T(1,128)} %param.17) | copy-start | bytes 388
  102.1 201.3 %all-gather.6.cloned.1.call-start = ((), (), s32[]{:S(2)}) async-start(), calls=%async_computation.3 | async-start | bytes 4423680 | tf_op jit(solution)/shard_map/all_gather | solution.py:1253
  162.8 2.1 copy-start.3
  164.5 4.1 copy-start.2
  168.5 23.5 %copy-start.1 = (bf16[256,1536]{1,0:T(8,128)(2,1)S(1)}, bf16[256,1536]{1,0:T(8,128)(2,1)}, u32[]{:S(2)}) copy-start(bf16[256,1536]{1,0:T(8,128)(2,1)} %refs_4_.3) | copy-start | bytes 2359300
  191.7 294.6 %reduce-scatter.3.cloned.1.call-start = ((), (), s32[]{:S(2)}) async-start(), calls=%async_computation.5 | async-start | bytes 8847360 | tf_op jit(solution)/shard_map/reduce_scatter | solution.py:1363
  194.0 35.7 %copy-start = (f32[256,1536]{1,0:T(8,128)}, f32[256,1536]{1,0:T(8,128)S(1)}, u32[]{:S(2)}) copy-start(f32[256,1536]{1,0:T(8,128)S(1)} %get-tuple-element.126.mixed_ref.refs_5_) | copy-start | bytes 4718596
  298.3 284.0 %reduce-scatter.5.cloned.1.call-start = ((), (), s32[]{:S(2)}) async-start(), calls=%async_computation.6 | async-start | bytes 4423680 | tf_op jit(solution)/shard_map/reduce_scatter | solution.py:1363
  485.4 0.7 copy-start.5
  594.6 6.8 %copy-start.4 = (f32[48,1536]{1,0:T(8,128)S(1)}, f32[48,1536]{1,0:T(8,128)}, u32[]{:S(2)}) copy-start(f32[48,1536]{1,0:T(8,128)} %get-tuple-element.169) | copy-start | bytes 884740
Sparse Core Ops, SparseCore 0:
  9.9 62.2 all-gather.3
  102.2 131.3 all-gather.7
  235.1 68.2 all-gather.5
  305.5 122.0 reduce-scatter.2
  485.6 79.8 reduce-scatter.4

commit v7 on v6

--- a/solution.py
+++ b/solution.py
@@ -237,7 +237,7 @@
         ),
         out_shape=shapes + [jax.ShapeDtypeStruct(x.shape, x.dtype) for x in (*swaps, *carried)],
         in_specs=specs + [far] * (len(after) + len(carried)),
-        out_specs=specs + [far] * len(carried),
+        out_specs=[far] * (len(specs) + len(carried)),
         input_output_aliases={
             len(specs) + len(after) + i: len(specs) + i for i in range(len(carried))
         },
@@ -322,7 +322,7 @@
         functools.partial(front_kernel, plans, sizes),
         out_shape=shapes + blocks,
         in_specs=[spec] * 6 + [pl.BlockSpec(memory_space=pl.ANY)] * 3,
-        out_specs=[spec] * 6,
+        out_specs=[pl.BlockSpec(memory_space=pl.ANY)] * 4 + [spec] * 2,
         scratch_shapes=[
             pltpu.VMEM(halves.shape, BF),
             pltpu.VMEM(out.shape, BF),
@@ -1040,7 +1040,7 @@
     return pl.pallas_call(
         functools.partial(project_kernel, plans, sizes),
         in_specs=[spec] * 6 + [far] * 2,
-        out_specs=[spec, far, spec, spec],
+        out_specs=[far, far, spec, spec],
         out_shape=[
             jax.ShapeDtypeStruct(s, BF)
             for s in ((count,) + kv, packed.shape, (n, width - 2 * HEAD_DIM), (n, D))

time: 618 us -> 615 us (level)
  Pallas kernels: 558 us -> 550 us
  waiting for transfers between devices: 8.52 us -> 14.8 us
  transfers between devices with their start and end apart: 5 -> 5, of which waited for: 2 -> 3; matrix products, arithmetic and copies ran while one was open for 4% -> 4% of each run, Pallas kernels for 84% -> 83%
where the time goes in v7:
time: 615 us; the launch traced here: 606 us
  Pallas kernels  550 us (89%)
  waiting for transfers between devices  14.8 us (2%)
  between operations  14.3 us (2%)
  local copies, waits for them, and re-layouts  11.9 us (2%)
  other arithmetic  11.3 us (2%)
    pallas_call x2, Pallas kernels, scatter(): pl.pallas_call(functools.partial(scatter_and_wait_kernel, plans, sizes, l...  109 us
    pallas_call x3, Pallas kernels, gather(): pl.pallas_call(functools.partial(gather_kernel, plans, sizes, len(swaps),...  82.9 us
    pallas_call x2, Pallas kernels, feed(): pl.pallas_call(functools.partial(feed_kernel, chunks, len(before)), grid=...  71.8 us
    pallas_call x1, Pallas kernels, front(): pl.pallas_call(functools.partial(front_kernel, plans, sizes), out_shape=s...  56.2 us
    pallas_call x1, Pallas kernels, attend_back(): pl.pallas_call(functools.partial(backward_kernel, heads), grid_spec=pltpu...  44.5 us
    pallas_call x1, Pallas kernels, feed_grads(): pl.pallas_call(functools.partial(grads_kernel, plans, sizes), out_shape=[...  38.4 us
    pallas_call x1, Pallas kernels, attend(): pl.pallas_call(functools.partial(forward_kernel, heads), grid_spec=pltpu....  27.6 us
    pallas_call x1, Pallas kernels, project(): pl.pallas_call(functools.partial(project_kernel, plans, sizes), in_specs=...  27.4 us
  transfers between devices with their start and end apart: 5, of which 3 were waited for; matrix products, arithmetic and copies ran while one was open for 4% of the time, Pallas kernels for 83%

profile of v7, /device:TPU:0, one launch (start us, length us, event | category | flops | bytes accessed | tf_op | source)
XLA Modules:
  0.0 606.3 jit_solution(9218997706764545973)
XLA Ops:
  9.4 56.2 %shard_map.254 = (bf16[32,48,1024]{2,1,0:T(8,128)(2,1)}, bf16[2,256,1536]{2,1,0:T(8,128)(2,1)}, f32[32,8,128]{2,1,0:T(8,128)}, bf16[16,48,1536]{2,1,0:T(8,128)(2...) custom-call(f32[48,1536]{1,0:T(8,128)} %refs_0_.1, f32[48,256]{1,0:T(8,128)} %refs_1_.1, ...), custom_call_target="tpu_custom_call" | custom-call | bytes 104857600 | tf_op jit(solution)/shard_map/pallas_call | solution.py:321
  72.6 27.4 %shard_map.255 = (bf16[4,512,256]{2,1,0:T(8,128)(2,1)}, bf16[3,4,96,768]{3,2,1,0:T(8,128)(2,1)}, bf16[512,768]{1,0:T(8,128)(2,1)}, bf16[512,1536]{1,0:T(8,128)(2,1)}) custom-call(bf16[512,1536]{1,0:T(8,128)(2,1)} %bitcast.84, bf16[1536,1024]{1,0:T(8,128)(2,1)} %bitcast.77, f32[1,1536]{1,0:T(1,128)} %slice.59.gain_ref.refs_6_, f32[1,1024]{1,0:T(1,128)} %bitcast.103, ...), custom_call_target="tpu_custom_call" | custom-call | flops 1610612736 | bytes 83886080 | tf_op jit(solution)/shard_map/pallas_call | solution.py:1040
  100.1 1.6 sort.17
  102.2 29.6 %shard_map.256 = bf16[4,4,512,256]{3,2,1,0:T(8,128)(2,1)} custom-call(bf16[4,512,256]{2,1,0:T(8,128)(2,1)} %get-tuple-element.73.refs_0_), custom_call_target="tpu_custom_call" | custom-call | bytes 83886080 | tf_op jit(solution)/shard_map/pallas_call | solution.py:234
  131.8 27.6 %shard_map.257 = (f32[512,768]{1,0:T(8,128)}, f32[2,8,256]{2,1,0:T(8,128)}) custom-call(s32[32]{0:T(128)} %fusion.1.slots, s32[2]{0:T(128)} %get-tuple-element.128.tops, bf16[512,768]{1,0:T(8,128)(2,1)} %get-tuple-element.72.q_ref, bf16[32,256,256]{2,1,0:T(8,128)(2,1)} %bitcast.74), custom_call_target="tpu_custom_call" | custom-call | flops 6643777536 | bytes 83886080 | tf_op jit(solution)/shard_map/pallas_call | solution.py:884
  159.4 1.7 convert_element_type.47.attn_ref
  161.6 3.6 fusion.7
  165.1 21.6 %shard_map.258 = (bf16[2,256,1536]{2,1,0:T(8,128)(2,1)}, bf16[3,4,96,384]{3,2,1,0:T(8,128)(2,1)}) custom-call(bf16[2,256,1536]{2,1,0:T(8,128)(2,1)} %get-tuple-element.142.refs_0_, bf16[3,4,96,384]{3,2,1,0:T(8,128)(2,1)} %get-tuple-element.76.refs_1_), custom_call_target="tpu_custom_call" | custom-call | bytes 31457280 | tf_op jit(solution)/shard_map/pallas_call | solution.py:234
  187.1 2.1 multiply_reduce_fusion
  190.4 31.8 %shard_map.259 = bf16[8,256,1536]{2,1,0:T(8,128)(2,1)} custom-call(bf16[256,1536]{1,0:T(8,128)(2,1)} %multiply_convert_fusion.refs_0_), custom_call_target="tpu_custom_call" | custom-call | bytes 125829120 | tf_op jit(solution)/shard_map/pallas_call | solution.py:234
  222.2 8.9 %all-gather.8.cloned.1.call-done.w_ref = bf16[4,3,384,768]{3,2,1,0:T(8,128)(2,1)} async-done(((bf16[1,3,384,768]{3,2,1,0:T(8,128)(2,1)}), bf16[4,3,384,768]{3,2,1,0:T(8,128)(2,1)}) %all-gather.8.cloned.1.call-update) | async-done | bytes 7077904 | tf_op jit(solution)/shard_map/all_gather | solution.py:1253
  231.1 43.2 %shard_map.260 = (bf16[2048,768]{1,0:T(8,128)(2,1)}, bf16[2048,768]{1,0:T(8,128)(2,1)}, bf16[2048,768]{1,0:T(8,128)(2,1)}, bf16[2048,1536]{1,0:T(8,128)(2,1)}, bf16[2048,1536]{1,0:T(8,128)(2,1)}) custom-call(bf16[2048,1536]{1,0:T(8,128)(2,1)} %bitcast.69, bf16[2048,1536]{1,0:T(8,128)(2,1)} %all-gather.4.cloned.1.call-done.refs_1_.c_ref, ...), custom_call_target="tpu_custom_call" | custom-call | flops 28991029248 | bytes 41943040 | tf_op jit(solution)/shard_map/pallas_call | solution.py:679
  274.2 21.5 %shard_map.261.refs_2_ = bf16[4,3,384,768]{3,2,1,0:T(8,128)(2,1)} custom-call(bf16[2048,1536]{1,0:T(8,128)(2,1)} %bitcast.70, bf16[2048,1536]{1,0:T(8,128)(2,1)} %all-gather.4.cloned.1.call-done.refs_1_.c_ref, bf16[2048,768]{1,0:T(8,128)(2,1)} %get-tuple-element.82.act_ref, bf16[2048,768]{1,0:T(8,128)(2,1)} %get-tuple-element.83.dgate_ref, ...), custom_call_target="tpu_custom_call" | custom-call | flops 14495514624 | bytes 41943040 | tf_op jit(solution)/shard_map/pallas_call | solution.py:707
  296.9 4.0 all-gather.6.cloned.1.call-done.w_ref
  300.9 28.6 %shard_map.262 = (bf16[2048,384]{1,0:T(8,128)(2,1)}, bf16[2048,384]{1,0:T(8,128)(2,1)}, bf16[2048,384]{1,0:T(8,128)(2,1)}, bf16[2048,1536]{1,0:T(8,128)(2,1)}, bf16[2048,1536]{1,0:T(8,128)(2,1)}) custom-call(bf16[2048,1536]{1,0:T(8,128)(2,1)} %bitcast.71, bf16[2048,1536]{1,0:T(8,128)(2,1)} %all-gather.4.cloned.1.call-done.refs_1_.c_ref, ...), custom_call_target="tpu_custom_call" | custom-call | flops 14495514624 | bytes 41943040 | tf_op jit(solution)/shard_map/pallas_call | solution.py:679
  329.5 38.4 %shard_map.263 = (f32[256,1536]{1,0:T(8,128)}, bf16[256,1536]{1,0:T(8,128)(2,1)}, f32[1,1536]{1,0:T(1,128)}, bf16[4,3,384,384]{3,2,1,0:T(8,128)(2,1)}) custom-call(bf16[8,256,1536]{2,1,0:T(8,128)(2,1)} %bitcast.107, f32[256,1536]{1,0:T(8,128)} %copy-done, bf16[256,1536]{1,0:T(8,128)(2,1)} %cot_ref.1, f32[1,1536]{1,0:T(1,128)} %slice.65.gain_ref, ...), custom_call_target="tpu_custom_call" | custom-call | flops 7247757312 | bytes 104857600 | tf_op jit(solution)/shard_map/pallas_call | solution.py:804
  367.9 24.4 %shard_map.264 = (bf16[512,768]{1,0:T(8,128)(2,1)}, bf16[768,1536]{1,0:T(8,128)(2,1)}) custom-call(bf16[256,1536]{1,0:T(8,128)(2,1)} %get-tuple-element.89.dproj_ref, bf16[768,1536]{1,0:T(8,128)(2,1)} %bitcast.81, bf16[512,768]{1,0:T(8,128)(2,1)} %copy-done.2), custom_call_target="tpu_custom_call" | custom-call | flops 2415919104 | bytes 41943040 | tf_op jit(solution)/shard_map/pallas_call | solution.py:1180
  392.3 44.5 %shard_map.265 = (bf16[512,768]{1,0:T(8,128)(2,1)}, bf16[32,256,256]{2,1,0:T(8,128)(2,1)}) custom-call(s32[32]{0:T(128)} %fusion.1.slots, s32[2]{0:T(128)} %get-tuple-element.128.tops, bf16[512,768]{1,0:T(8,128)(2,1)} %get-tuple-element.72.q_ref, bf16[32,256,256]{2,1,0:T(8,128)(2,1)} %bitcast.75, bf16[512,768]{1,0:T(8,128)(2,1)} %get-tuple-element.90.do_ref, ...), custom_call_target="tpu_custom_call" | custom-call | flops 16609443840 | bytes 125829120 | tf_op jit(solution)/shard_map/pallas_call | solution.py:972
  436.8 45.9 %shard_map.266 = (bf16[512,256]{1,0:T(8,128)(2,1)}, f32[48,1536]{1,0:T(8,128)}, bf16[4,3,384,384]{3,2,1,0:T(8,128)(2,1)}) custom-call(bf16[16,512,256]{2,1,0:T(8,128)(2,1)} %bitcast.76, bf16[16,48,1536]{2,1,0:T(8,128)(2,1)} %bitcast.80, bf16[4,3,384,384]{3,2,1,0:T(8,128)(2,1)} %get-tuple-element.95.refs_2_), custom_call_target="tpu_custom_call", output_to_operand_aliasing={{2}: (2, {})} | custom-call | bytes 131072000 | tf_op jit(solution)/shard_map/pallas_call | solution.py:522
  483.6 27.3 %shard_map.267 = (bf16[16,2,48,1024]{3,2,1,0:T(8,128)(2,1)}, bf16[512,1536]{1,0:T(8,128)(2,1)}, f32[1,1536]{1,0:T(1,128)}, f32[1,1024]{1,0:T(1,128)}, bf16[3,4,96,768]{3,2,1,0:T(8,128)(2,1)}) custom-call(bf16[512,768]{1,0:T(8,128)(2,1)} %get-tuple-element.92.dq_ref, bf16[512,256]{1,0:T(8,128)(2,1)} %get-tuple-element.96.dkv_ref, ...), custom_call_target="tpu_custom_call" | custom-call | flops 3221225472 | bytes 16777216 | tf_op jit(solution)/shard_map/pallas_call | solution.py:1120
  514.3 62.9 %shard_map.268 = (f32[2,48,1024]{2,1,0:T(8,128)}, f32[8,128]{1,0:T(8,128)}, f32[256,1536]{1,0:T(8,128)}, f32[256,1536]{1,0:T(8,128)}) custom-call(bf16[16,2,48,1024]{3,2,1,0:T(8,128)(2,1)} %get-tuple-element.98.refs_0_, f32[32,8,128]{2,1,0:T(8,128)} %bitcast.89, bf16[2,256,1536]{2,1,0:T(8,128)(2,1)} %bitcast.86, bf16[8,256,1536]{2,1,0:T(8,128)(2,1)} %bitcast.73), custom_call_target="tpu_custom_call" | custom-call | bytes 222822400 | tf_op jit(solution)/shard_map/pallas_call | solution.py:522
  578.5 1.3 slice_bitcast_fusion
  579.8 12.3 %shard_map.269.refs_8_ = bf16[3,4,96,384]{3,2,1,0:T(8,128)(2,1)} custom-call(bf16[3,4,96,384]{3,2,1,0:T(8,128)(2,1)} %bitcast.88, f32[2,48,1024]{2,1,0:T(8,128)} %get-tuple-element.104.refs_1_.refs_0_), custom_call_target="tpu_custom_call" | custom-call | tf_op jit(solution)/shard_map/pallas_call | solution.py:559
  592.1 6.8 %shard_map.270 = (f32[48,1536]{1,0:T(8,128)}, f32[48,256]{1,0:T(8,128)}, f32[48,256]{1,0:T(8,128)}, bf16[256,1536]{1,0:T(8,128)(2,1)}, bf16[256,1536]{1,0:T(8,12...) custom-call(f32[2,48,1024]{2,1,0:T(8,128)} %get-tuple-element.104.refs_1_.refs_0_, ...), custom_call_target="tpu_custom_call" | custom-call | bytes 20971520 | tf_op jit(solution)/shard_map/pallas_call | solution.py:620
  (81 shorter events, 19.3 us)
Async XLA Ops:
  7.2 65.4 %all-gather.4.cloned.1.call-start = ((), (), s32[]{:S(2)}) async-start(), calls=%async_computation.2 | async-start | bytes 7077888 | tf_op jit(solution)/shard_map/all_gather | solution.py:1288
  7.9 223.2 %all-gather.8.cloned.1.call-start = ((), (), s32[]{:S(2)}) async-start(), calls=%async_computation.4 | async-start | bytes 8847360 | tf_op jit(solution)/shard_map/all_gather | solution.py:1253
  9.4 58.1 %copy-start.6 = (s32[1,32]{1,0:T(1,128)S(1)}, s32[1,32]{1,0:T(1,128)}, u32[]{:S(2)}) copy-start(s32[1,32]{1,0:T(1,128)} %param.17) | copy-start | bytes 388
  100.0 200.9 %all-gather.6.cloned.1.call-start = ((), (), s32[]{:S(2)}) async-start(), calls=%async_computation.3 | async-start | bytes 4423680 | tf_op jit(solution)/shard_map/all_gather | solution.py:1253
  159.4 2.2 copy-start.3
  161.1 4.1 copy-start.2
  165.1 21.9 %copy-start.1 = (bf16[256,1536]{1,0:T(8,128)(2,1)S(1)}, bf16[256,1536]{1,0:T(8,128)(2,1)}, u32[]{:S(2)}) copy-start(bf16[256,1536]{1,0:T(8,128)(2,1)} %refs_4_.3) | copy-start | bytes 2359300
  186.7 296.8 %reduce-scatter.3.cloned.1.call-start = ((), (), s32[]{:S(2)}) async-start(), calls=%async_computation.5 | async-start | bytes 8847360 | tf_op jit(solution)/shard_map/reduce_scatter | solution.py:1363
  189.1 33.0 %copy-start = (f32[256,1536]{1,0:T(8,128)}, f32[256,1536]{1,0:T(8,128)S(1)}, u32[]{:S(2)}) copy-start(f32[256,1536]{1,0:T(8,128)S(1)} %get-tuple-element.126.mixed_ref.refs_5_) | copy-start | bytes 4718596
  295.8 284.0 %reduce-scatter.5.cloned.1.call-start = ((), (), s32[]{:S(2)}) async-start(), calls=%async_computation.6 | async-start | bytes 4423680 | tf_op jit(solution)/shard_map/reduce_scatter | solution.py:1363
  482.7 0.7 copy-start.5
  592.1 6.8 %copy-start.4 = (f32[48,1536]{1,0:T(8,128)S(1)}, f32[48,1536]{1,0:T(8,128)}, u32[]{:S(2)}) copy-start(f32[48,1536]{1,0:T(8,128)} %get-tuple-element.169) | copy-start | bytes 884740
Sparse Core Ops, SparseCore 0:
  9.9 62.6 all-gather.3
  100.1 130.9 all-gather.7
  232.6 68.2 all-gather.5
  303.1 122.0 reduce-scatter.2
  482.9 80.0 reduce-scatter.4

commit v8 on v7

--- a/solution.py
+++ b/solution.py
@@ -1001,8 +1001,14 @@
     return value * cosine + pltpu.roll(value, HEAD_DIM // 2, 1) * sine
 
 
-def project_kernel(plans, sizes, x_ref, w_ref, gain_ref, bias_ref, cos_ref, sin_ref, *refs):
-    packed_ref, _, kv_all_ref, swapped_ref, q_ref, normed_ref, kv_s = refs[:7]
+def project_kernel(plans, sizes, x_ref, w_hbm, gain_ref, bias_ref, cos_ref, sin_ref, *refs):
+    packed_ref, _, kv_all_ref, swapped_ref, q_ref, normed_ref, kv_s, w_ref, w_sems = refs[:9]
+    q_width = q_ref.shape[1]
+    loads = []
+    for i, (low, n) in enumerate(((q_width, 2 * HEAD_DIM), (0, q_width))):
+        span = (slice(None), pl.ds(low, n))
+        loads.append(pltpu.make_async_copy(w_hbm.at[span], w_ref.at[span], w_sems.at[i]))
+        loads[i].start()
     x = x_ref[...].astype(F32)
     normed_ref[...] = (x * inverse_rms(x) * gain_ref[...]).astype(BF)
     cosine, sine = cos_ref[...], sin_ref[...]
@@ -1012,11 +1018,13 @@
         cols = slice(low * HEAD_DIM, (low + n) * HEAD_DIM)
         return dot_nn(normed_ref[...], w_ref[:, cols]) + bias_ref[:, cols]
 
+    loads[0].wait()
     made = product(heads, 2)
     kv_s[:, :HEAD_DIM] = turned(made[:, :HEAD_DIM], cosine, sine).astype(BF)
     kv_s[:, HEAD_DIM:] = made[:, HEAD_DIM:].astype(BF)
 
     def queries():
+        loads[1].wait()
         for low in range(0, heads, 2):
             made = product(low, 2)
             for i in range(2):
@@ -1026,7 +1034,7 @@
                 ).astype(BF)
 
     gather_kernel(
-        plans, sizes, 1, 0, 0, kv_s, packed_ref, kv_all_ref, swapped_ref, *refs[7:], behind=queries
+        plans, sizes, 1, 0, 0, kv_s, packed_ref, kv_all_ref, swapped_ref, *refs[9:], behind=queries
     )
 
 
@@ -1039,7 +1047,7 @@
     kv = (n, 2 * HEAD_DIM)
     return pl.pallas_call(
         functools.partial(project_kernel, plans, sizes),
-        in_specs=[spec] * 6 + [far] * 2,
+        in_specs=[spec, far] + [spec] * 4 + [far] * 2,
         out_specs=[far, far, spec, spec],
         out_shape=[
             jax.ShapeDtypeStruct(s, BF)
@@ -1047,6 +1055,8 @@
         ],
         scratch_shapes=[
             pltpu.VMEM(kv, BF),
+            pltpu.VMEM(w.shape, BF),
+            pltpu.SemaphoreType.DMA((2,)),
             pltpu.SemaphoreType.DMA((count - 1,)),
             pltpu.SemaphoreType.DMA((count - 1,)),
             pltpu.SemaphoreType.DMA((1,)),
@@ -1138,8 +1148,14 @@
     )(dq, dkv, normed, x, w, cosine, sine, back)
 
 
-def exchange_back_kernel(sizes, dproj_ref, w_ref, attn_ref, dout_ref, o_ref, pair_s, sum_s, *sems):
-    send_sems, recv_sems = sems
+def exchange_back_kernel(sizes, dproj_ref, w_hbm, attn_hbm, dout_ref, o_ref, pair_s, sum_s, *refs):
+    w_ref, attn_ref, load_sems, send_sems, recv_sems = refs
+    loads = [
+        pltpu.make_async_copy(w_hbm, w_ref, load_sems.at[0]),
+        pltpu.make_async_copy(attn_hbm, attn_ref, load_sems.at[1]),
+    ]
+    for copy in loads:
+        copy.start()
     greet(("head",), sizes)
     me, count = lax.axis_index("head"), sizes["head"]
     tok = dproj_ref.shape[0]
@@ -1165,6 +1181,8 @@
             else:
                 sum_s[part, :] = made
 
+    for copy in loads:
+        copy.wait()
     use(me, dproj_ref[...], True, count == 1)
     for d in range(1, count):
         copies[d - 1].wait_recv()
@@ -1179,7 +1197,7 @@
     count = sizes["head"]
     return pl.pallas_call(
         functools.partial(exchange_back_kernel, sizes),
-        in_specs=[spec] * 3,
+        in_specs=[spec] + [pl.BlockSpec(memory_space=pl.ANY)] * 2,
         out_specs=[spec] * 2,
         out_shape=[
             jax.ShapeDtypeStruct(attn.shape, BF),
@@ -1188,6 +1206,9 @@
         scratch_shapes=[
             pltpu.VMEM((count,) + dproj.shape, BF),
             pltpu.VMEM(w.shape, F32),
+            pltpu.VMEM(w.shape, BF),
+            pltpu.VMEM(attn.shape, BF),
+            pltpu.SemaphoreType.DMA((2,)),
             pltpu.SemaphoreType.DMA((count - 1,)),
             pltpu.SemaphoreType.DMA((count - 1,)),
         ],

time: 615 us -> 614 us (level)
  no operation moved by 1% of the time
where the time goes in v8:
time: 614 us; the launch traced here: 605 us
  Pallas kernels  549 us (89%)
  waiting for transfers between devices  14.9 us (2%)
  between operations  14.3 us (2%)
  local copies, waits for them, and re-layouts  11.9 us (2%)
  other arithmetic  11.3 us (2%)
    pallas_call x2, Pallas kernels, scatter(): pl.pallas_call(functools.partial(scatter_and_wait_kernel, plans, sizes, l...  109 us
    pallas_call x3, Pallas kernels, gather(): pl.pallas_call(functools.partial(gather_kernel, plans, sizes, len(swaps),...  82.9 us
    pallas_call x2, Pallas kernels, feed(): pl.pallas_call(functools.partial(feed_kernel, chunks, len(before)), grid=...  71.8 us
    pallas_call x1, Pallas kernels, front(): pl.pallas_call(functools.partial(front_kernel, plans, sizes), out_shape=s...  56.2 us
    pallas_call x1, Pallas kernels, attend_back(): pl.pallas_call(functools.partial(backward_kernel, heads), grid_spec=pltpu...  44.5 us
    pallas_call x1, Pallas kernels, feed_grads(): pl.pallas_call(functools.partial(grads_kernel, plans, sizes), out_shape=[...  38.4 us
    pallas_call x1, Pallas kernels, attend(): pl.pallas_call(functools.partial(forward_kernel, heads), grid_spec=pltpu....  27.5 us
    pallas_call x1, Pallas kernels, project_back(): pl.pallas_call(project_back_kernel, in_specs=[spec] * 7 + [far], out_spec...  27.3 us
  transfers between devices with their start and end apart: 5, of which 3 were waited for; matrix products, arithmetic and copies ran while one was open for 4% of the time, Pallas kernels for 83%

profile of v8, /device:TPU:0, one launch (start us, length us, event | category | flops | bytes accessed | tf_op | source)
XLA Modules:
  0.0 605.3 jit_solution(15245183365373237071)
XLA Ops:
  9.4 56.2 %shard_map.254 = (bf16[32,48,1024]{2,1,0:T(8,128)(2,1)}, bf16[2,256,1536]{2,1,0:T(8,128)(2,1)}, f32[32,8,128]{2,1,0:T(8,128)}, bf16[16,48,1536]{2,1,0:T(8,128)(2...) custom-call(f32[48,1536]{1,0:T(8,128)} %refs_0_.1, f32[48,256]{1,0:T(8,128)} %refs_1_.1, ...), custom_call_target="tpu_custom_call" | custom-call | bytes 104857600 | tf_op jit(solution)/shard_map/pallas_call | solution.py:321
  72.6 27.2 %shard_map.255 = (bf16[4,512,256]{2,1,0:T(8,128)(2,1)}, bf16[3,4,96,768]{3,2,1,0:T(8,128)(2,1)}, bf16[512,768]{1,0:T(8,128)(2,1)}, bf16[512,1536]{1,0:T(8,128)(2,1)}) custom-call(bf16[512,1536]{1,0:T(8,128)(2,1)} %bitcast.84, bf16[1536,1024]{1,0:T(8,128)(2,1)} %bitcast.77, f32[1,1536]{1,0:T(1,128)} %slice.59.gain_ref.refs_6_, f32[1,1024]{1,0:T(1,128)} %bitcast.103, ...), custom_call_target="tpu_custom_call" | custom-call | flops 1610612736 | bytes 83886080 | tf_op jit(solution)/shard_map/pallas_call | solution.py:1048
  100.0 1.6 sort.17
  102.1 29.6 %shard_map.256 = bf16[4,4,512,256]{3,2,1,0:T(8,128)(2,1)} custom-call(bf16[4,512,256]{2,1,0:T(8,128)(2,1)} %get-tuple-element.73.refs_0_), custom_call_target="tpu_custom_call" | custom-call | bytes 83886080 | tf_op jit(solution)/shard_map/pallas_call | solution.py:234
  131.7 27.5 %shard_map.257 = (f32[512,768]{1,0:T(8,128)}, f32[2,8,256]{2,1,0:T(8,128)}) custom-call(s32[32]{0:T(128)} %fusion.1.slots, s32[2]{0:T(128)} %get-tuple-element.128.tops, bf16[512,768]{1,0:T(8,128)(2,1)} %get-tuple-element.72.q_ref, bf16[32,256,256]{2,1,0:T(8,128)(2,1)} %bitcast.74), custom_call_target="tpu_custom_call" | custom-call | flops 6643777536 | bytes 83886080 | tf_op jit(solution)/shard_map/pallas_call | solution.py:884
  159.2 1.7 convert_element_type.47.attn_hbm
  161.4 3.6 fusion.7
  164.9 21.5 %shard_map.258 = (bf16[2,256,1536]{2,1,0:T(8,128)(2,1)}, bf16[3,4,96,384]{3,2,1,0:T(8,128)(2,1)}) custom-call(bf16[2,256,1536]{2,1,0:T(8,128)(2,1)} %get-tuple-element.142.refs_0_, bf16[3,4,96,384]{3,2,1,0:T(8,128)(2,1)} %get-tuple-element.76.refs_1_), custom_call_target="tpu_custom_call" | custom-call | bytes 31457280 | tf_op jit(solution)/shard_map/pallas_call | solution.py:234
  186.9 2.1 multiply_reduce_fusion
  190.2 31.8 %shard_map.259 = bf16[8,256,1536]{2,1,0:T(8,128)(2,1)} custom-call(bf16[256,1536]{1,0:T(8,128)(2,1)} %multiply_convert_fusion.refs_0_), custom_call_target="tpu_custom_call" | custom-call | bytes 125829120 | tf_op jit(solution)/shard_map/pallas_call | solution.py:234
  222.0 9.0 %all-gather.8.cloned.1.call-done.w_ref = bf16[4,3,384,768]{3,2,1,0:T(8,128)(2,1)} async-done(((bf16[1,3,384,768]{3,2,1,0:T(8,128)(2,1)}), bf16[4,3,384,768]{3,2,1,0:T(8,128)(2,1)}) %all-gather.8.cloned.1.call-update) | async-done | bytes 7077904 | tf_op jit(solution)/shard_map/all_gather | solution.py:1274
  231.0 43.2 %shard_map.260 = (bf16[2048,768]{1,0:T(8,128)(2,1)}, bf16[2048,768]{1,0:T(8,128)(2,1)}, bf16[2048,768]{1,0:T(8,128)(2,1)}, bf16[2048,1536]{1,0:T(8,128)(2,1)}, bf16[2048,1536]{1,0:T(8,128)(2,1)}) custom-call(bf16[2048,1536]{1,0:T(8,128)(2,1)} %bitcast.69, bf16[2048,1536]{1,0:T(8,128)(2,1)} %all-gather.4.cloned.1.call-done.refs_1_.c_ref, ...), custom_call_target="tpu_custom_call" | custom-call | flops 28991029248 | bytes 41943040 | tf_op jit(solution)/shard_map/pallas_call | solution.py:679
  274.1 21.5 %shard_map.261.refs_2_ = bf16[4,3,384,768]{3,2,1,0:T(8,128)(2,1)} custom-call(bf16[2048,1536]{1,0:T(8,128)(2,1)} %bitcast.70, bf16[2048,1536]{1,0:T(8,128)(2,1)} %all-gather.4.cloned.1.call-done.refs_1_.c_ref, bf16[2048,768]{1,0:T(8,128)(2,1)} %get-tuple-element.82.act_ref, bf16[2048,768]{1,0:T(8,128)(2,1)} %get-tuple-element.83.dgate_ref, ...), custom_call_target="tpu_custom_call" | custom-call | flops 14495514624 | bytes 41943040 | tf_op jit(solution)/shard_map/pallas_call | solution.py:707
  296.8 4.0 all-gather.6.cloned.1.call-done.w_ref
  300.8 28.6 %shard_map.262 = (bf16[2048,384]{1,0:T(8,128)(2,1)}, bf16[2048,384]{1,0:T(8,128)(2,1)}, bf16[2048,384]{1,0:T(8,128)(2,1)}, bf16[2048,1536]{1,0:T(8,128)(2,1)}, bf16[2048,1536]{1,0:T(8,128)(2,1)}) custom-call(bf16[2048,1536]{1,0:T(8,128)(2,1)} %bitcast.71, bf16[2048,1536]{1,0:T(8,128)(2,1)} %all-gather.4.cloned.1.call-done.refs_1_.c_ref, ...), custom_call_target="tpu_custom_call" | custom-call | flops 14495514624 | bytes 41943040 | tf_op jit(solution)/shard_map/pallas_call | solution.py:679
  329.4 38.4 %shard_map.263 = (f32[256,1536]{1,0:T(8,128)}, bf16[256,1536]{1,0:T(8,128)(2,1)}, f32[1,1536]{1,0:T(1,128)}, bf16[4,3,384,384]{3,2,1,0:T(8,128)(2,1)}) custom-call(bf16[8,256,1536]{2,1,0:T(8,128)(2,1)} %bitcast.107, f32[256,1536]{1,0:T(8,128)} %copy-done, bf16[256,1536]{1,0:T(8,128)(2,1)} %cot_ref.1, f32[1,1536]{1,0:T(1,128)} %slice.65.gain_ref, ...), custom_call_target="tpu_custom_call" | custom-call | flops 7247757312 | bytes 104857600 | tf_op jit(solution)/shard_map/pallas_call | solution.py:804
  367.8 23.4 %shard_map.264 = (bf16[512,768]{1,0:T(8,128)(2,1)}, bf16[768,1536]{1,0:T(8,128)(2,1)}) custom-call(bf16[256,1536]{1,0:T(8,128)(2,1)} %get-tuple-element.89.dproj_ref, bf16[768,1536]{1,0:T(8,128)(2,1)} %bitcast.81, bf16[512,768]{1,0:T(8,128)(2,1)} %copy-done.2), custom_call_target="tpu_custom_call" | custom-call | flops 2415919104 | bytes 41943040 | tf_op jit(solution)/shard_map/pallas_call | solution.py:1198
  391.3 44.5 %shard_map.265 = (bf16[512,768]{1,0:T(8,128)(2,1)}, bf16[32,256,256]{2,1,0:T(8,128)(2,1)}) custom-call(s32[32]{0:T(128)} %fusion.1.slots, s32[2]{0:T(128)} %get-tuple-element.128.tops, bf16[512,768]{1,0:T(8,128)(2,1)} %get-tuple-element.72.q_ref, bf16[32,256,256]{2,1,0:T(8,128)(2,1)} %bitcast.75, bf16[512,768]{1,0:T(8,128)(2,1)} %get-tuple-element.90.do_ref, ...), custom_call_target="tpu_custom_call" | custom-call | flops 16609443840 | bytes 125829120 | tf_op jit(solution)/shard_map/pallas_call | solution.py:972
  435.8 45.9 %shard_map.266 = (bf16[512,256]{1,0:T(8,128)(2,1)}, f32[48,1536]{1,0:T(8,128)}, bf16[4,3,384,384]{3,2,1,0:T(8,128)(2,1)}) custom-call(bf16[16,512,256]{2,1,0:T(8,128)(2,1)} %bitcast.76, bf16[16,48,1536]{2,1,0:T(8,128)(2,1)} %bitcast.80, bf16[4,3,384,384]{3,2,1,0:T(8,128)(2,1)} %get-tuple-element.95.refs_2_), custom_call_target="tpu_custom_call", output_to_operand_aliasing={{2}: (2, {})} | custom-call | bytes 131072000 | tf_op jit(solution)/shard_map/pallas_call | solution.py:522
  482.5 27.3 %shard_map.267 = (bf16[16,2,48,1024]{3,2,1,0:T(8,128)(2,1)}, bf16[512,1536]{1,0:T(8,128)(2,1)}, f32[1,1536]{1,0:T(1,128)}, f32[1,1024]{1,0:T(1,128)}, bf16[3,4,96,768]{3,2,1,0:T(8,128)(2,1)}) custom-call(bf16[512,768]{1,0:T(8,128)(2,1)} %get-tuple-element.92.dq_ref, bf16[512,256]{1,0:T(8,128)(2,1)} %get-tuple-element.96.dkv_ref, ...), custom_call_target="tpu_custom_call" | custom-call | flops 3221225472 | bytes 16777216 | tf_op jit(solution)/shard_map/pallas_call | solution.py:1130
  513.3 62.9 %shard_map.268 = (f32[2,48,1024]{2,1,0:T(8,128)}, f32[8,128]{1,0:T(8,128)}, f32[256,1536]{1,0:T(8,128)}, f32[256,1536]{1,0:T(8,128)}) custom-call(bf16[16,2,48,1024]{3,2,1,0:T(8,128)(2,1)} %get-tuple-element.98.refs_0_, f32[32,8,128]{2,1,0:T(8,128)} %bitcast.89, bf16[2,256,1536]{2,1,0:T(8,128)(2,1)} %bitcast.86, bf16[8,256,1536]{2,1,0:T(8,128)(2,1)} %bitcast.73), custom_call_target="tpu_custom_call" | custom-call | bytes 222822400 | tf_op jit(solution)/shard_map/pallas_call | solution.py:522
  577.4 1.3 slice_bitcast_fusion
  578.8 12.3 %shard_map.269.refs_8_ = bf16[3,4,96,384]{3,2,1,0:T(8,128)(2,1)} custom-call(bf16[3,4,96,384]{3,2,1,0:T(8,128)(2,1)} %bitcast.88, f32[2,48,1024]{2,1,0:T(8,128)} %get-tuple-element.104.refs_1_.refs_0_), custom_call_target="tpu_custom_call" | custom-call | tf_op jit(solution)/shard_map/pallas_call | solution.py:559
  591.1 6.8 %shard_map.270 = (f32[48,1536]{1,0:T(8,128)}, f32[48,256]{1,0:T(8,128)}, f32[48,256]{1,0:T(8,128)}, bf16[256,1536]{1,0:T(8,128)(2,1)}, bf16[256,1536]{1,0:T(8,12...) custom-call(f32[2,48,1024]{2,1,0:T(8,128)} %get-tuple-element.104.refs_1_.refs_0_, ...), custom_call_target="tpu_custom_call" | custom-call | bytes 20971520 | tf_op jit(solution)/shard_map/pallas_call | solution.py:620
  (81 shorter events, 19.3 us)
Async XLA Ops:
  7.2 65.4 %all-gather.4.cloned.1.call-start = ((), (), s32[]{:S(2)}) async-start(), calls=%async_computation.2 | async-start | bytes 7077888 | tf_op jit(solution)/shard_map/all_gather | solution.py:1309
  7.9 223.0 %all-gather.8.cloned.1.call-start = ((), (), s32[]{:S(2)}) async-start(), calls=%async_computation.4 | async-start | bytes 8847360 | tf_op jit(solution)/shard_map/all_gather | solution.py:1274
  9.4 58.1 %copy-start.6 = (s32[1,32]{1,0:T(1,128)S(1)}, s32[1,32]{1,0:T(1,128)}, u32[]{:S(2)}) copy-start(s32[1,32]{1,0:T(1,128)} %param.17) | copy-start | bytes 388
  99.9 200.9 %all-gather.6.cloned.1.call-start = ((), (), s32[]{:S(2)}) async-start(), calls=%async_computation.3 | async-start | bytes 4423680 | tf_op jit(solution)/shard_map/all_gather | solution.py:1274
  159.2 2.2 copy-start.3
  160.9 4.1 copy-start.2
  164.9 21.9 %copy-start.1 = (bf16[256,1536]{1,0:T(8,128)(2,1)S(1)}, bf16[256,1536]{1,0:T(8,128)(2,1)}, u32[]{:S(2)}) copy-start(bf16[256,1536]{1,0:T(8,128)(2,1)} %refs_4_.3) | copy-start | bytes 2359300
  186.5 296.0 %reduce-scatter.3.cloned.1.call-start = ((), (), s32[]{:S(2)}) async-start(), calls=%async_computation.5 | async-start | bytes 8847360 | tf_op jit(solution)/shard_map/reduce_scatter | solution.py:1384
  188.9 33.0 %copy-start = (f32[256,1536]{1,0:T(8,128)}, f32[256,1536]{1,0:T(8,128)S(1)}, u32[]{:S(2)}) copy-start(f32[256,1536]{1,0:T(8,128)S(1)} %get-tuple-element.126.mixed_ref.refs_5_) | copy-start | bytes 4718596
  295.7 283.1 %reduce-scatter.5.cloned.1.call-start = ((), (), s32[]{:S(2)}) async-start(), calls=%async_computation.6 | async-start | bytes 4423680 | tf_op jit(solution)/shard_map/reduce_scatter | solution.py:1384
  481.7 0.7 copy-start.5
  591.1 6.8 %copy-start.4 = (f32[48,1536]{1,0:T(8,128)S(1)}, f32[48,1536]{1,0:T(8,128)}, u32[]{:S(2)}) copy-start(f32[48,1536]{1,0:T(8,128)} %get-tuple-element.169) | copy-start | bytes 884740
Sparse Core Ops, SparseCore 0:
  9.9 62.6 all-gather.3
  100.0 130.9 all-gather.7
  232.5 68.2 all-gather.5
  302.9 122.0 reduce-scatter.2
  481.9 80.0 reduce-scatter.4
